TPU v7x, 32 devices: a whole 2x2x4 slice. The times are simulated.
32 devices in a mesh: ctx: 16 (over z, y, x), fsdp: 2 (over core).
Axes of the slice: x: 2, y: 2, z: 4, core: 2. Of those that a mesh axis runs over, the one named last changes fastest.
Arguments:
- features: bfloat16 [3, 2048, 6144], P(None, 'ctx', 'fsdp'), may hold values from -6 to 6
- cotangent: bfloat16 [2048, 6144], P('ctx', 'fsdp'), may hold values from -6 to 6
- master_filters: float32 [4, 7, 384], P(None, None, 'fsdp'), may hold values from -2 to 2
Outputs:
- mixed: bfloat16 [2048, 6144], P('ctx', 'fsdp')
- feature_grads: bfloat16 [3, 2048, 6144], P(None, 'ctx', 'fsdp')
- filter_grads: float32 [4, 7, 384], P(None, None, 'fsdp')
All inputs are finite; a program needn't handle non-finite values.
Results may differ from a plain program's by a relative error of at most 0.007.
Values may be sent and summed in bfloat16 or wider, within the bound.
No kernel may reach another device: no remote copies, remote signals or barrier semaphores. Data moves between devices by JAX's collectives and lax.ppermute only.
A program may use at most 64 MiB of HBM per device.

v0:
```python
import math

import jax
import jax.numpy as jnp
from jax import lax
from jax.sharding import PartitionSpec as P


def from_behind(shard, axis, by):
    size = lax.axis_size(axis)
    pairs = [(i, i + by) for i in range(size) if 0 <= i + by < size]
    return lax.ppermute(shard, axis, pairs)


def causal(extended, weights):
    reach = weights.shape[0] - 1
    length = extended.shape[0] - reach
    result = weights[0] * extended[reach : reach + length]
    for lag in range(1, weights.shape[0]):
        result = result + weights[lag] * extended[reach - lag : reach - lag + length]
    return result


def anticausal(extended, weights):
    reach = weights.shape[0] - 1
    length = extended.shape[0] - reach
    result = weights[0] * extended[0:length]
    for lag in range(1, weights.shape[0]):
        result = result + weights[lag] * extended[lag : lag + length]
    return result


def per_device(features, cotangent, master_filters):
    gathered = lax.all_gather(
        master_filters.astype(jnp.bfloat16), "fsdp", axis=2, tiled=True
    ).astype(jnp.float32)
    groups = gathered.shape[2]
    repeats = features.shape[2] // groups
    weights = jnp.tile(gathered, (1, 1, repeats))
    reach = weights.shape[1] - 1
    length = features.shape[1]
    next_heads = from_behind((features[:, : 2 * reach, :], cotangent[: 2 * reach]), "ctx", -1)
    history = from_behind(features[:, length - reach :, :], "ctx", 1)
    inputs_ext = jnp.concatenate([history, features], axis=1).astype(jnp.float32)
    q_conv = causal(inputs_ext[0], weights[0])
    k_conv = causal(inputs_ext[1], weights[1])
    v_conv = causal(inputs_ext[2], weights[2])
    product = k_conv * v_conv
    prior = from_behind(product[length - reach :], "ctx", 1)
    product_ext = jnp.concatenate([prior, product], axis=0)
    mixer = causal(product_ext, weights[3])
    mixed = (q_conv * mixer).astype(jnp.bfloat16)
    upstream = cotangent.astype(jnp.float32)
    grad_qconv = upstream * mixer
    grad_mixer = upstream * q_conv
    next_inputs = jnp.concatenate(
        [inputs_ext[:, length:, :], next_heads[0].astype(jnp.float32)], axis=1
    )
    next_upstream = next_heads[1].astype(jnp.float32)
    next_q = causal(next_inputs[0], weights[0])
    next_k = causal(next_inputs[1], weights[1])
    next_v = causal(next_inputs[2], weights[2])
    next_product = jnp.concatenate([product_ext[length:], next_k * next_v], axis=0)
    next_mixer = causal(next_product, weights[3])
    next_gq = next_upstream * next_mixer
    next_gm = next_upstream * next_q
    next_gp = anticausal(next_gm, weights[3])
    incoming = (
        next_gq[:reach],
        next_gp * next_v[:reach],
        next_gp * next_k[:reach],
        next_gm[:reach],
    )
    grad_product = anticausal(jnp.concatenate([grad_mixer, incoming[3]], axis=0), weights[3])
    grad_kconv = grad_product * v_conv
    grad_vconv = grad_product * k_conv
    grad_q = anticausal(jnp.concatenate([grad_qconv, incoming[0]], axis=0), weights[0])
    grad_k = anticausal(jnp.concatenate([grad_kconv, incoming[1]], axis=0), weights[1])
    grad_v = anticausal(jnp.concatenate([grad_vconv, incoming[2]], axis=0), weights[2])
    feature_grads = jnp.stack([grad_q, grad_k, grad_v]).astype(jnp.bfloat16)
    pairs = (
        (grad_qconv, inputs_ext[0]),
        (grad_kconv, inputs_ext[1]),
        (grad_vconv, inputs_ext[2]),
        (grad_mixer, product_ext),
    )
    rows_out = []
    for grad_term, source in pairs:
        rows_out.append(
            jnp.stack(
                [
                    jnp.sum(grad_term * source[reach - lag : reach - lag + length], axis=0)
                    for lag in range(reach + 1)
                ]
            )
        )
    partial_sum = jnp.sum(jnp.stack(rows_out).reshape(4, reach + 1, repeats, groups), axis=2)
    count_all = length * lax.axis_size("ctx") * repeats * lax.axis_size("fsdp")
    factor = 1.0 / math.sqrt(count_all)
    summed = lax.psum(partial_sum, ("ctx", "fsdp"))
    portion = groups // lax.axis_size("fsdp")
    owned = lax.dynamic_slice_in_dim(summed, lax.axis_index("fsdp") * portion, portion, 2)
    filter_grads = owned * factor
    return (mixed, feature_grads, filter_grads)


def solution(mesh):
    return jax.shard_map(
        per_device,
        mesh=mesh,
        in_specs=(P(None, "ctx", "fsdp"), P("ctx", "fsdp"), P(None, None, "fsdp")),
        out_specs=(P("ctx", "fsdp"), P(None, "ctx", "fsdp"), P(None, None, "fsdp")),
        check_vma=False,
    )
```

profile of v0, /device:TPU:0, one launch (start us, length us, event | category | flops | bytes accessed | tf_op | source)
XLA Modules:
  0.0 174.6 jit_solution(3325772035668105656)
XLA Ops:
  0.6 0.9 slice.930
  1.5 1.3 collective-permute-start.2
  2.8 1.6 slice.826
  4.4 6.1 %collective-permute-start = (bf16[3,6,3072]{2,1,0:T(8,128)(2,1)}, bf16[3,6,3072]{2,1,0:T(8,128)(2,1)}, u32[]{:S(2)}, u32[]{:S(2)}) collective-permute-start(bf16[3,6,3072]{2,1,0:T(8,128)(2,1)} %slice.826), channel_id=1, source_target_pairs={{0,2},{2,4},{4,6},{6,8},{8,10},{10,12},{12,14},{14,16},{16,18},{18... | collective-permute-start | bytes 331784 | tf_op jit(solution)/shard_map/ppermute | solution.py:12
  10.6 1.0 slice.931
  11.5 1.3 collective-permute-start.3
  12.8 0.8 convert_element_type.22
  13.6 0.2 copy.10
  13.8 2.1 %all_gather.3 = bf16[4,7,384]{1,0,2:T(4,128)(2,1)S(1)} all-gather(bf16[4,7,192]{1,0,2:T(4,128)(2,1)S(1)} %copy.10), channel_id=1, replica_groups=mesh['ctx'=16,'fsdp'=2] {'fsdp'}, dimensions={2}, use_global_device_ids=true | all-gather | bytes 32256 | tf_op jit(solution)/shard_map/all_gather | solution.py:34
  15.9 0.1 convert_element_type.23
  16.0 28.4 %slice_reduce_fusion.20 = (f32[384]{0:T(512)S(1)}, f32[384]{0:T(512)S(1)}, f32[384]{0:T(512)S(1)}, f32[384]{0:T(512)S(1)}, f32[384]{0:T(512)S(1)}, /*index=5*/f3...) fusion(f32[4,7,384]{1,0,2:T(4,128)S(1)} %convert_element_type.23), kind=kLoop, calls=%fused_computation.329 | loop fusion | bytes 58368 | tf_op jit(solution)/shard_map/slice | solution.py:18
  44.4 0.0 copy-start.5
  44.4 12.8 %slice_reduce_fusion.19 = (f32[384]{0:T(512)S(1)}, f32[384]{0:T(512)S(1)}, f32[384]{0:T(512)S(1)}, f32[384]{0:T(512)S(1)}, f32[384]{0:T(512)S(1)}, /*index=5*/f3...) fusion(f32[4,7,384]{1,0,2:T(4,128)S(1)} %convert_element_type.23), kind=kLoop, calls=%fused_computation.328 | loop fusion | bytes 27648 | tf_op jit(solution)/shard_map/slice | solution.py:18
  57.3 0.6 tile.134
  57.9 0.6 tile.136
  58.9 0.6 tile.160
  59.5 0.6 tile.158
  60.1 0.6 tile.156
  60.7 0.6 tile.154
  61.3 0.6 tile.152
  61.9 0.6 tile.150
  62.5 0.6 tile.148
  63.2 0.6 tile.146
  63.8 0.6 tile.144
  64.4 0.6 tile.142
  65.0 0.6 tile.140
  65.6 0.6 tile.138
  66.2 0.0 collective-permute-done.2
  66.2 0.0 copy-start.4
  66.2 1.7 maximum_convert_fusion
  68.1 0.0 copy-start.68
  68.1 2.7 %convert_multiply_fusion = (f32[128,3072]{1,0:T(8,128)S(1)}, f32[128,3072]{1,0:T(8,128)}) fusion(bf16[128,3072]{1,0:T(8,128)(2,1)S(1)} %copy-done.4, f32[3,134,3072]{2,1,0:T(8,128)S(1)} %maximum_convert_fusion, f32[3072]{0:T(1024)S(1)} %tile.130, f32[3072]{0:T(1024)S(1)} %tile.128, f32[3072]{0:T(1024)S(1)} %tile.126, f32[3072]{0:T(1024)S(1)} %tile.124, ...), kind=kLoop, calls=%fused_computation.61 | loop fusion | flops 5898240 | bytes 15028224 | tf_op jit(solution)/shard_map/mul | solution.py:55
  71.2 1.1 fusion.174
  72.3 0.2 fusion.90
  72.6 0.8 slice_multiply_fusion.1
  73.4 5.5 %multiply_reduce_fusion.14 = (f32[3072]{0:T(1024)S(1)}, f32[3072]{0:T(1024)S(1)}, f32[3072]{0:T(1024)S(1)}, f32[3072]{0:T(1024)S(1)}, f32[3072]{0:T(1024)S(1)}, ...) fusion(f32[3,134,3072]{2,1,0:T(8,128)S(1)} %maximum_convert_fus, ...), kind=kLoop, calls=%fused_computation.191 | loop fusion | flops 18459648 | bytes 28643328 | tf_op jit(solution)/shard_map/reduce_sum | solution.py:92
  78.9 0.6 stack.137
  79.5 0.6 stack.136
  80.1 0.6 stack.135
  80.7 0.6 stack.134
  81.3 0.6 stack.133
  81.9 0.6 stack.132
  82.5 8.4 %fusion.178 = (f32[128,3072]{1,0:T(8,128)S(1)}, f32[128,3072]{1,0:T(8,128)}) fusion(f32[128,3072]{1,0:T(8,128)} %get-tuple-element.74, f32[3,134,3072]{2,1,0:T(8,128)} %copy-done, f32[3072]{0:T(1024)} %tile.146, f32[3072]{0:T(1024)} %tile.144, f32[3072]{0:T(1024)} %tile.142, f32[3072]{0:T(1024)} %tile.140, f32[3072]{0:T(1024)} %tile.138, f32[3072]{0:T(1024)} %tile.136, ...), kind=kLoop, calls=%fused_computation.394 | loop fusion | flops 5505024 | bytes 15814656 | tf_op jit(solution)/shard_map/mul | solution.py:48
  91.0 0.0 copy-start.69
  91.0 4.9 %collective-permute-start.1 = (f32[6,3072]{1,0:T(8,128)S(1)}, f32[6,3072]{1,0:T(8,128)S(1)}, u32[]{:S(2)}, u32[]{:S(2)}) collective-permute-start(f32[6,3072]{1,0:T(8,128)S(1)} %slice.1059), channel_id=1, source_target_pairs={{0,2},{2,4},{4,6},{6,8},{8,10},{10,12},{12,14},{14,16},{16,18},{18... | collective-permute-start | bytes 221192 | tf_op jit(solution)/shard_map/ppermute | solution.py:12
  96.0 0.2 fusion.81
  96.2 0.0 copy-start.7
  96.4 2.5 %fusion.77 = bf16[1,128,3072]{2,1,0:T(8,128)(2,1)} fusion(f32[6,3072]{1,0:T(8,128)S(1)} %copy-done.10, f32[128,3072]{1,0:T(8,128)S(1)} %copy-done.3, f32[3072]{0:T(1024)S(1)} %copy-done.69, f32[3072]{0:T(1024)S(1)} %copy-done.71, f32[3072]{0:T(1024)S(1)} %copy-done.73, f32[3072]{0:T(1024)S(1)} %copy-done.75, f32[3072]{0:T(1024)S(1)} %copy-done.77, ...), kind=kLoop, calls=%fused_computation.211 | loop fusion | flops 7864320 | bytes 2519040 | tf_op jit(solution)/shard_map/stack | solution.py:80
  99.0 0.8 slice_multiply_fusion
  99.8 0.0 copy-start.12
  99.8 1.6 multiply_reduce_fusion
  101.4 0.6 stack.153
  102.1 16.3 %multiply_reduce_fusion.21 = (f32[3072]{0:T(1024)}, f32[3072]{0:T(1024)S(1)}, f32[3072]{0:T(1024)S(1)}, f32[3072]{0:T(1024)S(1)}, f32[3072]{0:T(1024)S(1)}, /*in...) fusion(f32[3,134,3072]{2,1,0:T(8,128)} %copy-done, ...), kind=kLoop, calls=%fused_computation.198 | loop fusion | flops 19617792 | bytes 32575488 | tf_op jit(solution)/shard_map/reduce_sum | solution.py:92
  118.4 0.8 stack.129
  119.6 0.7 constant_dynamic-update-slice_fusion.14
  120.4 0.7 constant_dynamic-update-slice_fusion
  121.1 0.1 maximum_reduce_fusion
  121.2 44.8 %psum.7 = f32[4,7,384]{2,1,0:T(8,128)S(1)} all-reduce(f32[4,7,384]{2,1,0:T(8,128)S(1)} %maximum_reduce_fusion), channel_id=1, replica_groups=mesh['ctx'=16,'fsdp'=2] {'ctx','fsdp'}, use_global_device_ids=true, to_apply=%region_29.0 | all-reduce | flops 10752 | bytes 86016 | tf_op jit(solution)/shard_map/psum | solution.py:100
  165.9 0.1 dynamic-slice_multiply_fusion
  166.0 0.6 copy.11
  166.7 2.6 %multiply_convert_fusion = bf16[128,3072]{1,0:T(8,128)(2,1)} fusion(f32[128,3072]{1,0:T(8,128)} %get-tuple-element.84, f32[128,3072]{1,0:T(8,128)S(1)} %copy-done.2), kind=kLoop, calls=%fused_computation.205 | loop fusion | flops 786432 | bytes 3932160 | tf_op jit(solution)/shard_map/convert_element_type | solution.py:52
  169.4 1.7 fusion.76
  171.2 1.7 fusion.78
  172.9 1.7 pad_maximum_fusion
  (257 shorter events, 0.7 us)
Async XLA Ops:
  1.5 64.6 %collective-permute-start.2 = (bf16[12,3072]{1,0:T(8,128)(2,1)S(1)}, bf16[12,3072]{1,0:T(8,128)(2,1)S(1)}, u32[]{:S(2)}, u32[]{:S(2)}) collective-permute-start(bf16[12,3072]{1,0:T(8,128)(2,1)S(1)} %slice.930), channel_id=1, source_target_pairs={{2,0},{4,2},{6,4},{8,6},{10,8},{12,10},{14,12},{16,14},{18,16},{20... | collective-permute-start | bytes 221192 | tf_op jit(solution)/shard_map/ppermute | solution.py:12
  4.4 61.8 %collective-permute-start = (bf16[3,6,3072]{2,1,0:T(8,128)(2,1)}, bf16[3,6,3072]{2,1,0:T(8,128)(2,1)}, u32[]{:S(2)}, u32[]{:S(2)}) collective-permute-start(bf16[3,6,3072]{2,1,0:T(8,128)(2,1)} %slice.826), channel_id=1, source_target_pairs={{0,2},{2,4},{4,6},{6,8},{8,10},{10,12},{12,14},{14,16},{16,18},{18... | collective-permute-start | bytes 331784 | tf_op jit(solution)/shard_map/ppermute | solution.py:12
  11.5 59.4 %collective-permute-start.3 = (bf16[3,12,3072]{2,1,0:T(8,128)(2,1)S(1)}, bf16[3,12,3072]{2,1,0:T(8,128)(2,1)S(1)}, u32[]{:S(2)}, u32[]{:S(2)}) collective-permute-start(bf16[3,12,3072]{2,1,0:T(8,128)(2,1)S(1)} %slice.931), channel_id=1, source_target_pairs={{2,0},{4,2},{6,4},{8,6},{10,8},{12,10},{14,12},{16,14},{18,16},{20... | collective-permute-start | bytes 663560 | tf_op jit(solution)/shard_map/ppermute | solution.py:12
  44.4 21.8 %copy-start.5 = (bf16[3,128,3072]{2,1,0:T(8,128)(2,1)S(1)}, bf16[3,128,3072]{2,1,0:T(8,128)(2,1)}, u32[]{:S(2)}) copy-start(bf16[3,128,3072]{2,1,0:T(8,128)(2,1)} %param.3) | copy-start | bytes 7077892
  57.9 15.4 %copy-start.22 = (f32[3072]{0:T(1024)}, f32[3072]{0:T(1024)S(1)}, u32[]{:S(2)}) copy-start(f32[3072]{0:T(1024)S(1)} %tile.132) | copy-start | bytes 36868
  58.5 13.8 %copy-start.31 = (f32[3072]{0:T(1024)}, f32[3072]{0:T(1024)S(1)}, u32[]{:S(2)}) copy-start(f32[3072]{0:T(1024)S(1)} %tile.130) | copy-start | bytes 36868
  58.5 13.7 %copy-start.33 = (f32[3072]{0:T(1024)}, f32[3072]{0:T(1024)S(1)}, u32[]{:S(2)}) copy-start(f32[3072]{0:T(1024)S(1)} %tile.128) | copy-start | bytes 36868
  58.6 9.4 %copy-start.35 = (f32[3072]{0:T(1024)}, f32[3072]{0:T(1024)S(1)}, u32[]{:S(2)}) copy-start(f32[3072]{0:T(1024)S(1)} %tile.126) | copy-start | bytes 36868
  58.6 9.3 %copy-start.38 = (f32[3072]{0:T(1024)}, f32[3072]{0:T(1024)S(1)}, u32[]{:S(2)}) copy-start(f32[3072]{0:T(1024)S(1)} %tile.124) | copy-start | bytes 36868
  58.6 9.3 %copy-start.41 = (f32[3072]{0:T(1024)}, f32[3072]{0:T(1024)S(1)}, u32[]{:S(2)}) copy-start(f32[3072]{0:T(1024)S(1)} %tile.122) | copy-start | bytes 36868
  58.7 9.3 %copy-start.44 = (f32[3072]{0:T(1024)}, f32[3072]{0:T(1024)S(1)}, u32[]{:S(2)}) copy-start(f32[3072]{0:T(1024)S(1)} %tile.120) | copy-start | bytes 36868
  58.7 9.3 %copy-start.47 = (f32[3072]{0:T(1024)}, f32[3072]{0:T(1024)S(1)}, u32[]{:S(2)}) copy-start(f32[3072]{0:T(1024)S(1)} %tile.118) | copy-start | bytes 36868
  58.8 14.6 %copy-start.13 = (f32[3072]{0:T(1024)}, f32[3072]{0:T(1024)S(1)}, u32[]{:S(2)}) copy-start(f32[3072]{0:T(1024)S(1)} %tile.170) | copy-start | bytes 36868
  58.8 14.6 %copy-start.16 = (f32[3072]{0:T(1024)}, f32[3072]{0:T(1024)S(1)}, u32[]{:S(2)}) copy-start(f32[3072]{0:T(1024)S(1)} %tile.168) | copy-start | bytes 36868
  58.8 14.5 %copy-start.19 = (f32[3072]{0:T(1024)}, f32[3072]{0:T(1024)S(1)}, u32[]{:S(2)}) copy-start(f32[3072]{0:T(1024)S(1)} %tile.166) | copy-start | bytes 36868
  58.8 14.5 %copy-start.25 = (f32[3072]{0:T(1024)}, f32[3072]{0:T(1024)S(1)}, u32[]{:S(2)}) copy-start(f32[3072]{0:T(1024)S(1)} %tile.164) | copy-start | bytes 36868
  58.9 14.5 %copy-start.28 = (f32[3072]{0:T(1024)}, f32[3072]{0:T(1024)S(1)}, u32[]{:S(2)}) copy-start(f32[3072]{0:T(1024)S(1)} %tile.162) | copy-start | bytes 36868
  68.0 5.4 %copy-start = (f32[3,134,3072]{2,1,0:T(8,128)}, f32[3,134,3072]{2,1,0:T(8,128)S(1)}, u32[]{:S(2)}) copy-start(f32[3,134,3072]{2,1,0:T(8,128)S(1)} %maximum_convert_fusion) | copy-start | bytes 14819332
  68.0 3.0 %copy-start.50 = (f32[3072]{0:T(1024)S(1)}, f32[3072]{0:T(1024)}, u32[]{:S(2)}) copy-start(f32[3072]{0:T(1024)} %tile.160) | copy-start | bytes 36868
  68.0 3.0 %copy-start.52 = (f32[3072]{0:T(1024)S(1)}, f32[3072]{0:T(1024)}, u32[]{:S(2)}) copy-start(f32[3072]{0:T(1024)} %tile.158) | copy-start | bytes 36868
  68.0 3.0 %copy-start.54 = (f32[3072]{0:T(1024)S(1)}, f32[3072]{0:T(1024)}, u32[]{:S(2)}) copy-start(f32[3072]{0:T(1024)} %tile.156) | copy-start | bytes 36868
  68.0 3.0 %copy-start.56 = (f32[3072]{0:T(1024)S(1)}, f32[3072]{0:T(1024)}, u32[]{:S(2)}) copy-start(f32[3072]{0:T(1024)} %tile.154) | copy-start | bytes 36868
  68.0 3.0 %copy-start.58 = (f32[3072]{0:T(1024)S(1)}, f32[3072]{0:T(1024)}, u32[]{:S(2)}) copy-start(f32[3072]{0:T(1024)} %tile.152) | copy-start | bytes 36868
  68.0 3.0 %copy-start.60 = (f32[3072]{0:T(1024)S(1)}, f32[3072]{0:T(1024)}, u32[]{:S(2)}) copy-start(f32[3072]{0:T(1024)} %tile.150) | copy-start | bytes 36868
  68.1 3.0 %copy-start.62 = (f32[3072]{0:T(1024)S(1)}, f32[3072]{0:T(1024)}, u32[]{:S(2)}) copy-start(f32[3072]{0:T(1024)} %tile.148) | copy-start | bytes 36868
  68.1 3.0 %copy-start.64 = (f32[3072]{0:T(1024)S(1)}, f32[3072]{0:T(1024)}, u32[]{:S(2)}) copy-start(f32[3072]{0:T(1024)} %tile.134) | copy-start | bytes 36868
  68.1 3.0 %copy-start.66 = (f32[3072]{0:T(1024)S(1)}, f32[3072]{0:T(1024)}, u32[]{:S(2)}) copy-start(f32[3072]{0:T(1024)} %tile.136) | copy-start | bytes 36868
  68.1 3.0 %copy-start.68 = (f32[3072]{0:T(1024)S(1)}, f32[3072]{0:T(1024)}, u32[]{:S(2)}) copy-start(f32[3072]{0:T(1024)} %tile.146) | copy-start | bytes 36868
  68.1 3.0 %copy-start.70 = (f32[3072]{0:T(1024)S(1)}, f32[3072]{0:T(1024)}, u32[]{:S(2)}) copy-start(f32[3072]{0:T(1024)} %tile.144) | copy-start | bytes 36868
  68.1 3.0 %copy-start.72 = (f32[3072]{0:T(1024)S(1)}, f32[3072]{0:T(1024)}, u32[]{:S(2)}) copy-start(f32[3072]{0:T(1024)} %tile.142) | copy-start | bytes 36868
  68.1 3.0 %copy-start.74 = (f32[3072]{0:T(1024)S(1)}, f32[3072]{0:T(1024)}, u32[]{:S(2)}) copy-start(f32[3072]{0:T(1024)} %tile.140) | copy-start | bytes 36868
  68.1 3.0 %copy-start.76 = (f32[3072]{0:T(1024)S(1)}, f32[3072]{0:T(1024)}, u32[]{:S(2)}) copy-start(f32[3072]{0:T(1024)} %tile.138) | copy-start | bytes 36868
  82.5 13.5 %copy-start.23 = (f32[3072]{0:T(1024)S(1)}, f32[3072]{0:T(1024)}, u32[]{:S(2)}) copy-start(f32[3072]{0:T(1024)} %copy-done.22) | copy-start | bytes 36868
  82.5 13.5 %copy-start.26 = (f32[3072]{0:T(1024)S(1)}, f32[3072]{0:T(1024)}, u32[]{:S(2)}) copy-start(f32[3072]{0:T(1024)} %copy-done.25) | copy-start | bytes 36868
  82.5 13.5 %copy-start.29 = (f32[3072]{0:T(1024)S(1)}, f32[3072]{0:T(1024)}, u32[]{:S(2)}) copy-start(f32[3072]{0:T(1024)} %copy-done.28) | copy-start | bytes 36868
  90.9 5.3 %copy-start.84 = (f32[1,1,8,384]{3,2,1,0:T(8,128)S(1)}, f32[1,1,8,384]{3,2,1,0:T(8,128)}, u32[]{:S(2)}) copy-start(f32[1,1,8,384]{3,2,1,0:T(8,128)} %stack.132) | copy-start | bytes 36868
  90.9 5.4 %copy-start.83 = (f32[1,1,8,384]{3,2,1,0:T(8,128)S(1)}, f32[1,1,8,384]{3,2,1,0:T(8,128)}, u32[]{:S(2)}) copy-start(f32[1,1,8,384]{3,2,1,0:T(8,128)} %stack.133) | copy-start | bytes 36868
  90.9 5.4 %copy-start.82 = (f32[1,1,8,384]{3,2,1,0:T(8,128)S(1)}, f32[1,1,8,384]{3,2,1,0:T(8,128)}, u32[]{:S(2)}) copy-start(f32[1,1,8,384]{3,2,1,0:T(8,128)} %stack.134) | copy-start | bytes 36868
  90.9 5.4 %copy-start.81 = (f32[1,1,8,384]{3,2,1,0:T(8,128)S(1)}, f32[1,1,8,384]{3,2,1,0:T(8,128)}, u32[]{:S(2)}) copy-start(f32[1,1,8,384]{3,2,1,0:T(8,128)} %stack.135) | copy-start | bytes 36868
  90.9 5.4 %copy-start.3 = (f32[128,3072]{1,0:T(8,128)S(1)}, f32[128,3072]{1,0:T(8,128)}, u32[]{:S(2)}) copy-start(f32[128,3072]{1,0:T(8,128)} %get-tuple-element.72) | copy-start | bytes 4718596
  90.9 5.4 %copy-start.10 = (f32[6,3072]{1,0:T(8,128)S(1)}, f32[6,3072]{1,0:T(8,128)}, u32[]{:S(2)}) copy-start(f32[6,3072]{1,0:T(8,128)} %get-tuple-element.81) | copy-start | bytes 221188
  91.0 5.4 %copy-start.65 = (f32[3072]{0:T(1024)S(1)}, f32[3072]{0:T(1024)}, u32[]{:S(2)}) copy-start(f32[3072]{0:T(1024)} %tile.134) | copy-start | bytes 36868
  91.0 5.4 %copy-start.67 = (f32[3072]{0:T(1024)S(1)}, f32[3072]{0:T(1024)}, u32[]{:S(2)}) copy-start(f32[3072]{0:T(1024)} %tile.136) | copy-start | bytes 36868
  91.0 5.4 %copy-start.69 = (f32[3072]{0:T(1024)S(1)}, f32[3072]{0:T(1024)}, u32[]{:S(2)}) copy-start(f32[3072]{0:T(1024)} %tile.146) | copy-start | bytes 36868
  91.0 5.4 %copy-start.71 = (f32[3072]{0:T(1024)S(1)}, f32[3072]{0:T(1024)}, u32[]{:S(2)}) copy-start(f32[3072]{0:T(1024)} %tile.144) | copy-start | bytes 36868
  91.0 5.4 %copy-start.73 = (f32[3072]{0:T(1024)S(1)}, f32[3072]{0:T(1024)}, u32[]{:S(2)}) copy-start(f32[3072]{0:T(1024)} %tile.142) | copy-start | bytes 36868
  91.0 5.4 %copy-start.75 = (f32[3072]{0:T(1024)S(1)}, f32[3072]{0:T(1024)}, u32[]{:S(2)}) copy-start(f32[3072]{0:T(1024)} %tile.140) | copy-start | bytes 36868
  91.0 5.4 %copy-start.77 = (f32[3072]{0:T(1024)S(1)}, f32[3072]{0:T(1024)}, u32[]{:S(2)}) copy-start(f32[3072]{0:T(1024)} %tile.138) | copy-start | bytes 36868
  91.0 8.7 %collective-permute-start.1 = (f32[6,3072]{1,0:T(8,128)S(1)}, f32[6,3072]{1,0:T(8,128)S(1)}, u32[]{:S(2)}, u32[]{:S(2)}) collective-permute-start(f32[6,3072]{1,0:T(8,128)S(1)} %slice.1059), channel_id=1, source_target_pairs={{0,2},{2,4},{4,6},{6,8},{8,10},{10,12},{12,14},{14,16},{16,18},{18... | collective-permute-start | bytes 221192 | tf_op jit(solution)/shard_map/ppermute | solution.py:12
  96.2 2.7 %copy-start.7 = (f32[12,3072]{1,0:T(8,128)S(1)}, f32[12,3072]{1,0:T(8,128)}, u32[]{:S(2)}) copy-start(f32[12,3072]{1,0:T(8,128)} %get-tuple-element.80) | copy-start | bytes 442372
  96.2 2.7 %copy-start.11 = (f32[6,3072]{1,0:T(8,128)S(1)}, f32[6,3072]{1,0:T(8,128)}, u32[]{:S(2)}) copy-start(f32[6,3072]{1,0:T(8,128)} %get-tuple-element.82) | copy-start | bytes 221188
  96.2 2.7 %copy-start.14 = (f32[3072]{0:T(1024)S(1)}, f32[3072]{0:T(1024)}, u32[]{:S(2)}) copy-start(f32[3072]{0:T(1024)} %copy-done.13) | copy-start | bytes 36868
  96.2 2.7 %copy-start.17 = (f32[3072]{0:T(1024)S(1)}, f32[3072]{0:T(1024)}, u32[]{:S(2)}) copy-start(f32[3072]{0:T(1024)} %copy-done.16) | copy-start | bytes 36868
  96.3 2.7 %copy-start.20 = (f32[3072]{0:T(1024)S(1)}, f32[3072]{0:T(1024)}, u32[]{:S(2)}) copy-start(f32[3072]{0:T(1024)} %copy-done.19) | copy-start | bytes 36868
  96.4 3.3 %copy-start.80 = (f32[1,1,8,384]{3,2,1,0:T(8,128)S(1)}, f32[1,1,8,384]{3,2,1,0:T(8,128)}, u32[]{:S(2)}) copy-start(f32[1,1,8,384]{3,2,1,0:T(8,128)} %stack.136) | copy-start | bytes 36868
  102.1 18.3 %copy-start.79 = (f32[1,7,8,384]{3,2,1,0:T(8,128)S(1)}, f32[1,7,8,384]{3,2,1,0:T(8,128)}, u32[]{:S(2)}) copy-start(f32[1,7,8,384]{3,2,1,0:T(8,128)} %copy-done.78) | copy-start | bytes 258052
  118.4 48.3 %copy-start.2 = (f32[128,3072]{1,0:T(8,128)S(1)}, f32[128,3072]{1,0:T(8,128)}, u32[]{:S(2)}) copy-start(f32[128,3072]{1,0:T(8,128)} %get-tuple-element.77) | copy-start | bytes 4718596
  166.6 2.7 %copy-start.32 = (f32[3072]{0:T(1024)S(1)}, f32[3072]{0:T(1024)}, u32[]{:S(2)}) copy-start(f32[3072]{0:T(1024)} %copy-done.31) | copy-start | bytes 36868
  166.7 2.7 %copy-start.34 = (f32[3072]{0:T(1024)S(1)}, f32[3072]{0:T(1024)}, u32[]{:S(2)}) copy-start(f32[3072]{0:T(1024)} %copy-done.33) | copy-start | bytes 36868
  166.7 2.7 %copy-start.37 = (f32[3072]{0:T(1024)S(1)}, f32[3072]{0:T(1024)}, u32[]{:S(2)}) copy-start(f32[3072]{0:T(1024)} %copy-done.35) | copy-start | bytes 36868
  166.7 2.7 %copy-start.40 = (f32[3072]{0:T(1024)S(1)}, f32[3072]{0:T(1024)}, u32[]{:S(2)}) copy-start(f32[3072]{0:T(1024)} %copy-done.38) | copy-start | bytes 36868
  166.7 2.7 %copy-start.43 = (f32[3072]{0:T(1024)S(1)}, f32[3072]{0:T(1024)}, u32[]{:S(2)}) copy-start(f32[3072]{0:T(1024)} %copy-done.41) | copy-start | bytes 36868
  166.7 2.7 %copy-start.46 = (f32[3072]{0:T(1024)S(1)}, f32[3072]{0:T(1024)}, u32[]{:S(2)}) copy-start(f32[3072]{0:T(1024)} %copy-done.44) | copy-start | bytes 36868
  166.7 2.7 %copy-start.49 = (f32[3072]{0:T(1024)S(1)}, f32[3072]{0:T(1024)}, u32[]{:S(2)}) copy-start(f32[3072]{0:T(1024)} %copy-done.47) | copy-start | bytes 36868
  (25 other events, 47.9 us)
where the time goes:
time: 175 us
  local copies, waits for them, and re-layouts  61.2 us (35%)
  other arithmetic  50.5 us (29%)
  blocking collectives  46.9 us (27%)
  starting transfers between devices  13.6 us (8%)
  between operations  2.45 us (1%)
    psum x1, blocking collectives, per_device(): summed = lax.psum(partial_sum, ('ctx', 'fsdp'))  44.8 us
    slice x2, local copies, waits for them, and re-layouts, causal(): result = weights[0] * extended[reach:reach + length]  41.3 us
    reduce_sum x3, other arithmetic, per_device(): jnp.sum(grad_term * source[reach - lag:reach - lag + length], axis=0)  23.4 us
    ppermute x4, starting transfers between devices, from_behind(): return lax.ppermute(shard, axis, pairs)  13.6 us
    another operation x56, local copies, waits for them, and re-layouts, per_device(): weights = jnp.tile(gathered, (1, 1, repeats))  8.55 us
    mul x1, other arithmetic, per_device(): product = k_conv * v_conv  8.38 us
    another operation x4, other arithmetic, per_device(): feature_grads = jnp.stack([grad_q, grad_k, grad_v]).astype(jnp.bfloat16)  7.53 us
    another operation x30, local copies, waits for them, and re-layouts, per_device(): jnp.stack([jnp.sum(grad_term * source[reach - lag:reach - lag + length],...  6.53 us
  transfers between devices with their start and end apart: 4, of which 0 were waited for; matrix products, arithmetic and copies ran while one was open for 35% of the time, Pallas kernels for 0%

commit v1 on v0

v1 whole, which is shorter than its diff:
```python
import functools
import math

import jax
import jax.numpy as jnp
from jax import lax
from jax.experimental import pallas as pl
from jax.experimental.pallas import tpu as pltpu
from jax.sharding import PartitionSpec as P

LANES = 128
PAD = 16
STEP = 16


def shift_rows(value, axis, by):
    size = lax.axis_size(axis)
    pairs = [(i, i + by) for i in range(size) if 0 <= i + by < size]
    return lax.ppermute(value, axis, pairs)


def gather_filters(shard, axis):
    size = lax.axis_size(axis)
    if size != 2:
        return lax.all_gather(shard, axis, axis=2, tiled=True)
    other = lax.ppermute(shard, axis, [(0, 1), (1, 0)])
    first = lax.axis_index(axis) == 0
    return jnp.concatenate(
        [jnp.where(first, shard, other), jnp.where(first, other, shard)], axis=2
    )


def sum_over(value, axis):
    size = lax.axis_size(axis)
    if size & (size - 1):
        return lax.psum(value, axis)
    hop = 1
    while hop < size:
        value = value + lax.ppermute(value, axis, [(i, i ^ hop) for i in range(size)])
        hop *= 2
    return value


def sum_scatter(value, axis):
    size = lax.axis_size(axis)
    portion = value.shape[-1] // size
    if size != 2:
        total = sum_over(value, axis)
        return lax.dynamic_slice_in_dim(
            total, lax.axis_index(axis) * portion, portion, value.ndim - 1
        )
    first = lax.axis_index(axis) == 0
    low, high = value[..., :portion], value[..., portion:]
    sent = lax.ppermute(jnp.where(first, high, low), axis, [(0, 1), (1, 0)])
    return jnp.where(first, low, high) + sent


def kernel(
    taps,
    features_ref,
    cotangent_ref,
    weights_ref,
    before_ref,
    after_ref,
    mixed_ref,
    grads_ref,
    sums_ref,
    q_s,
    k_s,
    v_s,
    c_s,
    kc_s,
    vc_s,
    p_s,
    gq_s,
    gm_s,
    gk_s,
    gv_s,
    b_s,
    a_s,
):
    reach = taps - 1
    length = cotangent_ref.shape[0]
    columns = cotangent_ref.shape[1] // LANES

    @pl.when(pl.program_id(0) == 0)
    def _():
        sums_ref[...] = jnp.zeros_like(sums_ref)

    def causal(ref, w, start):
        total = None
        for lag in range(taps):
            term = w[lag] * ref[pl.ds(PAD + start - lag, STEP), :]
            total = term if total is None else total + term
        return total

    def anticausal(ref, w, start, source):
        total = None
        products = []
        for lag in range(taps):
            piece = ref[pl.ds(PAD + start + lag, STEP), :]
            term = w[lag] * piece
            total = term if total is None else total + term
            if source is not None:
                both = source * piece
                products.append(both[:8] + both[8:])
        return total, products

    def column(index, carry):
        lanes = pl.ds(pl.multiple_of(index * LANES, LANES), LANES)

        def weights(bank):
            return [weights_ref[bank, pl.ds(lag, 1), lanes] for lag in range(taps)]

        for bank, ref in enumerate((q_s, k_s, v_s)):
            ref[PAD : PAD + length, :] = features_ref[bank, :, lanes].astype(jnp.float32)
        c_s[PAD : PAD + length, :] = cotangent_ref[:, lanes].astype(jnp.float32)
        b_s[...] = before_ref[:, lanes].astype(jnp.float32)
        a_s[...] = after_ref[:, lanes].astype(jnp.float32)
        q_s[PAD - reach : PAD, :] = b_s[0:reach, :]
        k_s[PAD - 2 * reach : PAD, :] = b_s[reach : 3 * reach, :]
        v_s[PAD - 2 * reach : PAD, :] = b_s[3 * reach : 5 * reach, :]
        end = PAD + length
        q_s[end : end + 2 * reach, :] = a_s[0 : 2 * reach, :]
        c_s[end : end + 2 * reach, :] = a_s[2 * reach : 4 * reach, :]
        k_s[end : end + reach, :] = a_s[4 * reach : 5 * reach, :]
        v_s[end : end + reach, :] = a_s[5 * reach : 6 * reach, :]

        wk, wv = weights(1), weights(2)
        for start in range(-8, length + 8, STEP):
            rows = pl.ds(PAD + start, STEP)
            kc = causal(k_s, wk, start)
            vc = causal(v_s, wv, start)
            kc_s[rows, :] = kc
            vc_s[rows, :] = vc
            p_s[rows, :] = kc * vc
        wq, wm = weights(0), weights(3)
        for start in range(0, length + PAD, STEP):
            rows = pl.ds(PAD + start, STEP)
            upstream = c_s[rows, :]
            qc = causal(q_s, wq, start)
            gm_s[rows, :] = upstream * qc
            if start < length:
                mixer = causal(p_s, wm, start)
                mixed_ref[pl.ds(start, STEP), lanes] = (qc * mixer).astype(mixed_ref.dtype)
                gq_s[rows, :] = upstream * mixer
            else:
                rows = pl.ds(PAD + start, 8)
                mixer = None
                for lag in range(taps):
                    term = wm[lag] * p_s[pl.ds(PAD + start - lag, 8), :]
                    mixer = term if mixer is None else mixer + term
                gq_s[rows, :] = upstream[:8] * mixer
        sums = [[None] * taps for _ in range(4)]

        def collect(bank, products):
            for lag, value in enumerate(products):
                old = sums[bank][lag]
                sums[bank][lag] = value if old is None else old + value

        for start in range(0, length, STEP):
            rows = pl.ds(PAD + start, STEP)
            gp, products = anticausal(gm_s, wm, start, p_s[rows, :])
            collect(3, products)
            gk_s[rows, :] = gp * vc_s[rows, :]
            gv_s[rows, :] = gp * kc_s[rows, :]
        rows = pl.ds(PAD + length, 8)
        gp = None
        for lag in range(taps):
            term = wm[lag] * gm_s[pl.ds(PAD + length + lag, 8), :]
            gp = term if gp is None else gp + term
        gk_s[rows, :] = gp * vc_s[rows, :]
        gv_s[rows, :] = gp * kc_s[rows, :]
        for bank, (grad, source, w) in enumerate(
            ((gq_s, q_s, wq), (gk_s, k_s, wk), (gv_s, v_s, wv))
        ):
            for start in range(0, length, STEP):
                rows = pl.ds(PAD + start, STEP)
                value, products = anticausal(grad, w, start, source[rows, :])
                collect(bank, products)
                grads_ref[bank, pl.ds(start, STEP), lanes] = value.astype(grads_ref.dtype)
        for bank in range(4):
            for lag in range(taps):
                sums_ref[bank, lag, :, lanes] += sums[bank][lag]
        return carry

    lax.fori_loop(0, columns, column, 0)


def local_work(features, cotangent, weights, before, after):
    banks, length, channels = features.shape
    taps, groups = weights.shape[1:]
    repeats = channels // groups
    room = length + 2 * PAD
    scratch = [pltpu.VMEM((room, LANES), jnp.float32) for _ in range(11)]
    scratch += [
        pltpu.VMEM((before.shape[0], LANES), jnp.float32),
        pltpu.VMEM((after.shape[0], LANES), jnp.float32),
    ]
    return pl.pallas_call(
        functools.partial(kernel, taps),
        grid=(repeats,),
        out_shape=(
            jax.ShapeDtypeStruct(cotangent.shape, cotangent.dtype),
            jax.ShapeDtypeStruct(features.shape, features.dtype),
            jax.ShapeDtypeStruct((4, taps, 8, groups), jnp.float32),
        ),
        in_specs=[
            pl.BlockSpec((banks, length, groups), lambda i: (0, 0, i)),
            pl.BlockSpec((length, groups), lambda i: (0, i)),
            pl.BlockSpec(weights.shape, lambda i: (0, 0, 0)),
            pl.BlockSpec((before.shape[0], groups), lambda i: (0, i)),
            pl.BlockSpec((after.shape[0], groups), lambda i: (0, i)),
        ],
        out_specs=(
            pl.BlockSpec((length, groups), lambda i: (0, i)),
            pl.BlockSpec((banks, length, groups), lambda i: (0, 0, i)),
            pl.BlockSpec((4, taps, 8, groups), lambda i: (0, 0, 0, 0)),
        ),
        scratch_shapes=scratch,
        compiler_params=pltpu.CompilerParams(vmem_limit_bytes=32 * 1024 * 1024),
        name="local_work",
    )(features, cotangent, weights, before, after)


def per_device(features, cotangent, master_filters):
    reach = master_filters.shape[1] - 1
    length = features.shape[1]
    weights = gather_filters(master_filters.astype(jnp.bfloat16), "fsdp").astype(jnp.float32)
    tail = jnp.concatenate(
        [
            features[0, length - reach :],
            features[1, length - 2 * reach :],
            features[2, length - 2 * reach :],
        ],
        axis=0,
    )
    head = jnp.concatenate(
        [features[0, : 2 * reach], cotangent[: 2 * reach], features[1, :reach], features[2, :reach]],
        axis=0,
    )
    before = shift_rows(tail, "ctx", 1)
    after = shift_rows(head, "ctx", -1)
    mixed, feature_grads, sums = local_work(features, cotangent, weights, before, after)
    partial_sum = jnp.sum(sums, axis=2)
    repeats = features.shape[2] // weights.shape[2]
    count_all = length * lax.axis_size("ctx") * repeats * lax.axis_size("fsdp")
    factor = 1.0 / math.sqrt(count_all)
    filter_grads = sum_over(sum_scatter(partial_sum, "fsdp"), "ctx") * factor
    return (mixed, feature_grads, filter_grads)


def solution(mesh):
    return jax.shard_map(
        per_device,
        mesh=mesh,
        in_specs=(P(None, "ctx", "fsdp"), P("ctx", "fsdp"), P(None, None, "fsdp")),
        out_specs=(P("ctx", "fsdp"), P(None, "ctx", "fsdp"), P(None, None, "fsdp")),
        check_vma=False,
    )
```

time: 175 us -> 52.7 us (0.30)
  local copies, waits for them, and re-layouts: 61.2 us -> 5.92 us
  other arithmetic: 50.5 us -> 1.26 us
  blocking collectives: 46.9 us -> 0 us
  waiting for transfers between devices: 0.01 us -> 19 us
  Pallas kernels: 0 us -> 11.6 us
  between operations: 2.45 us -> 0.7 us
    psum x1 -> x0, blocking collectives: 44.8 us -> none  [per_device(): summed = lax.psum(partial_sum, ('ctx', 'fsdp'))]
    slice x6 -> x0, local copies, waits for them, and re-layouts: 43.9 us -> none  [the longest x2 41.3 us: causal(): result = weights[0] * extended[reach:reach + length]]
    reduce_sum x4 -> x1, other arithmetic: 23.5 us -> 0.08 us  [per_device(): partial_sum = jnp.sum(sums, axis=2)]
    ppermute x4 -> x8, waiting for transfers between devices: 0.01 us -> 19 us  [the longest x4 8.99 us: sum_over(): lax.ppermute(value, axis, [(i, i ^ hop) for i in range(size)])]
    another operation x86 -> x0, local copies, waits for them, and re-layouts: 15.1 us -> none  [the longest x56 8.55 us: per_device(): weights = jnp.tile(gathered, (1, 1, repeats))]
    mul x7 -> x1, other arithmetic: 14.1 us -> 0.01 us  [per_device(): filter_grads = sum_over(sum_scatter(partial_sum, 'fsdp'), 'ctx') * factor]
    pallas_call x0 -> x1, Pallas kernels: none -> 11.6 us  [local_work(): pl.pallas_call(functools.partial(kernel, taps), grid=(repeats,), out_shap...]
    another operation x4 -> x0, other arithmetic: 7.53 us -> none  [per_device(): feature_grads = jnp.stack([grad_q, grad_k, grad_v]).astype(jnp.bfloat16)]
  transfers between devices with their start and end apart: 4 -> 8, of which waited for: 0 -> 7; matrix products, arithmetic and copies ran while one was open for 35% -> 7% of each run, Pallas kernels for 0% -> 0%
where the time goes in v1:
time: 52.7 us; the launch traced here: 52.3 us
  waiting for transfers between devices  19 us (36%)
  starting transfers between devices  13.7 us (26%)
  Pallas kernels  11.6 us (22%)
  local copies, waits for them, and re-layouts  5.92 us (11%)
  other arithmetic  1.26 us (2%)
  between operations  0.7 us (1%)
    pallas_call x1, Pallas kernels, local_work(): pl.pallas_call(functools.partial(kernel, taps), grid=(repeats,), out_shap...  11.6 us
    ppermute x4, waiting for transfers between devices, sum_over(): lax.ppermute(value, axis, [(i, i ^ hop) for i in range(size)])  8.99 us
    ppermute x2, waiting for transfers between devices, shift_rows(): return lax.ppermute(value, axis, pairs)  8.86 us
    ppermute x4, starting transfers between devices, sum_over(): lax.ppermute(value, axis, [(i, i ^ hop) for i in range(size)])  7.57 us
    ppermute x2, starting transfers between devices, shift_rows(): return lax.ppermute(value, axis, pairs)  5.71 us
    unnamed x6, local copies, waits for them, and re-layouts  3.12 us
    ppermute x1, waiting for transfers between devices, sum_scatter(): sent = lax.ppermute(jnp.where(first, high, low), axis, [(0, 1), (1, 0)])  1.19 us
  transfers between devices with their start and end apart: 8, of which 7 were waited for; matrix products, arithmetic and copies ran while one was open for 7% of the time, Pallas kernels for 0%

profile of v1, /device:TPU:0, one launch (start us, length us, event | category | flops | bytes accessed | tf_op | source)
XLA Modules:
  0.0 52.3 jit_solution(16644776312282495778)
XLA Ops:
  0.6 0.0 copy-start.1
  0.6 0.8 %copy.9 = bf16[4,7,192]{2,1,0:T(8,128)(2,1)S(1)} copy(f32[4,7,192]{2,0,1:T(4,128)} %param.5) | data formatting | bytes 32256 | tf_op args[2]
  1.5 0.5 collective-permute-start
  1.9 0.9 %slice_bitcast_fusion.4 = (bf16[6,3072]{1,0:T(8,128)(2,1)S(1)}, bf16[6,3072]{1,0:T(8,128)(2,1)S(1)}, bf16[6,3072]{1,0:T(8,128)(2,1)S(1)}) fusion(bf16[3,128,3072]{2,1,0:T(8,128)(2,1)} %features_ref.1), kind=kLoop, calls=%fused_computation.6 | loop fusion | bytes 221184 | tf_op jit(solution)/shard_map/squeeze | solution.py:239
  2.8 1.0 %slice_bitcast_fusion = (bf16[12,3072]{1,0:T(8,128)(2,1)S(1)}, bf16[12,3072]{1,0:T(8,128)(2,1)S(1)}, bf16[12,3072]{1,0:T(8,128)(2,1)S(1)}) fusion(bf16[3,128,3072]{2,1,0:T(8,128)(2,1)} %features_ref.1), kind=kLoop, calls=%fused_computation.2 | loop fusion | bytes 442368 | tf_op jit(solution)/shard_map/squeeze | solution.py:239
  3.8 0.1 pad_maximum_fusion.1
  3.9 4.4 %collective-permute-start.1 = (bf16[30,3072]{1,0:T(8,128)(2,1)S(1)}, bf16[30,3072]{1,0:T(8,128)(2,1)S(1)}, u32[]{:S(2)}, u32[]{:S(2)}) collective-permute-start(bf16[30,3072]{1,0:T(8,128)(2,1)S(1)} %pad_maximum_fusion.1), channel_id=1, source_target_pairs={{0,2},{2,4},{4,6},{6,8},{8,10},{10,12},{12,14},{14,16},{16,18},{18... | collective-permute-start | bytes 552968 | tf_op jit(solution)/shard_map/ppermute | solution.py:19
  8.3 0.9 %slice.31 = bf16[12,3072]{1,0:T(8,128)(2,1)S(1)} slice(bf16[128,3072]{1,0:T(8,128)(2,1)} %cotangent_ref.1), slice={[0:12], [0:3072]} | slice | bytes 147456 | tf_op jit(solution)/shard_map/slice | solution.py:239
  9.2 0.1 pad_maximum_fusion
  9.3 1.3 %collective-permute-start.2 = (bf16[36,3072]{1,0:T(8,128)(2,1)S(1)}, bf16[36,3072]{1,0:T(8,128)(2,1)S(1)}, u32[]{:S(2)}, u32[]{:S(2)}) collective-permute-start(bf16[36,3072]{1,0:T(8,128)(2,1)S(1)} %pad_maximum_fusion), channel_id=1, source_target_pairs={{2,0},{4,2},{6,4},{8,6},{10,8},{12,10},{14,12},{16,14},{18,16},{20... | collective-permute-start | bytes 663560 | tf_op jit(solution)/shard_map/ppermute | solution.py:19
  10.6 0.0 collective-permute-done
  10.6 0.8 %broadcast_select_fusion.1 = (bf16[4,7,192]{2,1,0:T(8,128)(2,1)S(1)}, bf16[4,7,192]{2,1,0:T(8,128)(2,1)S(1)}) fusion(bf16[4,7,192]{2,1,0:T(8,128)(2,1)S(1)} %collective-permute-done, pred[]{:T(512)S(6)} %eq.4, f32[4,7,192]{2,0,1:T(4,128)} %param.5), kind=kLoop, calls=%fused_computation.14 | loop fusion | flops 10752 | bytes 53761 | tf_op jit(solution)/shard_map/jit(_where)/select_n | solution.py:29
  11.4 0.1 maximum_convert_fusion.weights_ref
  11.5 1.6 %collective-permute-done.1.before_ref = bf16[30,3072]{1,0:T(8,128)(2,1)S(1)} collective-permute-done((bf16[30,3072]{1,0:T(8,128)(2,1)S(1)}, bf16[30,3072]{1,0:T(8,128)(2,1)S(1)}, u32[]{:S(2)}, u32[]{:S(2)}) %collective-permute-start.1) | collective-permute-done | bytes 184352 | tf_op jit(solution)/shard_map/ppermute | solution.py:19
  13.1 7.2 %collective-permute-done.2.after_ref = bf16[36,3072]{1,0:T(8,128)(2,1)S(1)} collective-permute-done((bf16[36,3072]{1,0:T(8,128)(2,1)S(1)}, bf16[36,3072]{1,0:T(8,128)(2,1)S(1)}, u32[]{:S(2)}, u32[]{:S(2)}) %collective-permute-start.2) | collective-permute-done | bytes 221216 | tf_op jit(solution)/shard_map/ppermute | solution.py:19
  20.3 0.0 copy-done.1
  20.3 0.0 copy-start
  20.3 1.7 %copy-done = bf16[3,128,3072]{2,1,0:T(8,128)(2,1)S(1)} copy-done((bf16[3,128,3072]{2,1,0:T(8,128)(2,1)S(1)}, bf16[3,128,3072]{2,1,0:T(8,128)(2,1)}, u32[]{:S(2)}) %copy-start) | copy-done | bytes 2359320
  22.0 11.6 %local_work.1 = (bf16[128,3072]{1,0:T(8,128)(2,1)}, bf16[3,128,3072]{2,1,0:T(8,128)(2,1)}, f32[4,7,8,384]{3,2,1,0:T(8,128)S(1)}) custom-call(bf16[3,128,3072]{2,1,0:T(8,128)(2,1)S(1)} %copy-done, bf16[128,3072]{1,0:T(8,128)(2,1)S(1)} %copy-done.1, f32[4,7,384]{2,1,0:T(8,128)S(1)} %maximum_convert_fusion.weights_ref, ...), custom_call_target="tpu_custom_call" | custom-call | tf_op jit(solution)/shard_map/local_work/pallas_call | solution.py:200
  33.7 0.1 reduce_sum.9
  33.7 0.1 slice_select_fusion
  33.8 0.0 collective-permute-start.3
  33.8 1.2 %collective-permute-done.3 = f32[4,7,192]{2,1,0:T(8,128)S(1)} collective-permute-done((f32[4,7,192]{2,1,0:T(8,128)S(1)}, f32[4,7,192]{2,1,0:T(8,128)S(1)}, u32[]{:S(2)}, u32[]{:S(2)}) %collective-permute-start.3) | collective-permute-done | bytes 21536 | tf_op jit(solution)/shard_map/ppermute | solution.py:54
  35.0 0.1 select_add_fusion
  35.1 1.5 %collective-permute-start.4 = (f32[4,7,192]{2,1,0:T(8,128)S(1)}, f32[4,7,192]{2,1,0:T(8,128)S(1)}, u32[]{:S(2)}, u32[]{:S(2)}) collective-permute-start(f32[4,7,192]{2,1,0:T(8,128)S(1)} %select_add_fusion), channel_id=1, source_target_pairs={{0,2},{2,0},{4,6},{6,4},{8,10},{10,8},{12,14},{14,12},{16,18},{18,... | collective-permute-start | bytes 64520 | tf_op jit(solution)/shard_map/ppermute | solution.py:39
  36.6 2.4 %collective-permute-done.4 = f32[4,7,192]{2,1,0:T(8,128)S(1)} collective-permute-done((f32[4,7,192]{2,1,0:T(8,128)S(1)}, f32[4,7,192]{2,1,0:T(8,128)S(1)}, u32[]{:S(2)}, u32[]{:S(2)}) %collective-permute-start.4) | collective-permute-done | bytes 21536 | tf_op jit(solution)/shard_map/ppermute | solution.py:39
  39.0 1.7 %collective-permute-start.5 = (f32[4,7,192]{2,1,0:T(8,128)S(1)}, f32[4,7,192]{2,1,0:T(8,128)S(1)}, u32[]{:S(2)}, u32[]{:S(2)}) collective-permute-start(f32[4,7,192]{2,1,0:T(8,128)S(1)} %add.16), channel_id=1, source_target_pairs={{0,4},{2,6},{4,0},{6,2},{8,12},{10,14},{12,8},{14,10},{16,20},{18,... | collective-permute-start | bytes 64520 | tf_op jit(solution)/shard_map/ppermute | solution.py:39
  40.8 2.2 %collective-permute-done.5 = f32[4,7,192]{2,1,0:T(8,128)S(1)} collective-permute-done((f32[4,7,192]{2,1,0:T(8,128)S(1)}, f32[4,7,192]{2,1,0:T(8,128)S(1)}, u32[]{:S(2)}, u32[]{:S(2)}) %collective-permute-start.5) | collective-permute-done | bytes 21536 | tf_op jit(solution)/shard_map/ppermute | solution.py:39
  43.0 1.6 %collective-permute-start.6 = (f32[4,7,192]{2,1,0:T(8,128)S(1)}, f32[4,7,192]{2,1,0:T(8,128)S(1)}, u32[]{:S(2)}, u32[]{:S(2)}) collective-permute-start(f32[4,7,192]{2,1,0:T(8,128)S(1)} %add.17), channel_id=1, source_target_pairs={{0,8},{2,10},{4,12},{6,14},{8,0},{10,2},{12,4},{14,6},{16,24},{18,... | collective-permute-start | bytes 64520 | tf_op jit(solution)/shard_map/ppermute | solution.py:39
  44.5 2.3 %collective-permute-done.6 = f32[4,7,192]{2,1,0:T(8,128)S(1)} collective-permute-done((f32[4,7,192]{2,1,0:T(8,128)S(1)}, f32[4,7,192]{2,1,0:T(8,128)S(1)}, u32[]{:S(2)}, u32[]{:S(2)}) %collective-permute-start.6) | collective-permute-done | bytes 21536 | tf_op jit(solution)/shard_map/ppermute | solution.py:39
  46.9 2.8 %collective-permute-start.7 = (f32[4,7,192]{2,1,0:T(8,128)S(1)}, f32[4,7,192]{2,1,0:T(8,128)S(1)}, u32[]{:S(2)}, u32[]{:S(2)}) collective-permute-start(f32[4,7,192]{2,1,0:T(8,128)S(1)} %add.18), channel_id=1, source_target_pairs={{0,16},{2,18},{4,20},{6,22},{8,24},{10,26},{12,28},{14,30},{16,0},... | collective-permute-start | bytes 64520 | tf_op jit(solution)/shard_map/ppermute | solution.py:39
  49.6 2.1 %collective-permute-done.7 = f32[4,7,192]{2,1,0:T(8,128)S(1)} collective-permute-done((f32[4,7,192]{2,1,0:T(8,128)S(1)}, f32[4,7,192]{2,1,0:T(8,128)S(1)}, u32[]{:S(2)}, u32[]{:S(2)}) %collective-permute-start.7) | collective-permute-done | bytes 21536 | tf_op jit(solution)/shard_map/ppermute | solution.py:39
  51.7 0.6 %copy.7 = f32[4,7,192]{2,0,1:T(4,128)} copy(f32[4,7,192]{2,1,0:T(8,128)S(1)} %add_multiply_fusion) | data formatting | bytes 43008
  (4 shorter events, 0.0 us)
Async XLA Ops:
  0.6 19.7 %copy-start.1 = (bf16[128,3072]{1,0:T(8,128)(2,1)S(1)}, bf16[128,3072]{1,0:T(8,128)(2,1)}, u32[]{:S(2)}) copy-start(bf16[128,3072]{1,0:T(8,128)(2,1)} %cotangent_ref.1) | copy-start | bytes 2359300
  1.5 9.2 %collective-permute-start = (bf16[4,7,192]{2,1,0:T(8,128)(2,1)S(1)}, bf16[4,7,192]{2,1,0:T(8,128)(2,1)S(1)}, u32[]{:S(2)}, u32[]{:S(2)}) collective-permute-start(bf16[4,7,192]{2,1,0:T(8,128)(2,1)S(1)} %copy.9), channel_id=1, source_target_pairs={{0,1},{1,0},{2,3},{3,2},{4,5},{5,4},{6,7},{7,6},{8,9},{9,8},{10,11... | collective-permute-start | bytes 32264 | tf_op jit(solution)/shard_map/ppermute | solution.py:26
  3.9 9.2 %collective-permute-start.1 = (bf16[30,3072]{1,0:T(8,128)(2,1)S(1)}, bf16[30,3072]{1,0:T(8,128)(2,1)S(1)}, u32[]{:S(2)}, u32[]{:S(2)}) collective-permute-start(bf16[30,3072]{1,0:T(8,128)(2,1)S(1)} %pad_maximum_fusion.1), channel_id=1, source_target_pairs={{0,2},{2,4},{4,6},{6,8},{8,10},{10,12},{12,14},{14,16},{16,18},{18... | collective-permute-start | bytes 552968 | tf_op jit(solution)/shard_map/ppermute | solution.py:19
  9.3 11.0 %collective-permute-start.2 = (bf16[36,3072]{1,0:T(8,128)(2,1)S(1)}, bf16[36,3072]{1,0:T(8,128)(2,1)S(1)}, u32[]{:S(2)}, u32[]{:S(2)}) collective-permute-start(bf16[36,3072]{1,0:T(8,128)(2,1)S(1)} %pad_maximum_fusion), channel_id=1, source_target_pairs={{2,0},{4,2},{6,4},{8,6},{10,8},{12,10},{14,12},{16,14},{18,16},{20... | collective-permute-start | bytes 663560 | tf_op jit(solution)/shard_map/ppermute | solution.py:19
  20.3 1.7 %copy-start = (bf16[3,128,3072]{2,1,0:T(8,128)(2,1)S(1)}, bf16[3,128,3072]{2,1,0:T(8,128)(2,1)}, u32[]{:S(2)}) copy-start(bf16[3,128,3072]{2,1,0:T(8,128)(2,1)} %features_ref.1) | copy-start | bytes 7077892
  33.8 1.2 %collective-permute-start.3 = (f32[4,7,192]{2,1,0:T(8,128)S(1)}, f32[4,7,192]{2,1,0:T(8,128)S(1)}, u32[]{:S(2)}, u32[]{:S(2)}) collective-permute-start(f32[4,7,192]{2,1,0:T(8,128)S(1)} %slice_select_fusion), channel_id=1, source_target_pairs={{0,1},{1,0},{2,3},{3,2},{4,5},{5,4},{6,7},{7,6},{8,9},{9,8},{10,11... | collective-permute-start | bytes 64520 | tf_op jit(solution)/shard_map/ppermute | solution.py:54
  35.1 3.9 %collective-permute-start.4 = (f32[4,7,192]{2,1,0:T(8,128)S(1)}, f32[4,7,192]{2,1,0:T(8,128)S(1)}, u32[]{:S(2)}, u32[]{:S(2)}) collective-permute-start(f32[4,7,192]{2,1,0:T(8,128)S(1)} %select_add_fusion), channel_id=1, source_target_pairs={{0,2},{2,0},{4,6},{6,4},{8,10},{10,8},{12,14},{14,12},{16,18},{18,... | collective-permute-start | bytes 64520 | tf_op jit(solution)/shard_map/ppermute | solution.py:39
  39.0 3.9 %collective-permute-start.5 = (f32[4,7,192]{2,1,0:T(8,128)S(1)}, f32[4,7,192]{2,1,0:T(8,128)S(1)}, u32[]{:S(2)}, u32[]{:S(2)}) collective-permute-start(f32[4,7,192]{2,1,0:T(8,128)S(1)} %add.16), channel_id=1, source_target_pairs={{0,4},{2,6},{4,0},{6,2},{8,12},{10,14},{12,8},{14,10},{16,20},{18,... | collective-permute-start | bytes 64520 | tf_op jit(solution)/shard_map/ppermute | solution.py:39
  43.0 3.9 %collective-permute-start.6 = (f32[4,7,192]{2,1,0:T(8,128)S(1)}, f32[4,7,192]{2,1,0:T(8,128)S(1)}, u32[]{:S(2)}, u32[]{:S(2)}) collective-permute-start(f32[4,7,192]{2,1,0:T(8,128)S(1)} %add.17), channel_id=1, source_target_pairs={{0,8},{2,10},{4,12},{6,14},{8,0},{10,2},{12,4},{14,6},{16,24},{18,... | collective-permute-start | bytes 64520 | tf_op jit(solution)/shard_map/ppermute | solution.py:39
  46.9 4.8 %collective-permute-start.7 = (f32[4,7,192]{2,1,0:T(8,128)S(1)}, f32[4,7,192]{2,1,0:T(8,128)S(1)}, u32[]{:S(2)}, u32[]{:S(2)}) collective-permute-start(f32[4,7,192]{2,1,0:T(8,128)S(1)} %add.18), channel_id=1, source_target_pairs={{0,16},{2,18},{4,20},{6,22},{8,24},{10,26},{12,28},{14,30},{16,0},... | collective-permute-start | bytes 64520 | tf_op jit(solution)/shard_map/ppermute | solution.py:39

commit v2 on v1

v2 whole, which is shorter than its diff:
```python
import functools
import math

import jax
import jax.numpy as jnp
from jax import lax
from jax.experimental import pallas as pl
from jax.experimental.pallas import tpu as pltpu
from jax.sharding import PartitionSpec as P

LANES = 128
TILE = 8
PAD = 16
PIECES = 2
F32 = jnp.float32


def shift_rows(value, axis, by):
    size = lax.axis_size(axis)
    pairs = [(i, i + by) for i in range(size) if 0 <= i + by < size]
    return lax.ppermute(value, axis, pairs)


def gather_filters(shard, axis):
    size = lax.axis_size(axis)
    if size != 2:
        return lax.all_gather(shard, axis, axis=2, tiled=True)
    other = lax.ppermute(shard, axis, [(0, 1), (1, 0)])
    first = lax.axis_index(axis) == 0
    return jnp.concatenate(
        [jnp.where(first, shard, other), jnp.where(first, other, shard)], axis=2
    )


def sum_over(value, axis):
    size = lax.axis_size(axis)
    if size & (size - 1):
        return lax.psum(value, axis)
    hop = 1
    while hop < size:
        value = value + lax.ppermute(value, axis, [(i, i ^ hop) for i in range(size)])
        hop *= 2
    return value


def sum_scatter(value, axis):
    size = lax.axis_size(axis)
    portion = value.shape[-1] // size
    if size != 2:
        total = sum_over(value, axis)
        return lax.dynamic_slice_in_dim(
            total, lax.axis_index(axis) * portion, portion, value.ndim - 1
        )
    first = lax.axis_index(axis) == 0
    low, high = value[..., :portion], value[..., portion:]
    sent = lax.ppermute(jnp.where(first, high, low), axis, [(0, 1), (1, 0)])
    return jnp.where(first, low, high) + sent


def column_loop(ref, body):
    def step(index, carry):
        body(pl.ds(pl.multiple_of(index * LANES, LANES), LANES), index)
        return carry

    lax.fori_loop(0, ref.shape[-1] // LANES, step, 0)


def weight_rows(ref, bank, lanes):
    return [ref[bank, pl.ds(lag, 1), lanes] for lag in range(ref.shape[1])]


def dot_taps(weights, pieces):
    total = weights[0] * pieces[0]
    for weight, piece in zip(weights[1:], pieces[1:]):
        total = total + weight * piece
    return total


def back(ref, start, taps, rows=TILE):
    return [ref[pl.ds(PAD + start - lag, rows), :] for lag in range(taps)]


def ahead(ref, start, taps, rows=TILE):
    return [ref[pl.ds(PAD + start + lag, rows), :] for lag in range(taps)]


class Sums:
    def __init__(self, taps):
        self.taps = taps
        self.held = [[None] * taps for _ in range(4)]

    def add(self, bank, grad, pieces):
        for lag, piece in enumerate(pieces):
            term = grad * piece
            old = self.held[bank][lag]
            self.held[bank][lag] = term if old is None else old + term

    def store(self, ref, lanes):
        for bank in range(4):
            for lag in range(self.taps):
                ref[bank, lag, :, lanes] += self.held[bank][lag]


def pack_kernel(reach, tail_ref, head_ref, upstream_ref, before_ref, after_ref, b_s, a_s):
    def column(lanes, _):
        def rows(ref, bank, start, stop):
            return ref[bank, :, lanes].astype(F32)[start:stop]

        b_s[0:reach, :] = rows(tail_ref, 0, PAD - reach, PAD)
        b_s[reach : 3 * reach, :] = rows(tail_ref, 1, PAD - 2 * reach, PAD)
        b_s[3 * reach : 5 * reach, :] = rows(tail_ref, 2, PAD - 2 * reach, PAD)
        before_ref[:, lanes] = b_s[...].astype(before_ref.dtype)
        a_s[0 : 2 * reach, :] = rows(head_ref, 0, 0, 2 * reach)
        a_s[2 * reach : 4 * reach, :] = upstream_ref[:, lanes].astype(F32)[: 2 * reach]
        a_s[4 * reach : 5 * reach, :] = rows(head_ref, 1, 0, reach)
        a_s[5 * reach : 6 * reach, :] = rows(head_ref, 2, 0, reach)
        after_ref[:, lanes] = a_s[...].astype(after_ref.dtype)

    column_loop(before_ref, column)


def pack(features, cotangent, reach):
    banks, length, channels = features.shape
    last = length // PAD - 1
    kind = features.dtype
    return pl.pallas_call(
        functools.partial(pack_kernel, reach),
        grid=(1,),
        out_shape=(
            jax.ShapeDtypeStruct((5 * reach, channels), kind),
            jax.ShapeDtypeStruct((6 * reach, channels), kind),
        ),
        in_specs=[
            pl.BlockSpec((banks, PAD, channels), lambda i: (0, last, 0)),
            pl.BlockSpec((banks, PAD, channels), lambda i: (0, 0, 0)),
            pl.BlockSpec((PAD, channels), lambda i: (0, 0)),
        ],
        out_specs=(
            pl.BlockSpec((5 * reach, channels), lambda i: (0, 0)),
            pl.BlockSpec((6 * reach, channels), lambda i: (0, 0)),
        ),
        scratch_shapes=[
            pltpu.VMEM((5 * reach, LANES), F32),
            pltpu.VMEM((6 * reach, LANES), F32),
        ],
        cost_estimate=pl.CostEstimate(flops=10**6, bytes_accessed=10**6, transcendentals=0),
        compiler_params=pltpu.CompilerParams(vmem_limit_bytes=8 * 1024 * 1024),
        name="pack_halos",
    )(features, features, cotangent)


def interior_kernel(
    taps,
    features_ref,
    cotangent_ref,
    weights_ref,
    mixed_ref,
    grads_ref,
    sums_ref,
    q_s,
    k_s,
    v_s,
    kc_s,
    vc_s,
    p_s,
    gm_s,
):
    length = cotangent_ref.shape[0]

    @pl.when(pl.program_id(0) == 0)
    def _():
        sums_ref[...] = jnp.zeros_like(sums_ref)

    def column(lanes, _):
        for bank, ref in enumerate((q_s, k_s, v_s)):
            ref[PAD : PAD + length, :] = features_ref[bank, :, lanes].astype(F32)
        wq, wk, wv, wm = (weight_rows(weights_ref, bank, lanes) for bank in range(4))
        for start in range(TILE, length, TILE):
            rows = pl.ds(PAD + start, TILE)
            kc = dot_taps(wk, back(k_s, start, taps))
            vc = dot_taps(wv, back(v_s, start, taps))
            kc_s[rows, :] = kc
            vc_s[rows, :] = vc
            p_s[rows, :] = kc * vc
        sums = Sums(taps)
        rows = pl.ds(PAD + TILE, TILE)
        upstream = cotangent_ref[0:PAD, lanes].astype(F32)[TILE:]
        gm_s[rows, :] = upstream * dot_taps(wq, back(q_s, TILE, taps))
        for start in range(PAD, length, PAD):
            upstream = cotangent_ref[pl.ds(start, PAD), lanes].astype(F32)
            parts = []
            for half in (0, TILE):
                rows = pl.ds(PAD + start + half, TILE)
                up = upstream[half : half + TILE]
                sources = back(q_s, start + half, taps)
                products = back(p_s, start + half, taps)
                qc = dot_taps(wq, sources)
                mixer = dot_taps(wm, products)
                gq = up * mixer
                gm = up * qc
                parts.append(qc * mixer)
                gm_s[rows, :] = gm
                grads_ref[0, pl.ds(start + half, TILE), lanes] = gq
                sums.add(0, gq, sources)
                sums.add(3, gm, products)
            mixed_ref[pl.ds(start, PAD), lanes] = jnp.concatenate(parts, axis=0).astype(
                mixed_ref.dtype
            )
        for start in range(TILE, length - TILE, TILE):
            rows = pl.ds(PAD + start, TILE)
            gp = dot_taps(wm, ahead(gm_s, start, taps))
            gk = gp * vc_s[rows, :]
            gv = gp * kc_s[rows, :]
            grads_ref[1, pl.ds(start, TILE), lanes] = gk
            grads_ref[2, pl.ds(start, TILE), lanes] = gv
            sums.add(1, gk, back(k_s, start, taps))
            sums.add(2, gv, back(v_s, start, taps))
        sums.store(sums_ref, lanes)

    column_loop(cotangent_ref, column)


def interior(features, cotangent, weights):
    banks, length, channels = features.shape
    taps, groups = weights.shape[1:]
    repeats = channels // groups
    room = length + 2 * PAD
    work = length * channels * taps * 2
    return pl.pallas_call(
        functools.partial(interior_kernel, taps),
        grid=(repeats,),
        out_shape=(
            jax.ShapeDtypeStruct(cotangent.shape, cotangent.dtype),
            jax.ShapeDtypeStruct(features.shape, F32),
            jax.ShapeDtypeStruct((4, taps, TILE, groups), F32),
        ),
        in_specs=[
            pl.BlockSpec((banks, length, groups), lambda i: (0, 0, i)),
            pl.BlockSpec((length, groups), lambda i: (0, i)),
            pl.BlockSpec(weights.shape, lambda i: (0, 0, 0)),
        ],
        out_specs=(
            pl.BlockSpec((length, groups), lambda i: (0, i)),
            pl.BlockSpec((banks, length, groups), lambda i: (0, 0, i)),
            pl.BlockSpec((4, taps, TILE, groups), lambda i: (0, 0, 0, 0)),
        ),
        scratch_shapes=[pltpu.VMEM((room, LANES), F32) for _ in range(7)],
        cost_estimate=pl.CostEstimate(
            flops=9 * work, bytes_accessed=26 * length * channels, transcendentals=0
        ),
        compiler_params=pltpu.CompilerParams(vmem_limit_bytes=24 * 1024 * 1024),
        name="interior",
    )(features, cotangent, weights)


def edge_kernel(
    taps,
    length,
    groups,
    tail_ref,
    head_ref,
    up_tail_ref,
    up_head_ref,
    weights_ref,
    before_ref,
    after_ref,
    sums_in_ref,
    _mixed_in_ref,
    mixed_ref,
    ghead_ref,
    gtail_ref,
    sums_ref,
    acc,
    b_s,
    a_s,
    qh,
    kh,
    vh,
    ph,
    gmh,
    qt,
    kt,
    vt,
    gmt,
):
    reach = taps - 1
    columns = groups // LANES

    @pl.when(pl.program_id(0) == 0)
    def _():
        acc[...] = sums_in_ref[...]

    def column(lanes, index):
        part = pl.ds(pl.multiple_of(lax.rem(index, columns) * LANES, LANES), LANES)
        wq, wk, wv, wm = (weight_rows(weights_ref, bank, part) for bank in range(4))
        b_s[...] = before_ref[:, lanes].astype(F32)
        a_s[...] = after_ref[:, lanes].astype(F32)
        for bank, (ref, first) in enumerate(((qh, 0), (kh, reach), (vh, 3 * reach))):
            count = reach if bank == 0 else 2 * reach
            ref[PAD - count : PAD, :] = b_s[first : first + count, :]
            ref[PAD : 2 * PAD, :] = head_ref[bank, :, lanes].astype(F32)
        for bank, ref in enumerate((qt, kt, vt)):
            ref[0:PAD, :] = tail_ref[bank, :, lanes].astype(F32)
        qt[PAD : PAD + 2 * reach, :] = a_s[0 : 2 * reach, :]
        sums = Sums(taps)
        conv_k, conv_v = {}, {}
        for start in range(-TILE, PAD, TILE):
            conv_k[start] = dot_taps(wk, back(kh, start, taps))
            conv_v[start] = dot_taps(wv, back(vh, start, taps))
            ph[pl.ds(PAD + start, TILE), :] = conv_k[start] * conv_v[start]
        upstream = up_head_ref[:, lanes].astype(F32)
        parts = []
        for start in range(0, PAD, TILE):
            up = upstream[start : start + TILE]
            sources = back(qh, start, taps)
            products = back(ph, start, taps)
            qc = dot_taps(wq, sources)
            mixer = dot_taps(wm, products)
            gq = up * mixer
            gm = up * qc
            parts.append(qc * mixer)
            gmh[pl.ds(PAD + start, TILE), :] = gm
            ghead_ref[0, pl.ds(start, TILE), lanes] = gq
            sums.add(0, gq, sources)
            sums.add(3, gm, products)
        mixed_ref[:, lanes] = jnp.concatenate(parts, axis=0).astype(mixed_ref.dtype)
        gp = dot_taps(wm, ahead(gmh, 0, taps))
        gk = gp * conv_v[0]
        gv = gp * conv_k[0]
        ghead_ref[1, 0:TILE, lanes] = gk
        ghead_ref[2, 0:TILE, lanes] = gv
        sums.add(1, gk, back(kh, 0, taps))
        sums.add(2, gv, back(vh, 0, taps))
        qc = dot_taps(wq, back(qt, -TILE, taps))
        gmt[PAD - TILE : PAD, :] = up_tail_ref[:, lanes].astype(F32)[TILE:] * qc
        qc = dot_taps(wq, back(qt, 0, taps))
        gmt[PAD : PAD + TILE, :] = a_s[2 * reach : 2 * reach + TILE, :] * qc
        gp = dot_taps(wm, ahead(gmt, -TILE, taps))
        sources_k = back(kt, -TILE, taps)
        sources_v = back(vt, -TILE, taps)
        gk = gp * dot_taps(wv, sources_v)
        gv = gp * dot_taps(wk, sources_k)
        gtail_ref[0, :, lanes] = gk
        gtail_ref[1, :, lanes] = gv
        sums.add(1, gk, sources_k)
        sums.add(2, gv, sources_v)
        sums.store(acc, part)

    column_loop(mixed_ref, column)

    @pl.when(pl.program_id(0) == pl.num_programs(0) - 1)
    def _():
        sums_ref[...] = jnp.sum(acc[...], axis=2)


def edge(features, cotangent, weights, before, after, sums, mixed):
    banks, length, channels = features.shape
    taps, groups = weights.shape[1:]
    last = length // PAD - 1
    steps = 2 if channels % (2 * groups) == 0 else 1
    wide = channels // steps
    room = 2 * PAD + TILE
    work = TILE * channels * taps * 2
    return pl.pallas_call(
        functools.partial(edge_kernel, taps, length, groups),
        grid=(steps,),
        out_shape=(
            jax.ShapeDtypeStruct(mixed.shape, mixed.dtype),
            jax.ShapeDtypeStruct((banks, PAD, channels), F32),
            jax.ShapeDtypeStruct((banks - 1, TILE, channels), F32),
            jax.ShapeDtypeStruct((4, taps, groups), F32),
        ),
        in_specs=[
            pl.BlockSpec((banks, PAD, wide), lambda i: (0, last, i)),
            pl.BlockSpec((banks, PAD, wide), lambda i: (0, 0, i)),
            pl.BlockSpec((PAD, wide), lambda i: (last, i)),
            pl.BlockSpec((PAD, wide), lambda i: (0, i)),
            pl.BlockSpec(weights.shape, lambda i: (0, 0, 0)),
            pl.BlockSpec((before.shape[0], wide), lambda i: (0, i)),
            pl.BlockSpec((after.shape[0], wide), lambda i: (0, i)),
            pl.BlockSpec(sums.shape, lambda i: (0, 0, 0, 0)),
            pl.BlockSpec(memory_space=pl.ANY),
        ],
        out_specs=(
            pl.BlockSpec((PAD, wide), lambda i: (0, i)),
            pl.BlockSpec((banks, PAD, wide), lambda i: (0, 0, i)),
            pl.BlockSpec((banks - 1, TILE, wide), lambda i: (0, 0, i)),
            pl.BlockSpec((4, taps, groups), lambda i: (0, 0, 0)),
        ),
        scratch_shapes=[
            pltpu.VMEM(sums.shape, F32),
            pltpu.VMEM((before.shape[0], LANES), F32),
            pltpu.VMEM((after.shape[0], LANES), F32),
        ]
        + [pltpu.VMEM((room, LANES), F32) for _ in range(9)],
        input_output_aliases={8: 0},
        cost_estimate=pl.CostEstimate(
            flops=24 * work, bytes_accessed=2 * 10**6, transcendentals=0
        ),
        compiler_params=pltpu.CompilerParams(vmem_limit_bytes=16 * 1024 * 1024),
        name="edge",
    )(features, features, cotangent, cotangent, weights, before, after, sums, mixed)


def grads_kernel(
    taps,
    grads_ref,
    ghead_ref,
    gtail_ref,
    tail_ref,
    after_ref,
    weights_ref,
    *refs,
):
    out_ref, a_s, gq, gk, gv, q_s, k_s, v_s, p_s, gm_s = refs[-10:]
    reach = taps - 1
    length = grads_ref.shape[1]

    def column(lanes, _):
        wq, wk, wv, wm = (weight_rows(weights_ref, bank, lanes) for bank in range(4))
        a_s[...] = after_ref[:, lanes].astype(F32)
        for bank, ref in enumerate((q_s, k_s, v_s)):
            ref[0:PAD, :] = tail_ref[bank, :, lanes].astype(F32)
        q_s[PAD : PAD + 2 * reach, :] = a_s[0 : 2 * reach, :]
        k_s[PAD : PAD + reach, :] = a_s[4 * reach : 5 * reach, :]
        v_s[PAD : PAD + reach, :] = a_s[5 * reach : 6 * reach, :]
        for start in (-TILE, 0):
            kc = dot_taps(wk, back(k_s, start, taps))
            vc = dot_taps(wv, back(v_s, start, taps))
            p_s[pl.ds(PAD + start, TILE), :] = kc * vc
        first, second = (
            a_s[2 * reach : 2 * reach + TILE, :],
            a_s[2 * reach + TILE : 2 * reach + 2 * TILE, :],
        )
        gm_s[PAD : PAD + TILE, :] = first * dot_taps(wq, back(q_s, 0, taps))
        gm_s[PAD + TILE : 2 * PAD, :] = second * dot_taps(wq, back(q_s, TILE, taps))
        end = pl.ds(PAD + length, TILE)
        gq[end, :] = first * dot_taps(wm, back(p_s, 0, taps))
        gp = dot_taps(wm, ahead(gm_s, 0, taps))
        gk[end, :] = gp * vc
        gv[end, :] = gp * kc
        gq[PAD : 2 * PAD, :] = ghead_ref[0, :, lanes]
        gq[2 * PAD : PAD + length, :] = grads_ref[0, PAD:length, lanes]
        for bank, ref in ((1, gk), (2, gv)):
            ref[PAD : PAD + TILE, :] = ghead_ref[bank, 0:TILE, lanes]
            ref[PAD + TILE : PAD + length - TILE, :] = grads_ref[
                bank, TILE : length - TILE, lanes
            ]
            ref[PAD + length - TILE : PAD + length, :] = gtail_ref[bank - 1, :, lanes]
        for bank, (ref, weights) in enumerate(((gq, wq), (gk, wk), (gv, wv))):
            for start in range(0, length, PAD):
                out_ref[bank, pl.ds(start, PAD), lanes] = dot_taps(
                    weights, ahead(ref, start, taps, PAD)
                ).astype(out_ref.dtype)

    column_loop(grads_ref, column)


def feature_gradients(piece, pieces, features, grads, ghead, gtail, after, weights, earlier):
    banks, length, channels = features.shape
    taps, groups = weights.shape[1:]
    last = length // PAD - 1
    steps = channels // groups // pieces
    first = piece * steps
    room = length + 2 * PAD
    operands = [grads, ghead, gtail, features, after, weights]
    in_specs = [
        pl.BlockSpec((banks, length, groups), lambda i: (0, 0, first + i)),
        pl.BlockSpec((banks, PAD, groups), lambda i: (0, 0, first + i)),
        pl.BlockSpec((banks - 1, TILE, groups), lambda i: (0, 0, first + i)),
        pl.BlockSpec((banks, PAD, groups), lambda i: (0, last, first + i)),
        pl.BlockSpec((after.shape[0], groups), lambda i: (0, first + i)),
        pl.BlockSpec(weights.shape, lambda i: (0, 0, 0)),
    ]
    aliases = {}
    if earlier is not None:
        aliases = {len(operands): 0}
        operands.append(earlier)
        in_specs.append(pl.BlockSpec(memory_space=pl.ANY))
    work = length * channels * taps * 2 // pieces
    return pl.pallas_call(
        functools.partial(grads_kernel, taps),
        grid=(steps,),
        out_shape=jax.ShapeDtypeStruct(features.shape, features.dtype),
        in_specs=in_specs,
        out_specs=pl.BlockSpec((banks, length, groups), lambda i: (0, 0, first + i)),
        scratch_shapes=[pltpu.VMEM((after.shape[0], LANES), F32)]
        + [pltpu.VMEM((room, LANES), F32) for _ in range(3)]
        + [pltpu.VMEM((3 * PAD, LANES), F32) for _ in range(5)],
        input_output_aliases=aliases,
        cost_estimate=pl.CostEstimate(
            flops=4 * work,
            bytes_accessed=18 * length * channels // pieces,
            transcendentals=0,
        ),
        compiler_params=pltpu.CompilerParams(vmem_limit_bytes=16 * 1024 * 1024),
        name="feature_gradients",
    )(*operands)


def per_device(features, cotangent, master_filters):
    reach = master_filters.shape[1] - 1
    length = features.shape[1]
    tail, head = pack(features, cotangent, reach)
    before = shift_rows(tail, "ctx", 1)
    after = shift_rows(head, "ctx", -1)
    weights = gather_filters(master_filters.astype(jnp.bfloat16), "fsdp").astype(F32)
    mixed, grads, sums = interior(features, cotangent, weights)
    mixed, ghead, gtail, sums = edge(
        features, cotangent, weights, before, after, sums, mixed
    )
    repeats = features.shape[2] // weights.shape[2]
    pieces = PIECES if repeats % PIECES == 0 else 1
    feature_grads = None
    for piece in range(pieces):
        feature_grads = feature_gradients(
            piece, pieces, features, grads, ghead, gtail, after, weights, feature_grads
        )
    count_all = length * lax.axis_size("ctx") * repeats * lax.axis_size("fsdp")
    factor = 1.0 / math.sqrt(count_all)
    filter_grads = sum_over(sum_scatter(sums, "fsdp"), "ctx") * factor
    return (mixed, feature_grads, filter_grads)


def solution(mesh):
    return jax.shard_map(
        per_device,
        mesh=mesh,
        in_specs=(P(None, "ctx", "fsdp"), P("ctx", "fsdp"), P(None, None, "fsdp")),
        out_specs=(P("ctx", "fsdp"), P(None, "ctx", "fsdp"), P(None, None, "fsdp")),
        check_vma=False,
    )
```

time: 52.7 us -> 49.5 us (0.939)
  waiting for transfers between devices: 19 us -> 8.76 us
  Pallas kernels: 11.6 us -> 19.4 us
  starting transfers between devices: 13.7 us -> 15.9 us
  local copies, waits for them, and re-layouts: 5.92 us -> 4.19 us
  other arithmetic: 1.26 us -> 0.26 us
    pallas_call x1 -> x5, Pallas kernels: 11.6 us -> 19.4 us  [the longest x1 8.98 us: interior(): pl.pallas_call(functools.partial(interior_kernel, taps), grid=(repeats,),...]
    ppermute x2, waiting for transfers between devices: 8.86 us -> 1.13 us  [shift_rows(): return lax.ppermute(value, axis, pairs)]
    ppermute x4, waiting for transfers between devices: 8.99 us -> 6.43 us  [sum_over(): lax.ppermute(value, axis, [(i, i ^ hop) for i in range(size)])]
    squeeze x2 -> x0, local copies, waits for them, and re-layouts: 1.9 us -> none  [the longest x1 1.04 us: per_device(): features[0, :2 * reach]]
    ppermute x4, starting transfers between devices: 7.57 us -> 9.06 us  [sum_over(): lax.ppermute(value, axis, [(i, i ^ hop) for i in range(size)])]
    unnamed x6 -> x12, local copies, waits for them, and re-layouts: 3.12 us -> 4.19 us
    slice x1 -> x0, local copies, waits for them, and re-layouts: 0.9 us -> none  [per_device(): cotangent[:2 * reach]]
    select_n x1, other arithmetic: 0.76 us -> 0.01 us  [gather_filters(): jnp.where(first, shard, other)]
  transfers between devices with their start and end apart: 8 -> 8, of which waited for: 7 -> 5; matrix products, arithmetic and copies ran while one was open for 7% -> 0% of each run, Pallas kernels for 0% -> 32%
where the time goes in v2:
time: 49.5 us; the launch traced here: 49.2 us
  Pallas kernels  19.4 us (39%)
  starting transfers between devices  15.9 us (32%)
  waiting for transfers between devices  8.76 us (18%)
  local copies, waits for them, and re-layouts  4.19 us (8%)
  between operations  0.7 us (1%)
    ppermute x4, starting transfers between devices, sum_over(): lax.ppermute(value, axis, [(i, i ^ hop) for i in range(size)])  9.06 us
    pallas_call x1, Pallas kernels, interior(): pl.pallas_call(functools.partial(interior_kernel, taps), grid=(repeats,),...  8.98 us
    ppermute x4, waiting for transfers between devices, sum_over(): lax.ppermute(value, axis, [(i, i ^ hop) for i in range(size)])  6.43 us
    ppermute x2, starting transfers between devices, shift_rows(): return lax.ppermute(value, axis, pairs)  6.37 us
    pallas_call x2, Pallas kernels, feature_gradients(): pl.pallas_call(functools.partial(grads_kernel, taps), grid=(steps,), out_...  5.81 us
    unnamed x12, local copies, waits for them, and re-layouts  4.19 us
    pallas_call x1, Pallas kernels, edge(): pl.pallas_call(functools.partial(edge_kernel, taps, length, groups), grid...  3.48 us
    ppermute x1, waiting for transfers between devices, sum_scatter(): sent = lax.ppermute(jnp.where(first, high, low), axis, [(0, 1), (1, 0)])  1.19 us
  transfers between devices with their start and end apart: 8, of which 5 were waited for; matrix products, arithmetic and copies ran while one was open for 0% of the time, Pallas kernels for 32%

profile of v2, /device:TPU:0, one launch (start us, length us, event | category | flops | bytes accessed | tf_op | source)
XLA Modules:
  0.0 49.2 jit_solution(8675452374142626313)
XLA Ops:
  0.6 0.8 %copy.11 = bf16[4,7,192]{2,1,0:T(8,128)(2,1)S(1)} copy(f32[4,7,192]{2,0,1:T(4,128)} %param.5) | data formatting | bytes 32256 | tf_op args[2]
  1.4 0.5 collective-permute-start
  1.8 0.0 copy-start
  1.8 1.7 %copy-done = bf16[3,128,3072]{2,1,0:T(8,128)(2,1)S(1)} copy-done((bf16[3,128,3072]{2,1,0:T(8,128)(2,1)S(1)}, bf16[3,128,3072]{2,1,0:T(8,128)(2,1)}, u32[]{:S(2)}) %copy-start) | copy-done | bytes 2359320
  3.5 0.0 copy-start.2
  3.5 1.1 %copy-done.2 = bf16[128,3072]{1,0:T(8,128)(2,1)S(1)} copy-done((bf16[128,3072]{1,0:T(8,128)(2,1)S(1)}, bf16[128,3072]{1,0:T(8,128)(2,1)}, u32[]{:S(2)}) %copy-start.2) | copy-done | bytes 786456
  4.6 0.0 copy-start.4
  4.6 0.0 copy-start.1
  4.6 0.0 copy-start.3
  4.6 1.2 %pack_halos.1 = (bf16[30,3072]{1,0:T(8,128)(2,1)}, bf16[36,3072]{1,0:T(8,128)(2,1)}) custom-call(bf16[3,128,3072]{2,1,0:T(8,128)(2,1)S(1)} %copy-done, bf16[3,128,3072]{2,1,0:T(8,128)(2,1)S(1)} %copy-done, bf16[128,3072]{1,0:T(8,128)(2,1)S(1)} %copy-done.2), custom_call_target="tpu_custom_call" | custom-call | flops 1000000 | bytes 1000000 | tf_op jit(solution)/shard_map/pack_halos/pallas_call | solution.py:126
  5.8 5.1 %collective-permute-start.1 = (bf16[30,3072]{1,0:T(8,128)(2,1)}, bf16[30,3072]{1,0:T(8,128)(2,1)}, u32[]{:S(2)}, u32[]{:S(2)}) collective-permute-start(bf16[30,3072]{1,0:T(8,128)(2,1)} %get-tuple-element.12), channel_id=1, source_target_pairs={{0,2},{2,4},{4,6},{6,8},{8,10},{10,12},{12,14},{14,16},{16,18},{18... | collective-permute-start | bytes 552968 | tf_op jit(solution)/shard_map/ppermute | solution.py:21
  10.9 1.3 %collective-permute-start.2 = (bf16[36,3072]{1,0:T(8,128)(2,1)}, bf16[36,3072]{1,0:T(8,128)(2,1)S(1)}, u32[]{:S(2)}, u32[]{:S(2)}) collective-permute-start(bf16[36,3072]{1,0:T(8,128)(2,1)} %get-tuple-element.13), channel_id=1, source_target_pairs={{2,0},{4,2},{6,4},{8,6},{10,8},{12,10},{14,12},{16,14},{18,16},{20... | collective-permute-start | bytes 663560 | tf_op jit(solution)/shard_map/ppermute | solution.py:21
  12.2 0.0 collective-permute-done
  12.2 0.0 copy-done.4
  12.2 0.1 maximum_convert_fusion.weights_ref
  12.3 0.0 copy-done.1
  12.3 0.0 copy-done.3
  12.3 9.0 %interior.1 = (bf16[128,3072]{1,0:T(8,128)(2,1)}, f32[3,128,3072]{2,1,0:T(8,128)S(1)}, f32[4,7,8,384]{3,2,1,0:T(8,128)S(1)}) custom-call(bf16[3,128,3072]{2,1,0:T(8,128)(2,1)S(1)} %copy-done.1, bf16[128,3072]{1,0:T(8,128)(2,1)S(1)} %copy-done.3, f32[4,7,384]{2,1,0:T(8,128)S(1)} %maximum_convert_fusion.weights_ref), custom_call_target="tpu_custom_call" | custom-call | flops 49545216 | bytes 10223616 | tf_op jit(solution)/shard_map/interior/pallas_call | solution.py:229
  21.3 0.0 collective-permute-done.1.before_ref
  21.3 1.1 %collective-permute-done.2.after_ref = bf16[36,3072]{1,0:T(8,128)(2,1)S(1)} collective-permute-done((bf16[36,3072]{1,0:T(8,128)(2,1)}, bf16[36,3072]{1,0:T(8,128)(2,1)S(1)}, u32[]{:S(2)}, u32[]{:S(2)}) %collective-permute-start.2) | collective-permute-done | bytes 221216 | tf_op jit(solution)/shard_map/ppermute | solution.py:21
  22.4 3.5 %edge.1 = (bf16[128,3072]{1,0:T(8,128)(2,1)}, f32[3,16,3072]{2,1,0:T(8,128)S(1)}, f32[2,8,3072]{2,1,0:T(8,128)S(1)}, f32[4,7,384]{2,1,0:T(8,128)S(1)}) custom-call(bf16[3,128,3072]{2,1,0:T(8,128)(2,1)S(1)} %copy-done.1, bf16[3,128,3072]{2,1,0:T(8,128)(2,1)S(1)} %copy-done.1, bf16[128,3072]{1,0:T(8,128)(2,1)S(1)} %copy-done.3, ...), custom_call_target="tpu_custom_call", output_to_operand_aliasing={{0}: (8, {})} | custom-call | flops 8257536 | bytes 2000000 | tf_op jit(solution)/shard_map/edge/pallas_call | solution.py:364
  25.9 0.1 slice_select_fusion
  26.0 0.0 collective-permute-start.3
  26.0 1.2 %collective-permute-done.3 = f32[4,7,192]{2,1,0:T(8,128)S(1)} collective-permute-done((f32[4,7,192]{2,1,0:T(8,128)S(1)}, f32[4,7,192]{2,1,0:T(8,128)S(1)}, u32[]{:S(2)}, u32[]{:S(2)}) %collective-permute-start.3) | collective-permute-done | bytes 21536 | tf_op jit(solution)/shard_map/ppermute | solution.py:56
  27.2 0.1 select_add_fusion
  27.3 1.5 %collective-permute-start.4 = (f32[4,7,192]{2,1,0:T(8,128)S(1)}, f32[4,7,192]{2,1,0:T(8,128)S(1)}, u32[]{:S(2)}, u32[]{:S(2)}) collective-permute-start(f32[4,7,192]{2,1,0:T(8,128)S(1)} %select_add_fusion), channel_id=1, source_target_pairs={{0,2},{2,0},{4,6},{6,4},{8,10},{10,8},{12,14},{14,12},{16,18},{18,... | collective-permute-start | bytes 64520 | tf_op jit(solution)/shard_map/ppermute | solution.py:41
  28.8 2.4 %collective-permute-done.4 = f32[4,7,192]{2,1,0:T(8,128)S(1)} collective-permute-done((f32[4,7,192]{2,1,0:T(8,128)S(1)}, f32[4,7,192]{2,1,0:T(8,128)S(1)}, u32[]{:S(2)}, u32[]{:S(2)}) %collective-permute-start.4) | collective-permute-done | bytes 21536 | tf_op jit(solution)/shard_map/ppermute | solution.py:41
  31.2 1.8 %collective-permute-start.5 = (f32[4,7,192]{2,1,0:T(8,128)S(1)}, f32[4,7,192]{2,1,0:T(8,128)S(1)}, u32[]{:S(2)}, u32[]{:S(2)}) collective-permute-start(f32[4,7,192]{2,1,0:T(8,128)S(1)} %add.16), channel_id=1, source_target_pairs={{0,4},{2,6},{4,0},{6,2},{8,12},{10,14},{12,8},{14,10},{16,20},{18,... | collective-permute-start | bytes 64520 | tf_op jit(solution)/shard_map/ppermute | solution.py:41
  33.0 2.1 %collective-permute-done.5 = f32[4,7,192]{2,1,0:T(8,128)S(1)} collective-permute-done((f32[4,7,192]{2,1,0:T(8,128)S(1)}, f32[4,7,192]{2,1,0:T(8,128)S(1)}, u32[]{:S(2)}, u32[]{:S(2)}) %collective-permute-start.5) | collective-permute-done | bytes 21536 | tf_op jit(solution)/shard_map/ppermute | solution.py:41
  35.1 2.7 %collective-permute-start.6 = (f32[4,7,192]{2,1,0:T(8,128)S(1)}, f32[4,7,192]{2,1,0:T(8,128)S(1)}, u32[]{:S(2)}, u32[]{:S(2)}) collective-permute-start(f32[4,7,192]{2,1,0:T(8,128)S(1)} %add.17), channel_id=1, source_target_pairs={{0,8},{2,10},{4,12},{6,14},{8,0},{10,2},{12,4},{14,6},{16,24},{18,... | collective-permute-start | bytes 64520 | tf_op jit(solution)/shard_map/ppermute | solution.py:41
  37.9 1.9 %collective-permute-done.6 = f32[4,7,192]{2,1,0:T(8,128)S(1)} collective-permute-done((f32[4,7,192]{2,1,0:T(8,128)S(1)}, f32[4,7,192]{2,1,0:T(8,128)S(1)}, u32[]{:S(2)}, u32[]{:S(2)}) %collective-permute-start.6) | collective-permute-done | bytes 21536 | tf_op jit(solution)/shard_map/ppermute | solution.py:41
  39.7 3.0 %collective-permute-start.7 = (f32[4,7,192]{2,1,0:T(8,128)S(1)}, f32[4,7,192]{2,1,0:T(8,128)S(1)}, u32[]{:S(2)}, u32[]{:S(2)}) collective-permute-start(f32[4,7,192]{2,1,0:T(8,128)S(1)} %add.18), channel_id=1, source_target_pairs={{0,16},{2,18},{4,20},{6,22},{8,24},{10,26},{12,28},{14,30},{16,0},... | collective-permute-start | bytes 64520 | tf_op jit(solution)/shard_map/ppermute | solution.py:41
  42.8 2.9 %feature_gradients.2.refs_0_ = bf16[3,128,3072]{2,1,0:T(8,128)(2,1)} custom-call(f32[3,128,3072]{2,1,0:T(8,128)S(1)} %get-tuple-element.17.grads_ref, f32[3,16,3072]{2,1,0:T(8,128)S(1)} %get-tuple-element.18.ghead_ref, f32[2,8,3072]{2,1,0:T(8,128)S(1)} %get-tuple-element.19.gtail_ref, bf16[3,128,3072]{2,1,0:T(8,128)(2,1)S(1)} %copy-done.1, ...), custom_call_target="tpu_custom_call" | custom-call | flops 11010048 | bytes 3538944 | tf_op jit(solution)/shard_map/feature_gradients/pallas_call | solution.py:481
  45.7 2.9 %feature_gradients.3 = bf16[3,128,3072]{2,1,0:T(8,128)(2,1)} custom-call(f32[3,128,3072]{2,1,0:T(8,128)S(1)} %get-tuple-element.17.grads_ref, f32[3,16,3072]{2,1,0:T(8,128)S(1)} %get-tuple-element.18.ghead_ref, f32[2,8,3072]{2,1,0:T(8,128)S(1)} %get-tuple-element.19.gtail_ref, bf16[3,128,3072]{2,1,0:T(8,128)(2,1)S(1)} %copy-done.1, ...), custom_call_target="tpu_custom_call", output_to_operand_aliasing={{}: (6, {})} | custom-call | flops 11010048 | bytes 3538944 | tf_op jit(solution)/shard_map/feature_gradients/pallas_call | solution.py:481
  48.6 0.0 collective-permute-done.7
  48.6 0.6 %copy.9 = f32[4,7,192]{2,0,1:T(4,128)} copy(f32[4,7,192]{2,1,0:T(8,128)S(1)} %add_multiply_fusion) | data formatting | bytes 43008
  (5 shorter events, 0.0 us)
Async XLA Ops:
  1.4 10.8 %collective-permute-start = (bf16[4,7,192]{2,1,0:T(8,128)(2,1)S(1)}, bf16[4,7,192]{2,1,0:T(8,128)(2,1)S(1)}, u32[]{:S(2)}, u32[]{:S(2)}) collective-permute-start(bf16[4,7,192]{2,1,0:T(8,128)(2,1)S(1)} %copy.11), channel_id=1, source_target_pairs={{0,1},{1,0},{2,3},{3,2},{4,5},{5,4},{6,7},{7,6},{8,9},{9,8},{10,11... | collective-permute-start | bytes 32264 | tf_op jit(solution)/shard_map/ppermute | solution.py:28
  1.8 1.7 %copy-start = (bf16[3,128,3072]{2,1,0:T(8,128)(2,1)S(1)}, bf16[3,128,3072]{2,1,0:T(8,128)(2,1)}, u32[]{:S(2)}) copy-start(bf16[3,128,3072]{2,1,0:T(8,128)(2,1)} %tail_ref.7) | copy-start | bytes 7077892
  3.5 1.1 %copy-start.2 = (bf16[128,3072]{1,0:T(8,128)(2,1)S(1)}, bf16[128,3072]{1,0:T(8,128)(2,1)}, u32[]{:S(2)}) copy-start(bf16[128,3072]{1,0:T(8,128)(2,1)} %up_head_ref.1) | copy-start | bytes 2359300
  4.6 7.6 %copy-start.4 = (f32[4,7,192]{2,0,1:T(4,128)S(1)}, f32[4,7,192]{2,0,1:T(4,128)}, u32[]{:S(2)}) copy-start(f32[4,7,192]{2,0,1:T(4,128)} %param.5) | copy-start | bytes 64516
  4.6 7.7 %copy-start.1 = (bf16[3,128,3072]{2,1,0:T(8,128)(2,1)S(1)}, bf16[3,128,3072]{2,1,0:T(8,128)(2,1)}, u32[]{:S(2)}) copy-start(bf16[3,128,3072]{2,1,0:T(8,128)(2,1)} %tail_ref.7) | copy-start | bytes 7077892
  4.6 7.7 %copy-start.3 = (bf16[128,3072]{1,0:T(8,128)(2,1)S(1)}, bf16[128,3072]{1,0:T(8,128)(2,1)}, u32[]{:S(2)}) copy-start(bf16[128,3072]{1,0:T(8,128)(2,1)} %up_head_ref.1) | copy-start | bytes 2359300
  5.8 15.5 %collective-permute-start.1 = (bf16[30,3072]{1,0:T(8,128)(2,1)}, bf16[30,3072]{1,0:T(8,128)(2,1)}, u32[]{:S(2)}, u32[]{:S(2)}) collective-permute-start(bf16[30,3072]{1,0:T(8,128)(2,1)} %get-tuple-element.12), channel_id=1, source_target_pairs={{0,2},{2,4},{4,6},{6,8},{8,10},{10,12},{12,14},{14,16},{16,18},{18... | collective-permute-start | bytes 552968 | tf_op jit(solution)/shard_map/ppermute | solution.py:21
  10.9 11.5 %collective-permute-start.2 = (bf16[36,3072]{1,0:T(8,128)(2,1)}, bf16[36,3072]{1,0:T(8,128)(2,1)S(1)}, u32[]{:S(2)}, u32[]{:S(2)}) collective-permute-start(bf16[36,3072]{1,0:T(8,128)(2,1)} %get-tuple-element.13), channel_id=1, source_target_pairs={{2,0},{4,2},{6,4},{8,6},{10,8},{12,10},{14,12},{16,14},{18,16},{20... | collective-permute-start | bytes 663560 | tf_op jit(solution)/shard_map/ppermute | solution.py:21
  26.0 1.2 %collective-permute-start.3 = (f32[4,7,192]{2,1,0:T(8,128)S(1)}, f32[4,7,192]{2,1,0:T(8,128)S(1)}, u32[]{:S(2)}, u32[]{:S(2)}) collective-permute-start(f32[4,7,192]{2,1,0:T(8,128)S(1)} %slice_select_fusion), channel_id=1, source_target_pairs={{0,1},{1,0},{2,3},{3,2},{4,5},{5,4},{6,7},{7,6},{8,9},{9,8},{10,11... | collective-permute-start | bytes 64520 | tf_op jit(solution)/shard_map/ppermute | solution.py:56
  27.3 3.9 %collective-permute-start.4 = (f32[4,7,192]{2,1,0:T(8,128)S(1)}, f32[4,7,192]{2,1,0:T(8,128)S(1)}, u32[]{:S(2)}, u32[]{:S(2)}) collective-permute-start(f32[4,7,192]{2,1,0:T(8,128)S(1)} %select_add_fusion), channel_id=1, source_target_pairs={{0,2},{2,0},{4,6},{6,4},{8,10},{10,8},{12,14},{14,12},{16,18},{18,... | collective-permute-start | bytes 64520 | tf_op jit(solution)/shard_map/ppermute | solution.py:41
  31.2 3.9 %collective-permute-start.5 = (f32[4,7,192]{2,1,0:T(8,128)S(1)}, f32[4,7,192]{2,1,0:T(8,128)S(1)}, u32[]{:S(2)}, u32[]{:S(2)}) collective-permute-start(f32[4,7,192]{2,1,0:T(8,128)S(1)} %add.16), channel_id=1, source_target_pairs={{0,4},{2,6},{4,0},{6,2},{8,12},{10,14},{12,8},{14,10},{16,20},{18,... | collective-permute-start | bytes 64520 | tf_op jit(solution)/shard_map/ppermute | solution.py:41
  35.1 4.6 %collective-permute-start.6 = (f32[4,7,192]{2,1,0:T(8,128)S(1)}, f32[4,7,192]{2,1,0:T(8,128)S(1)}, u32[]{:S(2)}, u32[]{:S(2)}) collective-permute-start(f32[4,7,192]{2,1,0:T(8,128)S(1)} %add.17), channel_id=1, source_target_pairs={{0,8},{2,10},{4,12},{6,14},{8,0},{10,2},{12,4},{14,6},{16,24},{18,... | collective-permute-start | bytes 64520 | tf_op jit(solution)/shard_map/ppermute | solution.py:41
  39.7 8.8 %collective-permute-start.7 = (f32[4,7,192]{2,1,0:T(8,128)S(1)}, f32[4,7,192]{2,1,0:T(8,128)S(1)}, u32[]{:S(2)}, u32[]{:S(2)}) collective-permute-start(f32[4,7,192]{2,1,0:T(8,128)S(1)} %add.18), channel_id=1, source_target_pairs={{0,16},{2,18},{4,20},{6,22},{8,24},{10,26},{12,28},{14,30},{16,0},... | collective-permute-start | bytes 64520 | tf_op jit(solution)/shard_map/ppermute | solution.py:41

commit v3 on v0

v3 whole, which is shorter than its diff:
```python
import functools
import math

import jax
import jax.numpy as jnp
from jax import lax
from jax.experimental import pallas as pl
from jax.experimental.pallas import tpu as pltpu
from jax.sharding import PartitionSpec as P

LANES = 128
CHUNK = 16
PAD = 16
PIECES = 4
VMEM_LIMIT = 12 * 1024 * 1024
F32 = jnp.float32
VMEM_SPEC = pl.BlockSpec(memory_space=pltpu.VMEM)
ANY_SPEC = pl.BlockSpec(memory_space=pl.ANY)


def shift_rows(value, axis, by):
    size = lax.axis_size(axis)
    pairs = [(i, i + by) for i in range(size) if 0 <= i + by < size]
    return lax.ppermute(value, axis, pairs)


def gather_filters(shard, axis):
    size = lax.axis_size(axis)
    if size != 2:
        return lax.all_gather(shard, axis, axis=2, tiled=True)
    other = lax.ppermute(shard, axis, [(0, 1), (1, 0)])
    first = lax.axis_index(axis) == 0
    return jnp.concatenate(
        [jnp.where(first, shard, other), jnp.where(first, other, shard)], axis=2
    )


def sum_over(value, axis, beside=None):
    size = lax.axis_size(axis)
    if size & (size - 1):
        return lax.psum(value, axis), 0
    rounds = size.bit_length() - 1
    for step in range(rounds):
        pairs = [(i, i ^ (1 << step)) for i in range(size)]
        received = lax.ppermute(value, axis, pairs)
        value = value + received
        if beside is not None:
            value = value + beside(step)
    return value, rounds


def sum_scatter(value, axis):
    size = lax.axis_size(axis)
    portion = value.shape[-1] // size
    if size != 2:
        total, _ = sum_over(value, axis)
        return lax.dynamic_slice_in_dim(
            total, lax.axis_index(axis) * portion, portion, value.ndim - 1
        )
    first = lax.axis_index(axis) == 0
    low, high = value[..., :portion], value[..., portion:]
    sent = lax.ppermute(jnp.where(first, high, low), axis, [(0, 1), (1, 0)])
    return jnp.where(first, low, high) + sent


def dot_taps(weights, pieces):
    total = weights[0] * pieces[0]
    for weight, piece in zip(weights[1:], pieces[1:]):
        total = total + weight * piece
    return total


def weight_rows(ref, bank, lanes):
    return [ref[lag, pl.ds(bank, 1), lanes] for lag in range(ref.shape[0])]


def lane_slice(index):
    return pl.ds(pl.multiple_of(index * LANES, LANES), LANES)


def part_slice(repeat, groups, column):
    return pl.ds(pl.multiple_of(repeat * groups + column * LANES, LANES), LANES)


class Tokens:
    def __init__(self, ref, repeats, origin=0, lead=()):
        self.ref, self.repeats, self.origin, self.lead = ref, repeats, origin, lead

    def rows(self, token, count=1):
        start = (self.origin + token) * self.repeats
        if not isinstance(start, int):
            start = pl.multiple_of(start, self.repeats)
        return pl.ds(start, count * self.repeats)

    def __getitem__(self, token):
        return self.ref[(*self.lead, self.rows(token), slice(None))]

    def __setitem__(self, token, value):
        self.ref[(*self.lead, self.rows(token), slice(None))] = value

    def strided(self, token, repeat, count):
        start = (self.origin + token) * self.repeats + repeat
        return pl.ds(start, count, stride=self.repeats)

    def put(self, token, repeat, value):
        rows = self.strided(token, repeat, value.shape[0])
        self.ref[(*self.lead, rows, slice(None))] = value

    def take(self, token, repeat, count):
        return self.ref[(*self.lead, self.strided(token, repeat, count), slice(None))]


class Window:
    def __init__(self, load):
        self.load, self.held = load, {}

    def __call__(self, token):
        if token not in self.held:
            self.held[token] = self.load(token)
        return self.held[token]

    def back(self, token, taps):
        return [self(token - lag) for lag in range(taps)]

    def ahead(self, token, taps):
        return [self(token + lag) for lag in range(taps)]


class Sums:
    def __init__(self, taps):
        self.taps = taps
        self.held = {}

    def add(self, bank, grad, pieces):
        for lag, piece in enumerate(pieces):
            term = grad * piece
            old = self.held.get((bank, lag))
            self.held[bank, lag] = term if old is None else old + term

    def store(self, ref, lanes):
        for (bank, lag), value in self.held.items():
            ref[bank, lag, :, lanes] += value


def pack_kernel(
    reach,
    features_hbm,
    cotangent_hbm,
    master_ref,
    before_ref,
    after_ref,
    rounded_ref,
    tail,
    head,
    upstream,
    b_s,
    a_s,
    sems,
):
    length = cotangent_hbm.shape[0]
    copies = [
        pltpu.make_async_copy(features_hbm.at[:, length - PAD :, :], tail, sems.at[0]),
        pltpu.make_async_copy(features_hbm.at[:, :PAD, :], head, sems.at[1]),
        pltpu.make_async_copy(cotangent_hbm.at[:PAD, :], upstream, sems.at[2]),
    ]
    for copy in copies:
        copy.start()
    rounded_ref[...] = master_ref[...].astype(rounded_ref.dtype)
    for copy in copies:
        copy.wait()

    def column(index, carry):
        lanes = lane_slice(index)

        def rows(ref, bank, start, stop):
            return ref[bank, :, lanes].astype(F32)[start:stop]

        b_s[0:reach, :] = rows(tail, 0, PAD - reach, PAD)
        b_s[reach : 3 * reach, :] = rows(tail, 1, PAD - 2 * reach, PAD)
        b_s[3 * reach : 5 * reach, :] = rows(tail, 2, PAD - 2 * reach, PAD)
        before_ref[:, lanes] = b_s[...].astype(before_ref.dtype)
        a_s[0 : 2 * reach, :] = rows(head, 0, 0, 2 * reach)
        a_s[2 * reach : 4 * reach, :] = upstream[:, lanes].astype(F32)[: 2 * reach]
        a_s[4 * reach : 5 * reach, :] = rows(head, 1, 0, reach)
        a_s[5 * reach : 6 * reach, :] = rows(head, 2, 0, reach)
        after_ref[:, lanes] = a_s[...].astype(after_ref.dtype)
        return carry

    lax.fori_loop(0, before_ref.shape[1] // LANES, column, 0)


def pack(features, cotangent, master):
    reach = master.shape[0] - 1
    banks, length, channels = features.shape
    kind = features.dtype
    return pl.pallas_call(
        functools.partial(pack_kernel, reach),
        out_shape=(
            jax.ShapeDtypeStruct((5 * reach, channels), kind),
            jax.ShapeDtypeStruct((6 * reach, channels), kind),
            jax.ShapeDtypeStruct(master.shape, jnp.bfloat16),
        ),
        in_specs=[
            pl.BlockSpec(memory_space=pltpu.HBM),
            pl.BlockSpec(memory_space=pltpu.HBM),
            VMEM_SPEC,
        ],
        out_specs=(VMEM_SPEC,) * 3,
        scratch_shapes=[
            pltpu.VMEM((banks, PAD, channels), kind),
            pltpu.VMEM((banks, PAD, channels), kind),
            pltpu.VMEM((PAD, channels), kind),
            pltpu.VMEM((5 * reach, LANES), F32),
            pltpu.VMEM((6 * reach, LANES), F32),
            pltpu.SemaphoreType.DMA((3,)),
        ],
        cost_estimate=pl.CostEstimate(flops=10**6, bytes_accessed=10**6, transcendentals=0),
        compiler_params=pltpu.CompilerParams(vmem_limit_bytes=8 * 1024 * 1024),
        name="pack_halos",
    )(
        pltpu.with_memory_space_constraint(features, pltpu.HBM),
        pltpu.with_memory_space_constraint(cotangent, pltpu.HBM),
        master,
    )


def interior_kernel(
    taps,
    repeats,
    features_ref,
    cotangent_ref,
    weights_ref,
    mixed_ref,
    gq_ref,
    gk_ref,
    gv_ref,
    q_s,
    k_s,
    v_s,
    c_s,
    kc_s,
    vc_s,
    p_s,
    gm_s,
    sums_ref,
    m_s,
):
    reach = taps - 1
    groups = weights_ref.shape[2]
    length = cotangent_ref.shape[0]
    count = length // CHUNK
    sums_ref[...] = jnp.zeros_like(sums_ref)
    m_t = Tokens(m_s, repeats)

    def column_step(column, carry):
        lanes = lane_slice(column)
        gq_t, gk_t, gv_t = (
            Tokens(ref, repeats, 0, (column,)) for ref in (gq_ref, gk_ref, gv_ref)
        )
        q_t, k_t, v_t, c_t, kc_t, vc_t, p_t, gm_t = (
            Tokens(ref, repeats, PAD, (column,))
            for ref in (q_s, k_s, v_s, c_s, kc_s, vc_s, p_s, gm_s)
        )
        zero = jnp.zeros((reach * repeats, LANES), F32)
        for ref in (q_s, k_s, v_s, p_s):
            ref[column, (PAD - reach) * repeats : PAD * repeats, :] = zero
        gm_s[column, gm_t.rows(length, reach), :] = zero
        wq, wk, wv, wm = (weight_rows(weights_ref, bank, lanes) for bank in range(4))

        def forward(step, carry):
            base = pl.multiple_of(step * CHUNK, CHUNK)
            rows = pl.ds(base, CHUNK)
            for repeat in range(repeats):
                part = part_slice(repeat, groups, column)
                for bank, view in enumerate((q_t, k_t, v_t)):
                    view.put(base, repeat, features_ref[bank, rows, part].astype(F32))
                c_t.put(base, repeat, cotangent_ref[rows, part].astype(F32))
            k_w, v_w = (Window(lambda t, view=view: view[base + t]) for view in (k_t, v_t))
            for token in range(CHUNK):
                kc = dot_taps(wk, k_w.back(token, taps))
                vc = dot_taps(wv, v_w.back(token, taps))
                kc_t[base + token] = kc
                vc_t[base + token] = vc
                p_t[base + token] = kc * vc
            sums = Sums(taps)
            q_w, p_w = (Window(lambda t, view=view: view[base + t]) for view in (q_t, p_t))
            for token in range(CHUNK):
                up = c_t[base + token]
                sources = q_w.back(token, taps)
                products = p_w.back(token, taps)
                qc = dot_taps(wq, sources)
                mixer = dot_taps(wm, products)
                gq = up * mixer
                gm = up * qc
                m_t[token] = qc * mixer
                gm_t[base + token] = gm
                gq_t[base + token] = gq
                if token < 2 * reach:
                    gq = jnp.where(step > 0, gq, 0.0)
                    gm = jnp.where(step > 0, gm, 0.0)
                sums.add(0, gq, sources)
                sums.add(3, gm, products)
            sums.store(sums_ref, lanes)
            for repeat in range(repeats):
                part = part_slice(repeat, groups, column)
                mixed_ref[rows, part] = m_t.take(0, repeat, CHUNK).astype(mixed_ref.dtype)
            return carry

        def backward(step, carry):
            base = pl.multiple_of(step * CHUNK, CHUNK)
            k_w, v_w, gm_w = (
                Window(lambda t, view=view: view[base + t]) for view in (k_t, v_t, gm_t)
            )
            sums = Sums(taps)
            for token in range(CHUNK):
                gp = dot_taps(wm, gm_w.ahead(token, taps))
                if token < reach:
                    gp = jnp.where(step > 0, gp, 0.0)
                if token >= CHUNK - reach:
                    gp = jnp.where(step < count - 1, gp, 0.0)
                gk = gp * vc_t[base + token]
                gv = gp * kc_t[base + token]
                gk_t[base + token] = gk
                gv_t[base + token] = gv
                sums.add(1, gk, k_w.back(token, taps))
                sums.add(2, gv, v_w.back(token, taps))
            sums.store(sums_ref, lanes)
            return carry

        lax.fori_loop(0, count, forward, 0)
        lax.fori_loop(0, count, backward, 0)
        return carry

    lax.fori_loop(0, groups // LANES, column_step, 0)


def interior(features, cotangent, weights):
    length, channels = cotangent.shape
    taps, banks, groups = weights.shape
    repeats = channels // groups
    columns = groups // LANES
    work = length * channels * taps * 2
    grad = jax.ShapeDtypeStruct((columns, length * repeats, LANES), F32)
    held = jax.ShapeDtypeStruct((columns, (length + 2 * PAD) * repeats, LANES), F32)
    mixed, gq, gk, gv, *arrays, sums = pl.pallas_call(
        functools.partial(interior_kernel, taps, repeats),
        out_shape=(
            jax.ShapeDtypeStruct(cotangent.shape, cotangent.dtype),
            *[grad] * 3,
            *[held] * 8,
            jax.ShapeDtypeStruct((banks, taps, repeats, groups), F32),
        ),
        in_specs=[VMEM_SPEC] * 3,
        out_specs=(VMEM_SPEC,) * 13,
        scratch_shapes=[pltpu.VMEM((CHUNK * repeats, LANES), F32)],
        cost_estimate=pl.CostEstimate(
            flops=9 * work, bytes_accessed=22 * length * channels, transcendentals=0
        ),
        compiler_params=pltpu.CompilerParams(vmem_limit_bytes=VMEM_LIMIT),
        name="interior",
    )(features, cotangent, weights)
    return mixed, (gq, gk, gv), arrays, sums


def stage_halo(halo_ref, n_s, view, repeats, groups, column, rows):
    for repeat in range(repeats):
        n_s[0:rows, :] = halo_ref[0:rows, part_slice(repeat, groups, column)].astype(F32)
        view.put(0, repeat, n_s[...])


def edge_kernel(
    taps,
    repeats,
    weights_ref,
    before_ref,
    after_ref,
    sums_in_ref,
    q_a,
    k_a,
    v_a,
    c_a,
    kc_a,
    vc_a,
    p_a,
    gm_a,
    mixed_ref,
    ghead_ref,
    gtail_ref,
    sums_ref,
    acc,
    n_s,
    h_s,
    kc_s,
    vc_s,
    p_s,
    gm_s,
    m_s,
):
    reach = taps - 1
    groups = weights_ref.shape[2]
    length = q_a.shape[1] // repeats - 2 * PAD
    acc[...] = sums_in_ref[...]
    h_t, m_t = Tokens(h_s, repeats), Tokens(m_s, repeats)
    kc_t, vc_t, p_t, gm_t = (Tokens(ref, repeats, PAD) for ref in (kc_s, vc_s, p_s, gm_s))

    def column_step(column, carry):
        lanes = lane_slice(column)
        wq, wk, wv, wm = (weight_rows(weights_ref, bank, lanes) for bank in range(4))
        q_t, k_t, v_t, c_t, kc_i, vc_i, p_i, gm_i = (
            Tokens(ref, repeats, PAD, (column,))
            for ref in (q_a, k_a, v_a, c_a, kc_a, vc_a, p_a, gm_a)
        )
        sums = Sums(taps)

        stage_halo(before_ref, n_s, h_t, repeats, groups, column, 5 * reach)
        q_w = Window(lambda t: q_t[t] if t >= 0 else h_t[reach + t])
        k_w = Window(lambda t: k_t[t] if t >= 0 else h_t[3 * reach + t])
        v_w = Window(lambda t: v_t[t] if t >= 0 else h_t[5 * reach + t])
        gq_o, gk_o, gv_o = (Tokens(ghead_ref, repeats, 0, (bank, column)) for bank in range(3))
        for token in range(-reach, reach):
            kc = dot_taps(wk, k_w.back(token, taps))
            vc = dot_taps(wv, v_w.back(token, taps))
            p_t[token] = kc * vc
            if token >= 0:
                kc_t[token] = kc
                vc_t[token] = vc
        p_w = Window(lambda t: p_t[t] if t < reach else p_i[t])
        for token in range(CHUNK):
            up = c_t[token]
            sources = q_w.back(token, taps)
            products = p_w.back(token, taps)
            qc = dot_taps(wq, sources)
            mixer = dot_taps(wm, products)
            m_t[token] = qc * mixer
            if token < 2 * reach:
                gq = up * mixer
                gm = up * qc
                gm_t[token] = gm
                gq_o[token] = gq
                sums.add(0, gq, sources)
                sums.add(3, gm, products)
        gm_w = Window(lambda t: gm_t[t])
        for token in range(reach):
            gp = dot_taps(wm, gm_w.ahead(token, taps))
            gk = gp * vc_t[token]
            gv = gp * kc_t[token]
            gk_o[token] = gk
            gv_o[token] = gv
            sums.add(1, gk, k_w.back(token, taps))
            sums.add(2, gv, v_w.back(token, taps))
        for repeat in range(repeats):
            part = part_slice(repeat, groups, column)
            mixed_ref[:, part] = m_t.take(0, repeat, CHUNK).astype(mixed_ref.dtype)

        stage_halo(after_ref, n_s, h_t, repeats, groups, column, 4 * reach)
        q_w = Window(lambda t: q_t[length + t] if t < 0 else h_t[t])
        gk_o, gv_o = (Tokens(gtail_ref, repeats, reach, (bank, column)) for bank in range(2))
        for token in range(reach):
            gm_t[token] = h_t[2 * reach + token] * dot_taps(wq, q_w.back(token, taps))
        gm_w = Window(lambda t: gm_i[length + t] if t < 0 else gm_t[t])
        k_w, v_w = (Window(lambda t, view=view: view[length + t]) for view in (k_t, v_t))
        for token in range(-reach, 0):
            gp = dot_taps(wm, gm_w.ahead(token, taps))
            gk = gp * vc_i[length + token]
            gv = gp * kc_i[length + token]
            gk_o[token] = gk
            gv_o[token] = gv
            sums.add(1, gk, k_w.back(token, taps))
            sums.add(2, gv, v_w.back(token, taps))
        sums.store(acc, lanes)
        return carry

    lax.fori_loop(0, groups // LANES, column_step, 0)
    for bank in range(sums_ref.shape[1]):
        sums_ref[:, bank, :] = jnp.sum(acc[bank], axis=1)


def edge(weights, before, after, sums, arrays):
    taps, banks, groups = weights.shape
    channels = before.shape[1]
    repeats = channels // groups
    columns = groups // LANES
    reach = taps - 1
    halo_rows = -(-5 * reach // 8) * 8
    return pl.pallas_call(
        functools.partial(edge_kernel, taps, repeats),
        out_shape=(
            jax.ShapeDtypeStruct((CHUNK, channels), before.dtype),
            jax.ShapeDtypeStruct((3, columns, 2 * reach * repeats, LANES), F32),
            jax.ShapeDtypeStruct((2, columns, reach * repeats, LANES), F32),
            jax.ShapeDtypeStruct((taps, banks, groups), F32),
        ),
        in_specs=[VMEM_SPEC] * 12,
        out_specs=(VMEM_SPEC,) * 4,
        scratch_shapes=[
            pltpu.VMEM(sums.shape, F32),
            pltpu.VMEM((halo_rows, LANES), F32),
            pltpu.VMEM((halo_rows * repeats, LANES), F32),
        ]
        + [pltpu.VMEM((2 * PAD * repeats, LANES), F32) for _ in range(4)]
        + [pltpu.VMEM((CHUNK * repeats, LANES), F32)],
        cost_estimate=pl.CostEstimate(
            flops=10**7, bytes_accessed=4 * 10**6, transcendentals=0
        ),
        compiler_params=pltpu.CompilerParams(vmem_limit_bytes=VMEM_LIMIT),
        name="edge",
    )(weights, before, after, sums, *arrays)


def grads_kernel(taps, repeats, first, steps, count, *refs):
    refs = list(refs)
    top, bottom = first == 0, first + steps == count

    def pop(number):
        taken, refs[:number] = refs[:number], []
        return taken

    weights_ref, gq, gk, gv, ghead, gtail = pop(6)
    if top:
        middle, head = pop(2)
    else:
        pop(1)
    if bottom:
        after_ref, *ahead_of = pop(5)
    out_hbm, zero_ref = pop(2)
    copies = []
    out_s, o_s, sems = refs[-3:]
    reach = taps - 1
    groups = weights_ref.shape[2]
    columns = groups // LANES
    length = gq.shape[1] // repeats
    zero_ref[...] = jnp.zeros_like(zero_ref)
    if top:
        (mixed_hbm,) = pop(1)
        copies = [
            pltpu.make_async_copy(head, mixed_hbm.at[:CHUNK, :], sems.at[steps]),
            pltpu.make_async_copy(
                middle.at[CHUNK:, :], mixed_hbm.at[CHUNK:, :], sems.at[steps + 1]
            ),
        ]
        for copy in copies:
            copy.start()

    def load(bank, column, token):
        if token >= length:
            return Tokens(refs[0], repeats, 0, (bank, column))[token - length]
        if token < (reach if bank else 2 * reach):
            return Tokens(ghead, repeats, 0, (bank, column))[token]
        if bank and token >= length - reach:
            return Tokens(gtail, repeats, reach - length, (bank - 1, column))[token]
        return Tokens((gq, gk, gv)[bank], repeats, 0, (column,))[token]

    def next_shard(column, carry):
        gnext, n_s, h_s, p_s, gm_s = refs[:5]
        lanes = lane_slice(column)
        wq, wk, wv, wm = (weight_rows(weights_ref, bank, lanes) for bank in range(4))
        h_t, p_t, gm_t = (Tokens(ref, repeats) for ref in (h_s, p_s, gm_s))
        q_t, k_t, v_t, p_i = (
            Tokens(ref, repeats, PAD + length, (column,)) for ref in ahead_of
        )
        stage_halo(after_ref, n_s, h_t, repeats, groups, column, 6 * reach)
        q_w = Window(lambda t: q_t[t] if t < 0 else h_t[t])
        k_w = Window(lambda t: k_t[t] if t < 0 else h_t[4 * reach + t])
        v_w = Window(lambda t: v_t[t] if t < 0 else h_t[5 * reach + t])
        p_w = Window(lambda t: p_i[t] if t < 0 else p_t[t])
        gm_w = Window(lambda t: gm_t[t])
        next_q, next_k, next_v = (
            Tokens(gnext, repeats, 0, (bank, column)) for bank in range(3)
        )
        for token in range(2 * reach):
            gm_t[token] = h_t[2 * reach + token] * dot_taps(wq, q_w.back(token, taps))
        for token in range(reach):
            kc = dot_taps(wk, k_w.back(token, taps))
            vc = dot_taps(wv, v_w.back(token, taps))
            p_t[token] = kc * vc
            gp = dot_taps(wm, gm_w.ahead(token, taps))
            next_k[token] = gp * vc
            next_v[token] = gp * kc
            next_q[token] = h_t[2 * reach + token] * dot_taps(wm, p_w.back(token, taps))
        return carry

    def out_copy(slot):
        rows = slice((first + slot) * CHUNK, (first + slot + 1) * CHUNK)
        return pltpu.make_async_copy(out_s.at[slot], out_hbm.at[:, rows, :], sems.at[slot])

    if bottom:
        lax.fori_loop(0, columns, next_shard, 0)
    for slot in range(steps):
        base = (first + slot) * CHUNK

        def column_step(column, carry):
            lanes = lane_slice(column)
            o_t = Tokens(o_s, repeats)
            for bank in range(3):
                weights = weight_rows(weights_ref, bank, lanes)
                window = Window(lambda t: load(bank, column, base + t))
                for token in range(CHUNK):
                    o_t[token] = dot_taps(weights, window.ahead(token, taps))
                for repeat in range(repeats):
                    part = part_slice(repeat, groups, column)
                    out_s[slot, bank, :, part] = o_t.take(0, repeat, CHUNK).astype(out_s.dtype)
            return carry

        lax.fori_loop(0, columns, column_step, 0)
        out_copy(slot).start()
    for slot in range(steps):
        out_copy(slot).wait()
    for copy in copies:
        copy.wait()


def feature_gradients(
    piece, pieces, features, weights, grads, ghead, gtail, mixed, after, arrays, earlier, zero
):
    banks, length, channels = features.shape
    taps, _, groups = weights.shape
    repeats = channels // groups
    columns = groups // LANES
    reach = taps - 1
    count = length // CHUNK
    steps = count // pieces
    first = piece * steps
    operands = [weights, *grads, ghead, gtail]
    in_specs = [VMEM_SPEC] * len(operands)
    out_shape = [jax.ShapeDtypeStruct(features.shape, features.dtype), zero]
    out_specs = [ANY_SPEC, VMEM_SPEC]
    aliases = {}
    scratch = []
    if piece == 0:
        operands += mixed
        in_specs += [VMEM_SPEC] * 2
        out_shape.append(jax.ShapeDtypeStruct(mixed[0].shape, mixed[0].dtype))
        out_specs.append(ANY_SPEC)
    else:
        aliases = {len(operands): 0}
        operands.append(earlier)
        in_specs.append(ANY_SPEC)
    if piece == pieces - 1:
        q_a, k_a, v_a, _, _, _, p_a, _ = arrays
        operands += [after, q_a, k_a, v_a, p_a]
        in_specs += [VMEM_SPEC] * 5
        halo_rows = -(-after.shape[0] // 8) * 8
        scratch = [
            pltpu.VMEM((3, columns, reach * repeats, LANES), F32),
            pltpu.VMEM((halo_rows, LANES), F32),
            pltpu.VMEM((halo_rows * repeats, LANES), F32),
            pltpu.VMEM((reach * repeats, LANES), F32),
            pltpu.VMEM((2 * reach * repeats, LANES), F32),
        ]
    work = length * channels * taps * 2 // pieces
    return pl.pallas_call(
        functools.partial(grads_kernel, taps, repeats, first, steps, count),
        out_shape=out_shape,
        in_specs=in_specs,
        out_specs=out_specs,
        scratch_shapes=scratch
        + [
            pltpu.VMEM((steps, banks, CHUNK, channels), features.dtype),
            pltpu.VMEM((CHUNK * repeats, LANES), F32),
            pltpu.SemaphoreType.DMA((steps + 2,)),
        ],
        input_output_aliases=aliases,
        cost_estimate=pl.CostEstimate(
            flops=4 * work,
            bytes_accessed=18 * length * channels // pieces,
            transcendentals=0,
        ),
        compiler_params=pltpu.CompilerParams(vmem_limit_bytes=VMEM_LIMIT),
        name="feature_gradients",
    )(*operands)


def per_device(features, cotangent, master_filters):
    length = features.shape[1]
    tail, head, rounded = pack(features, cotangent, jnp.transpose(master_filters, (1, 0, 2)))
    staged, upstream, tail, head = lax.optimization_barrier((features, cotangent, tail, head))
    weights = gather_filters(rounded, "fsdp").astype(F32)
    before = shift_rows(tail, "ctx", 1)
    after = shift_rows(head, "ctx", -1)
    middle, grads, arrays, sums = interior(staged, upstream, weights)
    top, ghead, gtail, sums = edge(weights, before, after, sums, arrays)
    repeats = features.shape[2] // weights.shape[2]
    pieces = PIECES if (length // CHUNK) % PIECES == 0 else 1
    owned = sum_scatter(sums, "fsdp")
    made = {"grads": None}

    def beside(piece):
        if piece >= pieces:
            return 0.0
        made["grads"], zero, *rest = feature_gradients(
            piece,
            pieces,
            features,
            weights,
            grads,
            ghead,
            gtail,
            (middle, top),
            after,
            arrays,
            made["grads"],
            jax.ShapeDtypeStruct(owned.shape, F32),
        )
        if rest:
            made["mixed"] = rest[0]
        return zero

    summed, done = sum_over(owned, "ctx", beside)
    for piece in range(done, pieces):
        beside(piece)
    count_all = length * lax.axis_size("ctx") * repeats * lax.axis_size("fsdp")
    filter_grads = jnp.transpose(summed * (1.0 / math.sqrt(count_all)), (1, 0, 2))
    return (made["mixed"], made["grads"], filter_grads)


def solution(mesh):
    return jax.shard_map(
        per_device,
        mesh=mesh,
        in_specs=(P(None, "ctx", "fsdp"), P("ctx", "fsdp"), P(None, None, "fsdp")),
        out_specs=(P("ctx", "fsdp"), P(None, "ctx", "fsdp"), P(None, None, "fsdp")),
        check_vma=False,
    )
```

time: 175 us -> 43.4 us (0.25)
  local copies, waits for them, and re-layouts: 61.2 us -> 0.9 us
  other arithmetic: 50.5 us -> 0.92 us
  blocking collectives: 46.9 us -> 0 us
  Pallas kernels: 0 us -> 20.1 us
  starting transfers between devices: 13.6 us -> 17.6 us
  waiting for transfers between devices: 0.01 us -> 2.84 us
    slice x7 -> x0, local copies, waits for them, and re-layouts: 44.8 us -> none  [the longest x2 41.3 us: causal(): result = weights[0] * extended[reach:reach + length]]
    psum x1 -> x0, blocking collectives: 44.8 us -> none  [per_device(): summed = lax.psum(partial_sum, ('ctx', 'fsdp'))]
    reduce_sum x4 -> x0, other arithmetic: 23.5 us -> none  [the longest x3 23.4 us: per_device(): jnp.sum(grad_term * source[reach - lag:reach - lag + length], axis=0)]
    pallas_call x0 -> x7, Pallas kernels: none -> 20.1 us  [the longest x1 9.53 us: interior(): pl.pallas_call(functools.partial(interior_kernel, taps, repeats), out_sha...]
    another operation x86 -> x0, local copies, waits for them, and re-layouts: 15.1 us -> none  [the longest x56 8.55 us: per_device(): weights = jnp.tile(gathered, (1, 1, repeats))]
    mul x7 -> x0, other arithmetic: 14.1 us -> none  [the longest x1 8.38 us: per_device(): product = k_conv * v_conv]
    another operation x4 -> x0, other arithmetic: 7.53 us -> none  [per_device(): feature_grads = jnp.stack([grad_q, grad_k, grad_v]).astype(jnp.bfloat16)]
    convert_element_type x6 -> x1, other arithmetic: 5.15 us -> 0.08 us  [per_device(): weights = gather_filters(rounded, 'fsdp').astype(F32)]
  transfers between devices with their start and end apart: 4 -> 8, of which waited for: 0 -> 5; matrix products, arithmetic and copies ran while one was open for 35% -> 0% of each run, Pallas kernels for 0% -> 37%
where the time goes in v3:
time: 43.4 us; the launch traced here: 43.2 us
  Pallas kernels  20.1 us (46%)
  starting transfers between devices  17.6 us (41%)
  waiting for transfers between devices  2.84 us (7%)
  other arithmetic  0.92 us (2%)
  local copies, waits for them, and re-layouts  0.9 us (2%)
  between operations  0.8 us (2%)
    ppermute x4, starting transfers between devices, sum_over(): received = lax.ppermute(value, axis, pairs)  10.7 us
    pallas_call x1, Pallas kernels, interior(): pl.pallas_call(functools.partial(interior_kernel, taps, repeats), out_sha...  9.53 us
    ppermute x2, starting transfers between devices, shift_rows(): return lax.ppermute(value, axis, pairs)  6.38 us
    pallas_call x4, Pallas kernels, feature_gradients(): pl.pallas_call(functools.partial(grads_kernel, taps, repeats, first, step...  6.3 us
    pallas_call x1, Pallas kernels, pack(): pl.pallas_call(functools.partial(pack_kernel, reach), out_shape=(jax.Shap...  2.26 us
    pallas_call x1, Pallas kernels, edge(): pl.pallas_call(functools.partial(edge_kernel, taps, repeats), out_shape=(...  1.99 us
    ppermute x1, waiting for transfers between devices, sum_scatter(): sent = lax.ppermute(jnp.where(first, high, low), axis, [(0, 1), (1, 0)])  1.19 us
    ppermute x4, waiting for transfers between devices, sum_over(): received = lax.ppermute(value, axis, pairs)  1.09 us
  transfers between devices with their start and end apart: 8, of which 5 were waited for; matrix products, arithmetic and copies ran while one was open for 0% of the time, Pallas kernels for 37%

profile of v3, /device:TPU:0, one launch (start us, length us, event | category | flops | bytes accessed | tf_op | source)
XLA Modules:
  0.0 43.2 jit_solution(199996792867132488)
XLA Ops:
  0.6 0.0 copy-start.1
  0.6 0.0 copy-start
  0.7 0.0 copy-start.2
  0.7 0.9 %copy-done.2 = f32[4,7,192]{2,0,1:T(4,128)S(1)} copy-done((f32[4,7,192]{2,0,1:T(4,128)S(1)}, f32[4,7,192]{2,0,1:T(4,128)}, u32[]{:S(2)}) %copy-start.2) | copy-done | bytes 21528
  1.5 2.3 %pack_halos.1 = (bf16[30,3072]{1,0:T(8,128)(2,1)}, bf16[36,3072]{1,0:T(8,128)(2,1)}, bf16[7,4,192]{2,1,0:T(4,128)(2,1)S(1)}) custom-call(bf16[3,128,3072]{2,1,0:T(8,128)(2,1)} %features_ref, bf16[128,3072]{1,0:T(8,128)(2,1)} %cotangent_ref, f32[7,4,192]{2,1,0:T(4,128)S(1)} %bitcast.3), custom_call_target="tpu_custom_call" | custom-call | flops 1000000 | bytes 1000000 | tf_op jit(solution)/shard_map/pack_halos/pallas_call | solution.py:196
  3.8 0.5 %collective-permute-start = (bf16[7,4,192]{2,1,0:T(4,128)(2,1)S(1)}, bf16[7,4,192]{2,1,0:T(4,128)(2,1)S(1)}, u32[]{:S(2)}, u32[]{:S(2)}) collective-permute-start(bf16[7,4,192]{2,1,0:T(4,128)(2,1)S(1)} %get-tuple-element.36), channel_id=1, source_target_pairs={{0,1},{1,0},{2,3},{3,2},{4,5},{5,4},{6,7},{7,6},{8,9},{9,8},{10,11... | collective-permute-start | bytes 32264 | tf_op jit(solution)/shard_map/ppermute | solution.py:31
  4.3 5.1 %collective-permute-start.1 = (bf16[30,3072]{1,0:T(8,128)(2,1)}, bf16[30,3072]{1,0:T(8,128)(2,1)}, u32[]{:S(2)}, u32[]{:S(2)}) collective-permute-start(bf16[30,3072]{1,0:T(8,128)(2,1)} %get-tuple-element.44), channel_id=1, source_target_pairs={{0,2},{2,4},{4,6},{6,8},{8,10},{10,12},{12,14},{14,16},{16,18},{18... | collective-permute-start | bytes 552968 | tf_op jit(solution)/shard_map/ppermute | solution.py:24
  9.4 1.3 %collective-permute-start.2 = (bf16[36,3072]{1,0:T(8,128)(2,1)}, bf16[36,3072]{1,0:T(8,128)(2,1)S(1)}, u32[]{:S(2)}, u32[]{:S(2)}) collective-permute-start(bf16[36,3072]{1,0:T(8,128)(2,1)} %get-tuple-element.45), channel_id=1, source_target_pairs={{2,0},{4,2},{6,4},{8,6},{10,8},{12,10},{14,12},{16,14},{18,16},{20... | collective-permute-start | bytes 663560 | tf_op jit(solution)/shard_map/ppermute | solution.py:24
  10.7 0.0 collective-permute-done
  10.8 0.1 maximum_convert_fusion.weights_ref.refs_0_
  10.8 0.0 copy-done.1
  10.9 0.0 copy-done
  10.9 9.5 %interior.1 = (bf16[128,3072]{1,0:T(8,128)(2,1)S(1)}, f32[3,1024,128]{2,1,0:T(8,128)S(1)}, f32[3,1024,128]{2,1,0:T(8,128)S(1)}, f32[3,1024,128]{2,1,0:T(8,128)S(...) custom-call(bf16[3,128,3072]{2,1,0:T(8,128)(2,1)S(1)} %copy-done, ...), custom_call_target="tpu_custom_call" | custom-call | flops 49545216 | bytes 8650752 | tf_op jit(solution)/shard_map/interior/pallas_call | solution.py:345
  20.4 0.0 collective-permute-done.1.before_ref
  20.4 0.6 %collective-permute-done.2.after_ref.refs_7_ = bf16[36,3072]{1,0:T(8,128)(2,1)S(1)} collective-permute-done((bf16[36,3072]{1,0:T(8,128)(2,1)}, bf16[36,3072]{1,0:T(8,128)(2,1)S(1)}, u32[]{:S(2)}, u32[]{:S(2)}) %collective-permute-start.2) | collective-permute-done | bytes 221216 | tf_op jit(solution)/shard_map/ppermute | solution.py:24
  21.0 2.0 %edge.1 = (bf16[16,3072]{1,0:T(8,128)(2,1)S(1)}, f32[3,3,96,128]{3,2,1,0:T(8,128)S(1)}, f32[2,3,48,128]{3,2,1,0:T(8,128)S(1)}, f32[7,4,384]{2,1,0:T(4,128)S(1)}) custom-call(f32[7,4,384]{2,1,0:T(4,128)S(1)} %maximum_convert_fusion.weights_ref.refs_0_, bf16[30,3072]{1,0:T(8,128)(2,1)} %collective-permute-done.1.before_ref, ...), custom_call_target="tpu_custom_call" | custom-call | flops 10000000 | bytes 4000000 | tf_op jit(solution)/shard_map/edge/pallas_call | solution.py:485
  23.0 0.1 slice_select_fusion
  23.0 0.1 collective-permute-start.3
  23.1 1.2 %collective-permute-done.3 = f32[7,4,192]{2,1,0:T(4,128)S(1)} collective-permute-done((f32[7,4,192]{2,1,0:T(4,128)S(1)}, f32[7,4,192]{2,1,0:T(4,128)S(1)}, u32[]{:S(2)}, u32[]{:S(2)}) %collective-permute-start.3) | collective-permute-done | bytes 21536 | tf_op jit(solution)/shard_map/ppermute | solution.py:62
  24.3 0.1 select_add_fusion
  24.4 2.2 %collective-permute-start.4 = (f32[7,4,192]{2,1,0:T(4,128)S(1)}, f32[7,4,192]{2,1,0:T(4,128)S(1)}, u32[]{:S(2)}, u32[]{:S(2)}) collective-permute-start(f32[7,4,192]{2,1,0:T(4,128)S(1)} %select_add_fusion), channel_id=1, source_target_pairs={{0,2},{2,0},{4,6},{6,4},{8,10},{10,8},{12,14},{14,12},{16,18},{18,... | collective-permute-start | bytes 64520 | tf_op jit(solution)/shard_map/ppermute | solution.py:45
  26.6 1.5 %feature_gradients.4 = (bf16[3,128,3072]{2,1,0:T(8,128)(2,1)}, f32[7,4,192]{2,1,0:T(4,128)S(1)}, bf16[128,3072]{1,0:T(8,128)(2,1)}) custom-call(f32[7,4,384]{2,1,0:T(4,128)S(1)} %maximum_convert_fusion.weights_ref.refs_0_, f32[3,1024,128]{2,1,0:T(8,128)S(1)} %get-tuple-element.41.refs_1_, f32[3,1024,128]{2,1,0:T(8,128)S(1)} %get-tuple-element.42.refs_2_, ...), custom_call_target="tpu_custom_call" | custom-call | flops 5505024 | bytes 1769472 | tf_op jit(solution)/shard_map/feature_gradients/pallas_call | solution.py:651
  28.1 0.4 collective-permute-done.4
  28.4 2.3 %collective-permute-start.5 = (f32[7,4,192]{2,1,0:T(4,128)S(1)}, f32[7,4,192]{2,1,0:T(4,128)S(1)}, u32[]{:S(2)}, u32[]{:S(2)}) collective-permute-start(f32[7,4,192]{2,1,0:T(4,128)S(1)} %add_add_fusion.2), channel_id=1, source_target_pairs={{0,4},{2,6},{4,0},{6,2},{8,12},{10,14},{12,8},{14,10},{16,20},{18,... | collective-permute-start | bytes 64520 | tf_op jit(solution)/shard_map/ppermute | solution.py:45
  30.8 1.5 %feature_gradients.5 = (bf16[3,128,3072]{2,1,0:T(8,128)(2,1)}, f32[7,4,192]{2,1,0:T(4,128)S(1)}) custom-call(f32[7,4,384]{2,1,0:T(4,128)S(1)} %maximum_convert_fusion.weights_ref.refs_0_, f32[3,1024,128]{2,1,0:T(8,128)S(1)} %get-tuple-element.41.refs_1_, f32[3,1024,128]{2,1,0:T(8,128)S(1)} %get-tuple-element.42.refs_2_, ...), custom_call_target="tpu_custom_call", output_to_operand_aliasing={{0}: (6, {})} | custom-call | flops 5505024 | bytes 1769472 | tf_op jit(solution)/shard_map/feature_gradients/pallas_call | solution.py:651
  32.3 0.4 collective-permute-done.5
  32.6 3.0 %collective-permute-start.6 = (f32[7,4,192]{2,1,0:T(4,128)S(1)}, f32[7,4,192]{2,1,0:T(4,128)S(1)}, u32[]{:S(2)}, u32[]{:S(2)}) collective-permute-start(f32[7,4,192]{2,1,0:T(4,128)S(1)} %add_add_fusion.1), channel_id=1, source_target_pairs={{0,8},{2,10},{4,12},{6,14},{8,0},{10,2},{12,4},{14,6},{16,24},{18,... | collective-permute-start | bytes 64520 | tf_op jit(solution)/shard_map/ppermute | solution.py:45
  35.7 1.5 %feature_gradients.6 = (bf16[3,128,3072]{2,1,0:T(8,128)(2,1)}, f32[7,4,192]{2,1,0:T(4,128)S(1)}) custom-call(f32[7,4,384]{2,1,0:T(4,128)S(1)} %maximum_convert_fusion.weights_ref.refs_0_, f32[3,1024,128]{2,1,0:T(8,128)S(1)} %get-tuple-element.41.refs_1_, f32[3,1024,128]{2,1,0:T(8,128)S(1)} %get-tuple-element.42.refs_2_, ...), custom_call_target="tpu_custom_call", output_to_operand_aliasing={{0}: (6, {})} | custom-call | flops 5505024 | bytes 1769472 | tf_op jit(solution)/shard_map/feature_gradients/pallas_call | solution.py:651
  37.2 0.4 collective-permute-done.6
  37.5 3.1 %collective-permute-start.7 = (f32[7,4,192]{2,1,0:T(4,128)S(1)}, f32[7,4,192]{2,1,0:T(4,128)S(1)}, u32[]{:S(2)}, u32[]{:S(2)}) collective-permute-start(f32[7,4,192]{2,1,0:T(4,128)S(1)} %add_add_fusion), channel_id=1, source_target_pairs={{0,16},{2,18},{4,20},{6,22},{8,24},{10,26},{12,28},{14,30},{16,0},... | collective-permute-start | bytes 64520 | tf_op jit(solution)/shard_map/ppermute | solution.py:45
  40.6 1.9 %feature_gradients.7 = (bf16[3,128,3072]{2,1,0:T(8,128)(2,1)}, f32[7,4,192]{2,1,0:T(4,128)S(1)}) custom-call(f32[7,4,384]{2,1,0:T(4,128)S(1)} %maximum_convert_fusion.weights_ref.refs_0_, f32[3,1024,128]{2,1,0:T(8,128)S(1)} %get-tuple-element.41.refs_1_, f32[3,1024,128]{2,1,0:T(8,128)S(1)} %get-tuple-element.42.refs_2_, ...), custom_call_target="tpu_custom_call", output_to_operand_aliasing={{0}: (6, {})} | custom-call | flops 5505024 | bytes 1769472 | tf_op jit(solution)/shard_map/feature_gradients/pallas_call | solution.py:651
  42.5 0.0 collective-permute-done.7
  42.5 0.6 %multiply_bitcast_fusion = f32[4,7,192]{2,0,1:T(4,128)} fusion(f32[7,4,192]{2,1,0:T(4,128)S(1)} %get-tuple-element.68, f32[7,4,192]{2,1,0:T(4,128)S(1)} %add_add_fusion, f32[7,4,192]{2,1,0:T(4,128)S(1)} %collective-permute-done.7), kind=kLoop, calls=%fused_computation | loop fusion | flops 16128 | bytes 86016 | tf_op jit(solution)/shard_map/transpose | solution.py:712
  (4 shorter events, 0.1 us)
Async XLA Ops:
  0.6 10.2 %copy-start.1 = (bf16[128,3072]{1,0:T(8,128)(2,1)S(1)}, bf16[128,3072]{1,0:T(8,128)(2,1)}, u32[]{:S(2)}) copy-start(bf16[128,3072]{1,0:T(8,128)(2,1)} %cotangent_ref) | copy-start | bytes 2359300
  0.6 10.2 %copy-start = (bf16[3,128,3072]{2,1,0:T(8,128)(2,1)S(1)}, bf16[3,128,3072]{2,1,0:T(8,128)(2,1)}, u32[]{:S(2)}) copy-start(bf16[3,128,3072]{2,1,0:T(8,128)(2,1)} %features_ref) | copy-start | bytes 7077892
  0.7 0.9 %copy-start.2 = (f32[4,7,192]{2,0,1:T(4,128)S(1)}, f32[4,7,192]{2,0,1:T(4,128)}, u32[]{:S(2)}) copy-start(f32[4,7,192]{2,0,1:T(4,128)} %param.5) | copy-start | bytes 64516
  3.8 6.9 %collective-permute-start = (bf16[7,4,192]{2,1,0:T(4,128)(2,1)S(1)}, bf16[7,4,192]{2,1,0:T(4,128)(2,1)S(1)}, u32[]{:S(2)}, u32[]{:S(2)}) collective-permute-start(bf16[7,4,192]{2,1,0:T(4,128)(2,1)S(1)} %get-tuple-element.36), channel_id=1, source_target_pairs={{0,1},{1,0},{2,3},{3,2},{4,5},{5,4},{6,7},{7,6},{8,9},{9,8},{10,11... | collective-permute-start | bytes 32264 | tf_op jit(solution)/shard_map/ppermute | solution.py:31
  4.3 16.1 %collective-permute-start.1 = (bf16[30,3072]{1,0:T(8,128)(2,1)}, bf16[30,3072]{1,0:T(8,128)(2,1)}, u32[]{:S(2)}, u32[]{:S(2)}) collective-permute-start(bf16[30,3072]{1,0:T(8,128)(2,1)} %get-tuple-element.44), channel_id=1, source_target_pairs={{0,2},{2,4},{4,6},{6,8},{8,10},{10,12},{12,14},{14,16},{16,18},{18... | collective-permute-start | bytes 552968 | tf_op jit(solution)/shard_map/ppermute | solution.py:24
  9.4 11.5 %collective-permute-start.2 = (bf16[36,3072]{1,0:T(8,128)(2,1)}, bf16[36,3072]{1,0:T(8,128)(2,1)S(1)}, u32[]{:S(2)}, u32[]{:S(2)}) collective-permute-start(bf16[36,3072]{1,0:T(8,128)(2,1)} %get-tuple-element.45), channel_id=1, source_target_pairs={{2,0},{4,2},{6,4},{8,6},{10,8},{12,10},{14,12},{16,14},{18,16},{20... | collective-permute-start | bytes 663560 | tf_op jit(solution)/shard_map/ppermute | solution.py:24
  23.0 1.3 %collective-permute-start.3 = (f32[7,4,192]{2,1,0:T(4,128)S(1)}, f32[7,4,192]{2,1,0:T(4,128)S(1)}, u32[]{:S(2)}, u32[]{:S(2)}) collective-permute-start(f32[7,4,192]{2,1,0:T(4,128)S(1)} %slice_select_fusion), channel_id=1, source_target_pairs={{0,1},{1,0},{2,3},{3,2},{4,5},{5,4},{6,7},{7,6},{8,9},{9,8},{10,11... | collective-permute-start | bytes 64520 | tf_op jit(solution)/shard_map/ppermute | solution.py:62
  24.4 4.0 %collective-permute-start.4 = (f32[7,4,192]{2,1,0:T(4,128)S(1)}, f32[7,4,192]{2,1,0:T(4,128)S(1)}, u32[]{:S(2)}, u32[]{:S(2)}) collective-permute-start(f32[7,4,192]{2,1,0:T(4,128)S(1)} %select_add_fusion), channel_id=1, source_target_pairs={{0,2},{2,0},{4,6},{6,4},{8,10},{10,8},{12,14},{14,12},{16,18},{18,... | collective-permute-start | bytes 64520 | tf_op jit(solution)/shard_map/ppermute | solution.py:45
  28.4 4.2 %collective-permute-start.5 = (f32[7,4,192]{2,1,0:T(4,128)S(1)}, f32[7,4,192]{2,1,0:T(4,128)S(1)}, u32[]{:S(2)}, u32[]{:S(2)}) collective-permute-start(f32[7,4,192]{2,1,0:T(4,128)S(1)} %add_add_fusion.2), channel_id=1, source_target_pairs={{0,4},{2,6},{4,0},{6,2},{8,12},{10,14},{12,8},{14,10},{16,20},{18,... | collective-permute-start | bytes 64520 | tf_op jit(solution)/shard_map/ppermute | solution.py:45
  32.6 4.9 %collective-permute-start.6 = (f32[7,4,192]{2,1,0:T(4,128)S(1)}, f32[7,4,192]{2,1,0:T(4,128)S(1)}, u32[]{:S(2)}, u32[]{:S(2)}) collective-permute-start(f32[7,4,192]{2,1,0:T(4,128)S(1)} %add_add_fusion.1), channel_id=1, source_target_pairs={{0,8},{2,10},{4,12},{6,14},{8,0},{10,2},{12,4},{14,6},{16,24},{18,... | collective-permute-start | bytes 64520 | tf_op jit(solution)/shard_map/ppermute | solution.py:45
  37.5 5.0 %collective-permute-start.7 = (f32[7,4,192]{2,1,0:T(4,128)S(1)}, f32[7,4,192]{2,1,0:T(4,128)S(1)}, u32[]{:S(2)}, u32[]{:S(2)}) collective-permute-start(f32[7,4,192]{2,1,0:T(4,128)S(1)} %add_add_fusion), channel_id=1, source_target_pairs={{0,16},{2,18},{4,20},{6,22},{8,24},{10,26},{12,28},{14,30},{16,0},... | collective-permute-start | bytes 64520 | tf_op jit(solution)/shard_map/ppermute | solution.py:45

commit v4 on v3

--- a/solution.py
+++ b/solution.py
@@ -13,15 +13,24 @@
 PAD = 16
 PIECES = 4
 VMEM_LIMIT = 12 * 1024 * 1024
+PACK_LIMIT = 16 * 1024 * 1024
 F32 = jnp.float32
 VMEM_SPEC = pl.BlockSpec(memory_space=pltpu.VMEM)
 ANY_SPEC = pl.BlockSpec(memory_space=pl.ANY)
 
 
-def shift_rows(value, axis, by):
+def swap_pairs(near, far, axis):
     size = lax.axis_size(axis)
-    pairs = [(i, i + by) for i in range(size) if 0 <= i + by < size]
-    return lax.ppermute(value, axis, pairs)
+    inner = [(i, i ^ 1) for i in range(size) if i ^ 1 < size]
+    outer = [(i, i - 1 if i % 2 == 0 else i + 1) for i in range(size)]
+    outer = [(i, j) for i, j in outer if 0 <= j < size]
+    far = lax.ppermute(far, axis, outer)
+    near = lax.ppermute(near, axis, inner)
+    return near, far
+
+
+def is_even(axis):
+    return lax.rem(lax.axis_index(axis), 2) == 0
 
 
 def gather_filters(shard, axis):
@@ -146,28 +155,32 @@
     reach,
     features_hbm,
     cotangent_hbm,
-    master_ref,
-    before_ref,
-    after_ref,
+    master_hbm,
+    near_ref,
+    far_ref,
     rounded_ref,
     tail,
     head,
     upstream,
+    master,
     b_s,
     a_s,
     sems,
 ):
     length = cotangent_hbm.shape[0]
     copies = [
+        pltpu.make_async_copy(master_hbm, master, sems.at[3]),
         pltpu.make_async_copy(features_hbm.at[:, length - PAD :, :], tail, sems.at[0]),
         pltpu.make_async_copy(features_hbm.at[:, :PAD, :], head, sems.at[1]),
         pltpu.make_async_copy(cotangent_hbm.at[:PAD, :], upstream, sems.at[2]),
     ]
     for copy in copies:
         copy.start()
-    rounded_ref[...] = master_ref[...].astype(rounded_ref.dtype)
+    even = is_even("ctx")
+    b_s[...] = jnp.zeros_like(b_s)
     for copy in copies:
         copy.wait()
+    rounded_ref[...] = master[...].astype(rounded_ref.dtype)
 
     def column(index, carry):
         lanes = lane_slice(index)
@@ -178,50 +191,45 @@
         b_s[0:reach, :] = rows(tail, 0, PAD - reach, PAD)
         b_s[reach : 3 * reach, :] = rows(tail, 1, PAD - 2 * reach, PAD)
         b_s[3 * reach : 5 * reach, :] = rows(tail, 2, PAD - 2 * reach, PAD)
-        before_ref[:, lanes] = b_s[...].astype(before_ref.dtype)
         a_s[0 : 2 * reach, :] = rows(head, 0, 0, 2 * reach)
         a_s[2 * reach : 4 * reach, :] = upstream[:, lanes].astype(F32)[: 2 * reach]
         a_s[4 * reach : 5 * reach, :] = rows(head, 1, 0, reach)
         a_s[5 * reach : 6 * reach, :] = rows(head, 2, 0, reach)
-        after_ref[:, lanes] = a_s[...].astype(after_ref.dtype)
+        last, first = b_s[...], a_s[...]
+        near_ref[:, lanes] = jnp.where(even, last, first).astype(near_ref.dtype)
+        far_ref[:, lanes] = jnp.where(even, first, last).astype(far_ref.dtype)
         return carry
 
-    lax.fori_loop(0, before_ref.shape[1] // LANES, column, 0)
+    lax.fori_loop(0, near_ref.shape[1] // LANES, column, 0)
 
 
 def pack(features, cotangent, master):
     reach = master.shape[0] - 1
     banks, length, channels = features.shape
     kind = features.dtype
+    hbm = [
+        pltpu.with_memory_space_constraint(value, pltpu.HBM)
+        for value in (features, cotangent, master)
+    ]
+    message = jax.ShapeDtypeStruct((6 * reach, channels), kind)
     return pl.pallas_call(
         functools.partial(pack_kernel, reach),
-        out_shape=(
-            jax.ShapeDtypeStruct((5 * reach, channels), kind),
-            jax.ShapeDtypeStruct((6 * reach, channels), kind),
-            jax.ShapeDtypeStruct(master.shape, jnp.bfloat16),
-        ),
-        in_specs=[
-            pl.BlockSpec(memory_space=pltpu.HBM),
-            pl.BlockSpec(memory_space=pltpu.HBM),
-            VMEM_SPEC,
-        ],
+        out_shape=(message, message, jax.ShapeDtypeStruct(master.shape, jnp.bfloat16)),
+        in_specs=[pl.BlockSpec(memory_space=pltpu.HBM)] * 3,
         out_specs=(VMEM_SPEC,) * 3,
         scratch_shapes=[
             pltpu.VMEM((banks, PAD, channels), kind),
             pltpu.VMEM((banks, PAD, channels), kind),
             pltpu.VMEM((PAD, channels), kind),
-            pltpu.VMEM((5 * reach, LANES), F32),
+            pltpu.VMEM(master.shape, F32),
             pltpu.VMEM((6 * reach, LANES), F32),
-            pltpu.SemaphoreType.DMA((3,)),
+            pltpu.VMEM((6 * reach, LANES), F32),
+            pltpu.SemaphoreType.DMA((4,)),
         ],
         cost_estimate=pl.CostEstimate(flops=10**6, bytes_accessed=10**6, transcendentals=0),
-        compiler_params=pltpu.CompilerParams(vmem_limit_bytes=8 * 1024 * 1024),
+        compiler_params=pltpu.CompilerParams(vmem_limit_bytes=PACK_LIMIT),
         name="pack_halos",
-    )(
-        pltpu.with_memory_space_constraint(features, pltpu.HBM),
-        pltpu.with_memory_space_constraint(cotangent, pltpu.HBM),
-        master,
-    )
+    )(*hbm)
 
 
 def interior_kernel(
@@ -362,9 +370,9 @@
     return mixed, (gq, gk, gv), arrays, sums
 
 
-def stage_halo(halo_ref, n_s, view, repeats, groups, column, rows):
+def stage_halo(load, n_s, view, repeats, groups, column, rows):
     for repeat in range(repeats):
-        n_s[0:rows, :] = halo_ref[0:rows, part_slice(repeat, groups, column)].astype(F32)
+        n_s[0:rows, :] = load(part_slice(repeat, groups, column)).astype(F32)
         view.put(0, repeat, n_s[...])
 
 
@@ -372,8 +380,8 @@
     taps,
     repeats,
     weights_ref,
-    before_ref,
-    after_ref,
+    near_ref,
+    far_ref,
     sums_in_ref,
     q_a,
     k_a,
@@ -386,6 +394,7 @@
     mixed_ref,
     ghead_ref,
     gtail_ref,
+    after_ref,
     sums_ref,
     acc,
     n_s,
@@ -400,6 +409,7 @@
     groups = weights_ref.shape[2]
     length = q_a.shape[1] // repeats - 2 * PAD
     acc[...] = sums_in_ref[...]
+    even = is_even("ctx")
     h_t, m_t = Tokens(h_s, repeats), Tokens(m_s, repeats)
     kc_t, vc_t, p_t, gm_t = (Tokens(ref, repeats, PAD) for ref in (kc_s, vc_s, p_s, gm_s))
 
@@ -412,7 +422,18 @@
         )
         sums = Sums(taps)
 
-        stage_halo(before_ref, n_s, h_t, repeats, groups, column, 5 * reach)
+        def before(part):
+            rows = slice(0, 5 * reach)
+            return jnp.where(
+                even, far_ref[rows, part].astype(F32), near_ref[rows, part].astype(F32)
+            )
+
+        def after(part):
+            value = jnp.where(even, near_ref[:, part].astype(F32), far_ref[:, part].astype(F32))
+            after_ref[:, part] = value.astype(after_ref.dtype)
+            return value
+
+        stage_halo(before, n_s, h_t, repeats, groups, column, 5 * reach)
         q_w = Window(lambda t: q_t[t] if t >= 0 else h_t[reach + t])
         k_w = Window(lambda t: k_t[t] if t >= 0 else h_t[3 * reach + t])
         v_w = Window(lambda t: v_t[t] if t >= 0 else h_t[5 * reach + t])
@@ -452,7 +473,7 @@
             part = part_slice(repeat, groups, column)
             mixed_ref[:, part] = m_t.take(0, repeat, CHUNK).astype(mixed_ref.dtype)
 
-        stage_halo(after_ref, n_s, h_t, repeats, groups, column, 4 * reach)
+        stage_halo(after, n_s, h_t, repeats, groups, column, 6 * reach)
         q_w = Window(lambda t: q_t[length + t] if t < 0 else h_t[t])
         gk_o, gv_o = (Tokens(gtail_ref, repeats, reach, (bank, column)) for bank in range(2))
         for token in range(reach):
@@ -475,23 +496,24 @@
         sums_ref[:, bank, :] = jnp.sum(acc[bank], axis=1)
 
 
-def edge(weights, before, after, sums, arrays):
+def edge(weights, near, far, sums, arrays):
     taps, banks, groups = weights.shape
-    channels = before.shape[1]
+    channels = near.shape[1]
     repeats = channels // groups
     columns = groups // LANES
     reach = taps - 1
-    halo_rows = -(-5 * reach // 8) * 8
+    halo_rows = -(-6 * reach // 8) * 8
     return pl.pallas_call(
         functools.partial(edge_kernel, taps, repeats),
         out_shape=(
-            jax.ShapeDtypeStruct((CHUNK, channels), before.dtype),
+            jax.ShapeDtypeStruct((CHUNK, channels), near.dtype),
             jax.ShapeDtypeStruct((3, columns, 2 * reach * repeats, LANES), F32),
             jax.ShapeDtypeStruct((2, columns, reach * repeats, LANES), F32),
+            jax.ShapeDtypeStruct(near.shape, near.dtype),
             jax.ShapeDtypeStruct((taps, banks, groups), F32),
         ),
         in_specs=[VMEM_SPEC] * 12,
-        out_specs=(VMEM_SPEC,) * 4,
+        out_specs=(VMEM_SPEC,) * 5,
         scratch_shapes=[
             pltpu.VMEM(sums.shape, F32),
             pltpu.VMEM((halo_rows, LANES), F32),
@@ -504,7 +526,7 @@
         ),
         compiler_params=pltpu.CompilerParams(vmem_limit_bytes=VMEM_LIMIT),
         name="edge",
-    )(weights, before, after, sums, *arrays)
+    )(weights, near, far, sums, *arrays)
 
 
 def grads_kernel(taps, repeats, first, steps, count, *refs):
@@ -558,7 +580,7 @@
         q_t, k_t, v_t, p_i = (
             Tokens(ref, repeats, PAD + length, (column,)) for ref in ahead_of
         )
-        stage_halo(after_ref, n_s, h_t, repeats, groups, column, 6 * reach)
+        stage_halo(lambda part: after_ref[:, part], n_s, h_t, repeats, groups, column, 6 * reach)
         q_w = Window(lambda t: q_t[t] if t < 0 else h_t[t])
         k_w = Window(lambda t: k_t[t] if t < 0 else h_t[4 * reach + t])
         v_w = Window(lambda t: v_t[t] if t < 0 else h_t[5 * reach + t])
@@ -672,13 +694,11 @@
 
 def per_device(features, cotangent, master_filters):
     length = features.shape[1]
-    tail, head, rounded = pack(features, cotangent, jnp.transpose(master_filters, (1, 0, 2)))
-    staged, upstream, tail, head = lax.optimization_barrier((features, cotangent, tail, head))
+    near, far, rounded = pack(features, cotangent, jnp.transpose(master_filters, (1, 0, 2)))
     weights = gather_filters(rounded, "fsdp").astype(F32)
-    before = shift_rows(tail, "ctx", 1)
-    after = shift_rows(head, "ctx", -1)
-    middle, grads, arrays, sums = interior(staged, upstream, weights)
-    top, ghead, gtail, sums = edge(weights, before, after, sums, arrays)
+    halos = swap_pairs(near, far, "ctx")
+    middle, grads, arrays, sums = interior(features, cotangent, weights)
+    top, ghead, gtail, after, sums = edge(weights, *halos, sums, arrays)
     repeats = features.shape[2] // weights.shape[2]
     pieces = PIECES if (length // CHUNK) % PIECES == 0 else 1
     owned = sum_scatter(sums, "fsdp")

time: 43.4 us -> 40.2 us (0.926)
  starting transfers between devices: 17.6 us -> 14.2 us
  local copies, waits for them, and re-layouts: 0.9 us -> 0.01 us
  waiting for transfers between devices: 2.84 us -> 3.71 us
    ppermute x2, starting transfers between devices: 6.38 us -> 3.91 us  [the longest x1 2.56 us: swap_pairs(): near = lax.ppermute(near, axis, inner)]
    ppermute x4, waiting for transfers between devices: 1.09 us -> 2.12 us  [sum_over(): received = lax.ppermute(value, axis, pairs)]
    ppermute x4, starting transfers between devices: 10.7 us -> 9.71 us  [sum_over(): received = lax.ppermute(value, axis, pairs)]
    unnamed x6 -> x4, local copies, waits for them, and re-layouts: 0.9 us -> 0.01 us
  transfers between devices with their start and end apart: 8 -> 8, of which waited for: 5 -> 5; matrix products, arithmetic and copies ran while one was open for 0% -> 0% of each run, Pallas kernels for 37% -> 39%
where the time goes in v4:
time: 40.2 us; the launch traced here: 40.1 us
  Pallas kernels  20.4 us (51%)
  starting transfers between devices  14.2 us (35%)
  waiting for transfers between devices  3.71 us (9%)
  other arithmetic  0.92 us (2%)
  between operations  0.76 us (2%)
    ppermute x4, starting transfers between devices, sum_over(): received = lax.ppermute(value, axis, pairs)  9.71 us
    pallas_call x1, Pallas kernels, interior(): pl.pallas_call(functools.partial(interior_kernel, taps, repeats), out_sha...  9.53 us
    pallas_call x4, Pallas kernels, feature_gradients(): pl.pallas_call(functools.partial(grads_kernel, taps, repeats, first, step...  6.3 us
    ppermute x1, starting transfers between devices, swap_pairs(): near = lax.ppermute(near, axis, inner)  2.56 us
    pallas_call x1, Pallas kernels, pack(): pl.pallas_call(functools.partial(pack_kernel, reach), out_shape=(message,...  2.49 us
    pallas_call x1, Pallas kernels, edge(): pl.pallas_call(functools.partial(edge_kernel, taps, repeats), out_shape=(...  2.12 us
    ppermute x4, waiting for transfers between devices, sum_over(): received = lax.ppermute(value, axis, pairs)  2.12 us
    ppermute x1, starting transfers between devices, swap_pairs(): far = lax.ppermute(far, axis, outer)  1.35 us
  transfers between devices with their start and end apart: 8, of which 5 were waited for; matrix products, arithmetic and copies ran while one was open for 0% of the time, Pallas kernels for 39%

profile of v4, /device:TPU:0, one launch (start us, length us, event | category | flops | bytes accessed | tf_op | source)
XLA Modules:
  0.0 40.1 jit_solution(6357869777575925259)
XLA Ops:
  0.6 0.0 copy-start.1
  0.6 0.0 copy-start
  0.7 2.5 %pack_halos.1 = (bf16[36,3072]{1,0:T(8,128)(2,1)}, bf16[36,3072]{1,0:T(8,128)(2,1)}, bf16[7,4,192]{2,1,0:T(4,128)(2,1)S(1)}) custom-call(bf16[3,128,3072]{2,1,0:T(8,128)(2,1)} %features_ref.1, bf16[128,3072]{1,0:T(8,128)(2,1)} %cotangent_ref.1, f32[7,4,192]{2,1,0:T(4,128)} %bitcast.3), custom_call_target="tpu_custom_call" | custom-call | flops 1000000 | bytes 1000000 | tf_op jit(solution)/shard_map/pack_halos/pallas_call | solution.py:215
  3.2 0.5 %collective-permute-start = (bf16[7,4,192]{2,1,0:T(4,128)(2,1)S(1)}, bf16[7,4,192]{2,1,0:T(4,128)(2,1)S(1)}, u32[]{:S(2)}, u32[]{:S(2)}) collective-permute-start(bf16[7,4,192]{2,1,0:T(4,128)(2,1)S(1)} %get-tuple-element.33), channel_id=1, source_target_pairs={{0,1},{1,0},{2,3},{3,2},{4,5},{5,4},{6,7},{7,6},{8,9},{9,8},{10,11... | collective-permute-start | bytes 32264 | tf_op jit(solution)/shard_map/ppermute | solution.py:40
  3.7 2.6 %collective-permute-start.1 = (bf16[36,3072]{1,0:T(8,128)(2,1)}, bf16[36,3072]{1,0:T(8,128)(2,1)S(1)}, u32[]{:S(2)}, u32[]{:S(2)}) collective-permute-start(bf16[36,3072]{1,0:T(8,128)(2,1)} %get-tuple-element.37), channel_id=1, source_target_pairs={{0,2},{2,0},{4,6},{6,4},{8,10},{10,8},{12,14},{14,12},{16,18},{18,... | collective-permute-start | bytes 663560 | tf_op jit(solution)/shard_map/ppermute | solution.py:28
  6.2 1.3 %collective-permute-start.2 = (bf16[36,3072]{1,0:T(8,128)(2,1)}, bf16[36,3072]{1,0:T(8,128)(2,1)}, u32[]{:S(2)}, u32[]{:S(2)}) collective-permute-start(bf16[36,3072]{1,0:T(8,128)(2,1)} %get-tuple-element.38), channel_id=1, source_target_pairs={{2,4},{4,2},{6,8},{8,6},{10,12},{12,10},{14,16},{16,14},{18,20},{2... | collective-permute-start | bytes 663560 | tf_op jit(solution)/shard_map/ppermute | solution.py:27
  7.6 0.0 collective-permute-done
  7.6 0.1 maximum_convert_fusion.weights_ref.refs_0_
  7.7 0.0 copy-done.1
  7.7 0.0 copy-done
  7.7 9.5 %interior.1 = (bf16[128,3072]{1,0:T(8,128)(2,1)S(1)}, f32[3,1024,128]{2,1,0:T(8,128)S(1)}, f32[3,1024,128]{2,1,0:T(8,128)S(1)}, f32[3,1024,128]{2,1,0:T(8,128)S(...) custom-call(bf16[3,128,3072]{2,1,0:T(8,128)(2,1)S(1)} %copy-done, ...), custom_call_target="tpu_custom_call" | custom-call | flops 49545216 | bytes 8650752 | tf_op jit(solution)/shard_map/interior/pallas_call | solution.py:353
  17.2 0.4 %collective-permute-done.1.near_ref = bf16[36,3072]{1,0:T(8,128)(2,1)S(1)} collective-permute-done((bf16[36,3072]{1,0:T(8,128)(2,1)}, bf16[36,3072]{1,0:T(8,128)(2,1)S(1)}, u32[]{:S(2)}, u32[]{:S(2)}) %collective-permute-start.1) | collective-permute-done | bytes 221216 | tf_op jit(solution)/shard_map/ppermute | solution.py:28
  17.6 0.0 collective-permute-done.2.far_ref
  17.6 2.1 %edge.1 = (bf16[16,3072]{1,0:T(8,128)(2,1)S(1)}, f32[3,3,96,128]{3,2,1,0:T(8,128)S(1)}, f32[2,3,48,128]{3,2,1,0:T(8,128)S(1)}, bf16[36,3072]{1,0:T(8,128)(2,1)S(1)}, f32[7,4,384]{2,1,0:T(4,128)S(1)}) custom-call(f32[7,4,384]{2,1,0:T(4,128)S(1)} %maximum_convert_fusion.weights_ref.refs_0_, bf16[36,3072]{1,0:T(8,128)(2,1)S(1)} %collective-permute-done.1.near_ref, ...), custom_call_target="tpu_custom_call" | custom-call | flops 10000000 | bytes 4000000 | tf_op jit(solution)/shard_map/edge/pallas_call | solution.py:506
  19.8 0.1 slice_select_fusion
  19.9 0.1 collective-permute-start.3
  19.9 1.2 %collective-permute-done.3 = f32[7,4,192]{2,1,0:T(4,128)S(1)} collective-permute-done((f32[7,4,192]{2,1,0:T(4,128)S(1)}, f32[7,4,192]{2,1,0:T(4,128)S(1)}, u32[]{:S(2)}, u32[]{:S(2)}) %collective-permute-start.3) | collective-permute-done | bytes 21536 | tf_op jit(solution)/shard_map/ppermute | solution.py:71
  21.1 0.1 select_add_fusion
  21.2 3.5 %collective-permute-start.4 = (f32[7,4,192]{2,1,0:T(4,128)S(1)}, f32[7,4,192]{2,1,0:T(4,128)S(1)}, u32[]{:S(2)}, u32[]{:S(2)}) collective-permute-start(f32[7,4,192]{2,1,0:T(4,128)S(1)} %select_add_fusion), channel_id=1, source_target_pairs={{0,2},{2,0},{4,6},{6,4},{8,10},{10,8},{12,14},{14,12},{16,18},{18,... | collective-permute-start | bytes 64520 | tf_op jit(solution)/shard_map/ppermute | solution.py:54
  24.7 1.5 %feature_gradients.4 = (bf16[3,128,3072]{2,1,0:T(8,128)(2,1)}, f32[7,4,192]{2,1,0:T(4,128)S(1)}, bf16[128,3072]{1,0:T(8,128)(2,1)}) custom-call(f32[7,4,384]{2,1,0:T(4,128)S(1)} %maximum_convert_fusion.weights_ref.refs_0_, f32[3,1024,128]{2,1,0:T(8,128)S(1)} %get-tuple-element.34.refs_1_, f32[3,1024,128]{2,1,0:T(8,128)S(1)} %get-tuple-element.35.refs_2_, ...), custom_call_target="tpu_custom_call" | custom-call | flops 5505024 | bytes 1769472 | tf_op jit(solution)/shard_map/feature_gradients/pallas_call | solution.py:673
  26.2 0.4 collective-permute-done.4
  26.6 1.3 %collective-permute-start.5 = (f32[7,4,192]{2,1,0:T(4,128)S(1)}, f32[7,4,192]{2,1,0:T(4,128)S(1)}, u32[]{:S(2)}, u32[]{:S(2)}) collective-permute-start(f32[7,4,192]{2,1,0:T(4,128)S(1)} %add_add_fusion.2), channel_id=1, source_target_pairs={{0,4},{2,6},{4,0},{6,2},{8,12},{10,14},{12,8},{14,10},{16,20},{18,... | collective-permute-start | bytes 64520 | tf_op jit(solution)/shard_map/ppermute | solution.py:54
  27.9 1.5 %feature_gradients.5 = (bf16[3,128,3072]{2,1,0:T(8,128)(2,1)}, f32[7,4,192]{2,1,0:T(4,128)S(1)}) custom-call(f32[7,4,384]{2,1,0:T(4,128)S(1)} %maximum_convert_fusion.weights_ref.refs_0_, f32[3,1024,128]{2,1,0:T(8,128)S(1)} %get-tuple-element.34.refs_1_, f32[3,1024,128]{2,1,0:T(8,128)S(1)} %get-tuple-element.35.refs_2_, ...), custom_call_target="tpu_custom_call", output_to_operand_aliasing={{0}: (6, {})} | custom-call | flops 5505024 | bytes 1769472 | tf_op jit(solution)/shard_map/feature_gradients/pallas_call | solution.py:673
  29.4 1.1 %collective-permute-done.5 = f32[7,4,192]{2,1,0:T(4,128)S(1)} collective-permute-done((f32[7,4,192]{2,1,0:T(4,128)S(1)}, f32[7,4,192]{2,1,0:T(4,128)S(1)}, u32[]{:S(2)}, u32[]{:S(2)}) %collective-permute-start.5) | collective-permute-done | bytes 21536 | tf_op jit(solution)/shard_map/ppermute | solution.py:54
  30.5 1.8 %collective-permute-start.6 = (f32[7,4,192]{2,1,0:T(4,128)S(1)}, f32[7,4,192]{2,1,0:T(4,128)S(1)}, u32[]{:S(2)}, u32[]{:S(2)}) collective-permute-start(f32[7,4,192]{2,1,0:T(4,128)S(1)} %add_add_fusion.1), channel_id=1, source_target_pairs={{0,8},{2,10},{4,12},{6,14},{8,0},{10,2},{12,4},{14,6},{16,24},{18,... | collective-permute-start | bytes 64520 | tf_op jit(solution)/shard_map/ppermute | solution.py:54
  32.3 1.5 %feature_gradients.6 = (bf16[3,128,3072]{2,1,0:T(8,128)(2,1)}, f32[7,4,192]{2,1,0:T(4,128)S(1)}) custom-call(f32[7,4,384]{2,1,0:T(4,128)S(1)} %maximum_convert_fusion.weights_ref.refs_0_, f32[3,1024,128]{2,1,0:T(8,128)S(1)} %get-tuple-element.34.refs_1_, f32[3,1024,128]{2,1,0:T(8,128)S(1)} %get-tuple-element.35.refs_2_, ...), custom_call_target="tpu_custom_call", output_to_operand_aliasing={{0}: (6, {})} | custom-call | flops 5505024 | bytes 1769472 | tf_op jit(solution)/shard_map/feature_gradients/pallas_call | solution.py:673
  33.8 0.6 %collective-permute-done.6 = f32[7,4,192]{2,1,0:T(4,128)S(1)} collective-permute-done((f32[7,4,192]{2,1,0:T(4,128)S(1)}, f32[7,4,192]{2,1,0:T(4,128)S(1)}, u32[]{:S(2)}, u32[]{:S(2)}) %collective-permute-start.6) | collective-permute-done | bytes 21536 | tf_op jit(solution)/shard_map/ppermute | solution.py:54
  34.5 3.1 %collective-permute-start.7 = (f32[7,4,192]{2,1,0:T(4,128)S(1)}, f32[7,4,192]{2,1,0:T(4,128)S(1)}, u32[]{:S(2)}, u32[]{:S(2)}) collective-permute-start(f32[7,4,192]{2,1,0:T(4,128)S(1)} %add_add_fusion), channel_id=1, source_target_pairs={{0,16},{2,18},{4,20},{6,22},{8,24},{10,26},{12,28},{14,30},{16,0},... | collective-permute-start | bytes 64520 | tf_op jit(solution)/shard_map/ppermute | solution.py:54
  37.5 1.9 %feature_gradients.7 = (bf16[3,128,3072]{2,1,0:T(8,128)(2,1)}, f32[7,4,192]{2,1,0:T(4,128)S(1)}) custom-call(f32[7,4,384]{2,1,0:T(4,128)S(1)} %maximum_convert_fusion.weights_ref.refs_0_, f32[3,1024,128]{2,1,0:T(8,128)S(1)} %get-tuple-element.34.refs_1_, f32[3,1024,128]{2,1,0:T(8,128)S(1)} %get-tuple-element.35.refs_2_, ...), custom_call_target="tpu_custom_call", output_to_operand_aliasing={{0}: (6, {})} | custom-call | flops 5505024 | bytes 1769472 | tf_op jit(solution)/shard_map/feature_gradients/pallas_call | solution.py:673
  39.4 0.0 collective-permute-done.7
  39.4 0.6 %multiply_bitcast_fusion = f32[4,7,192]{2,0,1:T(4,128)} fusion(f32[7,4,192]{2,1,0:T(4,128)S(1)} %get-tuple-element.62, f32[7,4,192]{2,1,0:T(4,128)S(1)} %add_add_fusion, f32[7,4,192]{2,1,0:T(4,128)S(1)} %collective-permute-done.7), kind=kLoop, calls=%fused_computation | loop fusion | flops 16128 | bytes 86016 | tf_op jit(solution)/shard_map/transpose | solution.py:732
  (4 shorter events, 0.1 us)
Async XLA Ops:
  0.6 7.1 %copy-start.1 = (bf16[128,3072]{1,0:T(8,128)(2,1)S(1)}, bf16[128,3072]{1,0:T(8,128)(2,1)}, u32[]{:S(2)}) copy-start(bf16[128,3072]{1,0:T(8,128)(2,1)} %cotangent_ref.1) | copy-start | bytes 2359300
  0.6 7.1 %copy-start = (bf16[3,128,3072]{2,1,0:T(8,128)(2,1)S(1)}, bf16[3,128,3072]{2,1,0:T(8,128)(2,1)}, u32[]{:S(2)}) copy-start(bf16[3,128,3072]{2,1,0:T(8,128)(2,1)} %features_ref.1) | copy-start | bytes 7077892
  3.2 4.4 %collective-permute-start = (bf16[7,4,192]{2,1,0:T(4,128)(2,1)S(1)}, bf16[7,4,192]{2,1,0:T(4,128)(2,1)S(1)}, u32[]{:S(2)}, u32[]{:S(2)}) collective-permute-start(bf16[7,4,192]{2,1,0:T(4,128)(2,1)S(1)} %get-tuple-element.33), channel_id=1, source_target_pairs={{0,1},{1,0},{2,3},{3,2},{4,5},{5,4},{6,7},{7,6},{8,9},{9,8},{10,11... | collective-permute-start | bytes 32264 | tf_op jit(solution)/shard_map/ppermute | solution.py:40
  3.7 14.0 %collective-permute-start.1 = (bf16[36,3072]{1,0:T(8,128)(2,1)}, bf16[36,3072]{1,0:T(8,128)(2,1)S(1)}, u32[]{:S(2)}, u32[]{:S(2)}) collective-permute-start(bf16[36,3072]{1,0:T(8,128)(2,1)} %get-tuple-element.37), channel_id=1, source_target_pairs={{0,2},{2,0},{4,6},{6,4},{8,10},{10,8},{12,14},{14,12},{16,18},{18,... | collective-permute-start | bytes 663560 | tf_op jit(solution)/shard_map/ppermute | solution.py:28
  6.2 11.4 %collective-permute-start.2 = (bf16[36,3072]{1,0:T(8,128)(2,1)}, bf16[36,3072]{1,0:T(8,128)(2,1)}, u32[]{:S(2)}, u32[]{:S(2)}) collective-permute-start(bf16[36,3072]{1,0:T(8,128)(2,1)} %get-tuple-element.38), channel_id=1, source_target_pairs={{2,4},{4,2},{6,8},{8,6},{10,12},{12,10},{14,16},{16,14},{18,20},{2... | collective-permute-start | bytes 663560 | tf_op jit(solution)/shard_map/ppermute | solution.py:27
  19.9 1.3 %collective-permute-start.3 = (f32[7,4,192]{2,1,0:T(4,128)S(1)}, f32[7,4,192]{2,1,0:T(4,128)S(1)}, u32[]{:S(2)}, u32[]{:S(2)}) collective-permute-start(f32[7,4,192]{2,1,0:T(4,128)S(1)} %slice_select_fusion), channel_id=1, source_target_pairs={{0,1},{1,0},{2,3},{3,2},{4,5},{5,4},{6,7},{7,6},{8,9},{9,8},{10,11... | collective-permute-start | bytes 64520 | tf_op jit(solution)/shard_map/ppermute | solution.py:71
  21.2 5.3 %collective-permute-start.4 = (f32[7,4,192]{2,1,0:T(4,128)S(1)}, f32[7,4,192]{2,1,0:T(4,128)S(1)}, u32[]{:S(2)}, u32[]{:S(2)}) collective-permute-start(f32[7,4,192]{2,1,0:T(4,128)S(1)} %select_add_fusion), channel_id=1, source_target_pairs={{0,2},{2,0},{4,6},{6,4},{8,10},{10,8},{12,14},{14,12},{16,18},{18,... | collective-permute-start | bytes 64520 | tf_op jit(solution)/shard_map/ppermute | solution.py:54
  26.6 3.9 %collective-permute-start.5 = (f32[7,4,192]{2,1,0:T(4,128)S(1)}, f32[7,4,192]{2,1,0:T(4,128)S(1)}, u32[]{:S(2)}, u32[]{:S(2)}) collective-permute-start(f32[7,4,192]{2,1,0:T(4,128)S(1)} %add_add_fusion.2), channel_id=1, source_target_pairs={{0,4},{2,6},{4,0},{6,2},{8,12},{10,14},{12,8},{14,10},{16,20},{18,... | collective-permute-start | bytes 64520 | tf_op jit(solution)/shard_map/ppermute | solution.py:54
  30.5 3.9 %collective-permute-start.6 = (f32[7,4,192]{2,1,0:T(4,128)S(1)}, f32[7,4,192]{2,1,0:T(4,128)S(1)}, u32[]{:S(2)}, u32[]{:S(2)}) collective-permute-start(f32[7,4,192]{2,1,0:T(4,128)S(1)} %add_add_fusion.1), channel_id=1, source_target_pairs={{0,8},{2,10},{4,12},{6,14},{8,0},{10,2},{12,4},{14,6},{16,24},{18,... | collective-permute-start | bytes 64520 | tf_op jit(solution)/shard_map/ppermute | solution.py:54
  34.5 4.9 %collective-permute-start.7 = (f32[7,4,192]{2,1,0:T(4,128)S(1)}, f32[7,4,192]{2,1,0:T(4,128)S(1)}, u32[]{:S(2)}, u32[]{:S(2)}) collective-permute-start(f32[7,4,192]{2,1,0:T(4,128)S(1)} %add_add_fusion), channel_id=1, source_target_pairs={{0,16},{2,18},{4,20},{6,22},{8,24},{10,26},{12,28},{14,30},{16,0},... | collective-permute-start | bytes 64520 | tf_op jit(solution)/shard_map/ppermute | solution.py:54

commit v5 on v4

--- a/solution.py
+++ b/solution.py
@@ -117,6 +117,31 @@
 
     def take(self, token, repeat, count):
         return self.ref[(*self.lead, self.strided(token, repeat, count), slice(None))]
+
+
+def held_tokens(reach):
+    wide = 2 * reach
+    return (
+        (0, CHUNK, reach),
+        (0, reach, wide),
+        (0, reach, wide),
+        (0, CHUNK, 0),
+        (0, 0, reach),
+        (0, 0, reach),
+        (reach, CHUNK, reach),
+        (0, 0, reach),
+    )
+
+
+class Held:
+    def __init__(self, ref, repeats, column, span):
+        self.first, self.last, self.tail = span
+        self.view = Tokens(ref, repeats, 0, (column,))
+
+    def __getitem__(self, token):
+        if token < 0:
+            return self.view[self.last - self.first + self.tail + token]
+        return self.view[token - self.first]
 
 
 class Window:
@@ -236,27 +261,23 @@
     taps,
     repeats,
     features_ref,
-    cotangent_ref,
+    cotangent_hbm,
     weights_ref,
     mixed_ref,
     gq_ref,
     gk_ref,
     gv_ref,
-    q_s,
-    k_s,
-    v_s,
-    c_s,
-    kc_s,
-    vc_s,
-    p_s,
-    gm_s,
-    sums_ref,
-    m_s,
+    *refs,
 ):
+    *held_refs, sums_ref = refs[:9]
+    *work_refs, m_s, cotangent_ref, sem = refs[9:]
+    q_s, k_s, v_s, c_s, kc_s, vc_s, p_s, gm_s = work_refs
     reach = taps - 1
     groups = weights_ref.shape[2]
     length = cotangent_ref.shape[0]
     count = length // CHUNK
+    fetch = pltpu.make_async_copy(cotangent_hbm, cotangent_ref, sem)
+    fetch.start()
     sums_ref[...] = jnp.zeros_like(sums_ref)
     m_t = Tokens(m_s, repeats)
 
@@ -266,23 +287,21 @@
             Tokens(ref, repeats, 0, (column,)) for ref in (gq_ref, gk_ref, gv_ref)
         )
         q_t, k_t, v_t, c_t, kc_t, vc_t, p_t, gm_t = (
-            Tokens(ref, repeats, PAD, (column,))
-            for ref in (q_s, k_s, v_s, c_s, kc_s, vc_s, p_s, gm_s)
+            Tokens(ref, repeats, PAD) for ref in work_refs
         )
         zero = jnp.zeros((reach * repeats, LANES), F32)
         for ref in (q_s, k_s, v_s, p_s):
-            ref[column, (PAD - reach) * repeats : PAD * repeats, :] = zero
-        gm_s[column, gm_t.rows(length, reach), :] = zero
+            ref[(PAD - reach) * repeats : PAD * repeats, :] = zero
+        gm_s[gm_t.rows(length, reach), :] = zero
         wq, wk, wv, wm = (weight_rows(weights_ref, bank, lanes) for bank in range(4))
 
-        def forward(step, carry):
+        def products(step, carry):
             base = pl.multiple_of(step * CHUNK, CHUNK)
             rows = pl.ds(base, CHUNK)
             for repeat in range(repeats):
                 part = part_slice(repeat, groups, column)
-                for bank, view in enumerate((q_t, k_t, v_t)):
-                    view.put(base, repeat, features_ref[bank, rows, part].astype(F32))
-                c_t.put(base, repeat, cotangent_ref[rows, part].astype(F32))
+                k_t.put(base, repeat, features_ref[1, rows, part].astype(F32))
+                v_t.put(base, repeat, features_ref[2, rows, part].astype(F32))
             k_w, v_w = (Window(lambda t, view=view: view[base + t]) for view in (k_t, v_t))
             for token in range(CHUNK):
                 kc = dot_taps(wk, k_w.back(token, taps))
@@ -290,14 +309,23 @@
                 kc_t[base + token] = kc
                 vc_t[base + token] = vc
                 p_t[base + token] = kc * vc
+            return carry
+
+        def forward(step, carry):
+            base = pl.multiple_of(step * CHUNK, CHUNK)
+            rows = pl.ds(base, CHUNK)
+            for repeat in range(repeats):
+                part = part_slice(repeat, groups, column)
+                q_t.put(base, repeat, features_ref[0, rows, part].astype(F32))
+                c_t.put(base, repeat, cotangent_ref[rows, part].astype(F32))
             sums = Sums(taps)
             q_w, p_w = (Window(lambda t, view=view: view[base + t]) for view in (q_t, p_t))
             for token in range(CHUNK):
                 up = c_t[base + token]
                 sources = q_w.back(token, taps)
-                products = p_w.back(token, taps)
+                inner = p_w.back(token, taps)
                 qc = dot_taps(wq, sources)
-                mixer = dot_taps(wm, products)
+                mixer = dot_taps(wm, inner)
                 gq = up * mixer
                 gm = up * qc
                 m_t[token] = qc * mixer
@@ -307,7 +335,7 @@
                     gq = jnp.where(step > 0, gq, 0.0)
                     gm = jnp.where(step > 0, gm, 0.0)
                 sums.add(0, gq, sources)
-                sums.add(3, gm, products)
+                sums.add(3, gm, inner)
             sums.store(sums_ref, lanes)
             for repeat in range(repeats):
                 part = part_slice(repeat, groups, column)
@@ -335,8 +363,19 @@
             sums.store(sums_ref, lanes)
             return carry
 
+        lax.fori_loop(0, count, products, 0)
+
+        @pl.when(column == 0)
+        def _():
+            fetch.wait()
+
         lax.fori_loop(0, count, forward, 0)
         lax.fori_loop(0, count, backward, 0)
+        for ref, work, (first, last, tail) in zip(held_refs, work_refs, held_tokens(reach)):
+            for token in (*range(first, last), *range(length - tail, length)):
+                row = token - first if token < last else token - length + last - first + tail
+                target = Tokens(ref, repeats, 0, (column,))
+                target[row] = Tokens(work, repeats, PAD)[token]
         return carry
 
     lax.fori_loop(0, groups // LANES, column_step, 0)
@@ -349,24 +388,33 @@
     columns = groups // LANES
     work = length * channels * taps * 2
     grad = jax.ShapeDtypeStruct((columns, length * repeats, LANES), F32)
-    held = jax.ShapeDtypeStruct((columns, (length + 2 * PAD) * repeats, LANES), F32)
+    held = [
+        jax.ShapeDtypeStruct((columns, (last - first + tail) * repeats, LANES), F32)
+        for first, last, tail in held_tokens(taps - 1)
+    ]
+    work_shape = ((length + 2 * PAD) * repeats, LANES)
     mixed, gq, gk, gv, *arrays, sums = pl.pallas_call(
         functools.partial(interior_kernel, taps, repeats),
         out_shape=(
             jax.ShapeDtypeStruct(cotangent.shape, cotangent.dtype),
             *[grad] * 3,
-            *[held] * 8,
+            *held,
             jax.ShapeDtypeStruct((banks, taps, repeats, groups), F32),
         ),
-        in_specs=[VMEM_SPEC] * 3,
+        in_specs=[VMEM_SPEC, pl.BlockSpec(memory_space=pltpu.HBM), VMEM_SPEC],
         out_specs=(VMEM_SPEC,) * 13,
-        scratch_shapes=[pltpu.VMEM((CHUNK * repeats, LANES), F32)],
+        scratch_shapes=[pltpu.VMEM(work_shape, F32) for _ in range(8)]
+        + [
+            pltpu.VMEM((CHUNK * repeats, LANES), F32),
+            pltpu.VMEM(cotangent.shape, cotangent.dtype),
+            pltpu.SemaphoreType.DMA,
+        ],
         cost_estimate=pl.CostEstimate(
             flops=9 * work, bytes_accessed=22 * length * channels, transcendentals=0
         ),
         compiler_params=pltpu.CompilerParams(vmem_limit_bytes=VMEM_LIMIT),
         name="interior",
-    )(features, cotangent, weights)
+    )(features, pltpu.with_memory_space_constraint(cotangent, pltpu.HBM), weights)
     return mixed, (gq, gk, gv), arrays, sums
 
 
@@ -407,7 +455,6 @@
 ):
     reach = taps - 1
     groups = weights_ref.shape[2]
-    length = q_a.shape[1] // repeats - 2 * PAD
     acc[...] = sums_in_ref[...]
     even = is_even("ctx")
     h_t, m_t = Tokens(h_s, repeats), Tokens(m_s, repeats)
@@ -417,8 +464,10 @@
         lanes = lane_slice(column)
         wq, wk, wv, wm = (weight_rows(weights_ref, bank, lanes) for bank in range(4))
         q_t, k_t, v_t, c_t, kc_i, vc_i, p_i, gm_i = (
-            Tokens(ref, repeats, PAD, (column,))
-            for ref in (q_a, k_a, v_a, c_a, kc_a, vc_a, p_a, gm_a)
+            Held(ref, repeats, column, span)
+            for ref, span in zip(
+                (q_a, k_a, v_a, c_a, kc_a, vc_a, p_a, gm_a), held_tokens(reach)
+            )
         )
         sums = Sums(taps)
 
@@ -474,16 +523,16 @@
             mixed_ref[:, part] = m_t.take(0, repeat, CHUNK).astype(mixed_ref.dtype)
 
         stage_halo(after, n_s, h_t, repeats, groups, column, 6 * reach)
-        q_w = Window(lambda t: q_t[length + t] if t < 0 else h_t[t])
+        q_w = Window(lambda t: q_t[t] if t < 0 else h_t[t])
         gk_o, gv_o = (Tokens(gtail_ref, repeats, reach, (bank, column)) for bank in range(2))
         for token in range(reach):
             gm_t[token] = h_t[2 * reach + token] * dot_taps(wq, q_w.back(token, taps))
-        gm_w = Window(lambda t: gm_i[length + t] if t < 0 else gm_t[t])
-        k_w, v_w = (Window(lambda t, view=view: view[length + t]) for view in (k_t, v_t))
+        gm_w = Window(lambda t: gm_i[t] if t < 0 else gm_t[t])
+        k_w, v_w = (Window(lambda t, view=view: view[t]) for view in (k_t, v_t))
         for token in range(-reach, 0):
             gp = dot_taps(wm, gm_w.ahead(token, taps))
-            gk = gp * vc_i[length + token]
-            gv = gp * kc_i[length + token]
+            gk = gp * vc_i[token]
+            gv = gp * kc_i[token]
             gk_o[token] = gk
             gv_o[token] = gv
             sums.add(1, gk, k_w.back(token, taps))
@@ -578,7 +627,8 @@
         wq, wk, wv, wm = (weight_rows(weights_ref, bank, lanes) for bank in range(4))
         h_t, p_t, gm_t = (Tokens(ref, repeats) for ref in (h_s, p_s, gm_s))
         q_t, k_t, v_t, p_i = (
-            Tokens(ref, repeats, PAD + length, (column,)) for ref in ahead_of
+            Held(ref, repeats, column, held_tokens(reach)[which])
+            for ref, which in zip(ahead_of, (0, 1, 2, 6))
         )
         stage_halo(lambda part: after_ref[:, part], n_s, h_t, repeats, groups, column, 6 * reach)
         q_w = Window(lambda t: q_t[t] if t < 0 else h_t[t])

time: 40.2 us -> 38.2 us (0.950)
  Pallas kernels: 20.4 us -> 18.6 us
    pallas_call x1, Pallas kernels: 2.12 us -> 1.2 us  [edge(): pl.pallas_call(functools.partial(edge_kernel, taps, repeats), out_shape=(...]
    pallas_call x1, Pallas kernels: 2.49 us -> 1.72 us  [pack(): pl.pallas_call(functools.partial(pack_kernel, reach), out_shape=(message,...]
    ppermute x1, starting transfers between devices: 1.35 us -> 0.66 us  [swap_pairs(): far = lax.ppermute(far, axis, outer)]
    ppermute x1, waiting for transfers between devices: 0.4 us -> 0.86 us  [swap_pairs(): near = lax.ppermute(near, axis, inner)]
  transfers between devices with their start and end apart: 8 -> 8, of which waited for: 5 -> 5; matrix products, arithmetic and copies ran while one was open for 0% -> 0% of each run, Pallas kernels for 39% -> 41%
where the time goes in v5:
time: 38.2 us; the launch traced here: 38 us
  Pallas kernels  18.6 us (49%)
  starting transfers between devices  13.9 us (36%)
  waiting for transfers between devices  3.79 us (10%)
  other arithmetic  0.92 us (2%)
  between operations  0.77 us (2%)
    ppermute x4, starting transfers between devices, sum_over(): received = lax.ppermute(value, axis, pairs)  10.1 us
    pallas_call x1, Pallas kernels, interior(): pl.pallas_call(functools.partial(interior_kernel, taps, repeats), out_sha...  9.42 us
    pallas_call x4, Pallas kernels, feature_gradients(): pl.pallas_call(functools.partial(grads_kernel, taps, repeats, first, step...  6.3 us
    ppermute x1, starting transfers between devices, swap_pairs(): near = lax.ppermute(near, axis, inner)  2.56 us
    ppermute x4, waiting for transfers between devices, sum_over(): received = lax.ppermute(value, axis, pairs)  1.73 us
    pallas_call x1, Pallas kernels, pack(): pl.pallas_call(functools.partial(pack_kernel, reach), out_shape=(message,...  1.72 us
    pallas_call x1, Pallas kernels, edge(): pl.pallas_call(functools.partial(edge_kernel, taps, repeats), out_shape=(...  1.2 us
    ppermute x1, waiting for transfers between devices, sum_scatter(): sent = lax.ppermute(jnp.where(first, high, low), axis, [(0, 1), (1, 0)])  1.19 us
  transfers between devices with their start and end apart: 8, of which 5 were waited for; matrix products, arithmetic and copies ran while one was open for 0% of the time, Pallas kernels for 41%

profile of v5, /device:TPU:0, one launch (start us, length us, event | category | flops | bytes accessed | tf_op | source)
XLA Modules:
  0.0 38.0 jit_solution(14879988063329807875)
XLA Ops:
  0.6 0.0 copy-start
  0.6 1.7 %pack_halos.1 = (bf16[36,3072]{1,0:T(8,128)(2,1)S(1)}, bf16[36,3072]{1,0:T(8,128)(2,1)S(1)}, bf16[7,4,192]{2,1,0:T(4,128)(2,1)S(1)}) custom-call(bf16[3,128,3072]{2,1,0:T(8,128)(2,1)} %features_ref.1, bf16[128,3072]{1,0:T(8,128)(2,1)} %cotangent_hbm.3, f32[7,4,192]{2,1,0:T(4,128)} %bitcast.3), custom_call_target="tpu_custom_call" | custom-call | flops 1000000 | bytes 1000000 | tf_op jit(solution)/shard_map/pack_halos/pallas_call | solution.py:240
  2.4 0.5 %collective-permute-start = (bf16[7,4,192]{2,1,0:T(4,128)(2,1)S(1)}, bf16[7,4,192]{2,1,0:T(4,128)(2,1)S(1)}, u32[]{:S(2)}, u32[]{:S(2)}) collective-permute-start(bf16[7,4,192]{2,1,0:T(4,128)(2,1)S(1)} %get-tuple-element.33), channel_id=1, source_target_pairs={{0,1},{1,0},{2,3},{3,2},{4,5},{5,4},{6,7},{7,6},{8,9},{9,8},{10,11... | collective-permute-start | bytes 32264 | tf_op jit(solution)/shard_map/ppermute | solution.py:40
  2.9 2.6 %collective-permute-start.1 = (bf16[36,3072]{1,0:T(8,128)(2,1)S(1)}, bf16[36,3072]{1,0:T(8,128)(2,1)S(1)}, u32[]{:S(2)}, u32[]{:S(2)}) collective-permute-start(bf16[36,3072]{1,0:T(8,128)(2,1)S(1)} %get-tuple-element.37), channel_id=1, source_target_pairs={{0,2},{2,0},{4,6},{6,4},{8,10},{10,8},{12,14},{14,12},{16,18},{18,... | collective-permute-start | bytes 663560 | tf_op jit(solution)/shard_map/ppermute | solution.py:28
  5.5 0.7 %collective-permute-start.2 = (bf16[36,3072]{1,0:T(8,128)(2,1)S(1)}, bf16[36,3072]{1,0:T(8,128)(2,1)S(1)}, u32[]{:S(2)}, u32[]{:S(2)}) collective-permute-start(bf16[36,3072]{1,0:T(8,128)(2,1)S(1)} %get-tuple-element.38), channel_id=1, source_target_pairs={{2,4},{4,2},{6,8},{8,6},{10,12},{12,10},{14,16},{16,14},{18,20},{2... | collective-permute-start | bytes 663560 | tf_op jit(solution)/shard_map/ppermute | solution.py:27
  6.1 0.0 collective-permute-done
  6.2 0.1 maximum_convert_fusion.weights_ref.refs_0_
  6.2 0.0 copy-done
  6.3 9.4 %interior.1 = (bf16[128,3072]{1,0:T(8,128)(2,1)S(1)}, f32[3,1024,128]{2,1,0:T(8,128)S(1)}, f32[3,1024,128]{2,1,0:T(8,128)S(1)}, f32[3,1024,128]{2,1,0:T(8,128)S(...) custom-call(bf16[3,128,3072]{2,1,0:T(8,128)(2,1)S(1)} %copy-done, ...), custom_call_target="tpu_custom_call" | custom-call | flops 49545216 | bytes 8650752 | tf_op jit(solution)/shard_map/interior/pallas_call | solution.py:396
  15.7 0.9 %collective-permute-done.1.near_ref = bf16[36,3072]{1,0:T(8,128)(2,1)S(1)} collective-permute-done((bf16[36,3072]{1,0:T(8,128)(2,1)S(1)}, bf16[36,3072]{1,0:T(8,128)(2,1)S(1)}, u32[]{:S(2)}, u32[]{:S(2)}) %collective-permute-start.1) | collective-permute-done | bytes 221216 | tf_op jit(solution)/shard_map/ppermute | solution.py:28
  16.5 0.0 collective-permute-done.2.far_ref
  16.5 1.2 %edge.1 = (bf16[16,3072]{1,0:T(8,128)(2,1)S(1)}, f32[3,3,96,128]{3,2,1,0:T(8,128)S(1)}, f32[2,3,48,128]{3,2,1,0:T(8,128)S(1)}, bf16[36,3072]{1,0:T(8,128)(2,1)S(1)}, f32[7,4,384]{2,1,0:T(4,128)S(1)}) custom-call(f32[7,4,384]{2,1,0:T(4,128)S(1)} %maximum_convert_fusion.weights_ref.refs_0_, bf16[36,3072]{1,0:T(8,128)(2,1)S(1)} %collective-permute-done.1.near_ref, ...), custom_call_target="tpu_custom_call" | custom-call | flops 10000000 | bytes 4000000 | tf_op jit(solution)/shard_map/edge/pallas_call | solution.py:555
  17.7 0.1 slice_select_fusion
  17.8 0.1 collective-permute-start.3
  17.9 1.2 %collective-permute-done.3 = f32[7,4,192]{2,1,0:T(4,128)S(1)} collective-permute-done((f32[7,4,192]{2,1,0:T(4,128)S(1)}, f32[7,4,192]{2,1,0:T(4,128)S(1)}, u32[]{:S(2)}, u32[]{:S(2)}) %collective-permute-start.3) | collective-permute-done | bytes 21536 | tf_op jit(solution)/shard_map/ppermute | solution.py:71
  19.1 0.1 select_add_fusion
  19.2 3.5 %collective-permute-start.4 = (f32[7,4,192]{2,1,0:T(4,128)S(1)}, f32[7,4,192]{2,1,0:T(4,128)S(1)}, u32[]{:S(2)}, u32[]{:S(2)}) collective-permute-start(f32[7,4,192]{2,1,0:T(4,128)S(1)} %select_add_fusion), channel_id=1, source_target_pairs={{0,2},{2,0},{4,6},{6,4},{8,10},{10,8},{12,14},{14,12},{16,18},{18,... | collective-permute-start | bytes 64520 | tf_op jit(solution)/shard_map/ppermute | solution.py:54
  22.7 1.5 %feature_gradients.4 = (bf16[3,128,3072]{2,1,0:T(8,128)(2,1)}, f32[7,4,192]{2,1,0:T(4,128)S(1)}, bf16[128,3072]{1,0:T(8,128)(2,1)}) custom-call(f32[7,4,384]{2,1,0:T(4,128)S(1)} %maximum_convert_fusion.weights_ref.refs_0_, f32[3,1024,128]{2,1,0:T(8,128)S(1)} %get-tuple-element.34.refs_1_, f32[3,1024,128]{2,1,0:T(8,128)S(1)} %get-tuple-element.35.refs_2_, ...), custom_call_target="tpu_custom_call" | custom-call | flops 5505024 | bytes 1769472 | tf_op jit(solution)/shard_map/feature_gradients/pallas_call | solution.py:723
  24.2 0.4 collective-permute-done.4
  24.6 1.5 %collective-permute-start.5 = (f32[7,4,192]{2,1,0:T(4,128)S(1)}, f32[7,4,192]{2,1,0:T(4,128)S(1)}, u32[]{:S(2)}, u32[]{:S(2)}) collective-permute-start(f32[7,4,192]{2,1,0:T(4,128)S(1)} %add_add_fusion.2), channel_id=1, source_target_pairs={{0,4},{2,6},{4,0},{6,2},{8,12},{10,14},{12,8},{14,10},{16,20},{18,... | collective-permute-start | bytes 64520 | tf_op jit(solution)/shard_map/ppermute | solution.py:54
  26.1 1.5 %feature_gradients.5 = (bf16[3,128,3072]{2,1,0:T(8,128)(2,1)}, f32[7,4,192]{2,1,0:T(4,128)S(1)}) custom-call(f32[7,4,384]{2,1,0:T(4,128)S(1)} %maximum_convert_fusion.weights_ref.refs_0_, f32[3,1024,128]{2,1,0:T(8,128)S(1)} %get-tuple-element.34.refs_1_, f32[3,1024,128]{2,1,0:T(8,128)S(1)} %get-tuple-element.35.refs_2_, ...), custom_call_target="tpu_custom_call", output_to_operand_aliasing={{0}: (6, {})} | custom-call | flops 5505024 | bytes 1769472 | tf_op jit(solution)/shard_map/feature_gradients/pallas_call | solution.py:723
  27.6 0.9 %collective-permute-done.5 = f32[7,4,192]{2,1,0:T(4,128)S(1)} collective-permute-done((f32[7,4,192]{2,1,0:T(4,128)S(1)}, f32[7,4,192]{2,1,0:T(4,128)S(1)}, u32[]{:S(2)}, u32[]{:S(2)}) %collective-permute-start.5) | collective-permute-done | bytes 21536 | tf_op jit(solution)/shard_map/ppermute | solution.py:54
  28.5 2.0 %collective-permute-start.6 = (f32[7,4,192]{2,1,0:T(4,128)S(1)}, f32[7,4,192]{2,1,0:T(4,128)S(1)}, u32[]{:S(2)}, u32[]{:S(2)}) collective-permute-start(f32[7,4,192]{2,1,0:T(4,128)S(1)} %add_add_fusion.1), channel_id=1, source_target_pairs={{0,8},{2,10},{4,12},{6,14},{8,0},{10,2},{12,4},{14,6},{16,24},{18,... | collective-permute-start | bytes 64520 | tf_op jit(solution)/shard_map/ppermute | solution.py:54
  30.5 1.5 %feature_gradients.6 = (bf16[3,128,3072]{2,1,0:T(8,128)(2,1)}, f32[7,4,192]{2,1,0:T(4,128)S(1)}) custom-call(f32[7,4,384]{2,1,0:T(4,128)S(1)} %maximum_convert_fusion.weights_ref.refs_0_, f32[3,1024,128]{2,1,0:T(8,128)S(1)} %get-tuple-element.34.refs_1_, f32[3,1024,128]{2,1,0:T(8,128)S(1)} %get-tuple-element.35.refs_2_, ...), custom_call_target="tpu_custom_call", output_to_operand_aliasing={{0}: (6, {})} | custom-call | flops 5505024 | bytes 1769472 | tf_op jit(solution)/shard_map/feature_gradients/pallas_call | solution.py:723
  32.0 0.4 %collective-permute-done.6 = f32[7,4,192]{2,1,0:T(4,128)S(1)} collective-permute-done((f32[7,4,192]{2,1,0:T(4,128)S(1)}, f32[7,4,192]{2,1,0:T(4,128)S(1)}, u32[]{:S(2)}, u32[]{:S(2)}) %collective-permute-start.6) | collective-permute-done | bytes 21536 | tf_op jit(solution)/shard_map/ppermute | solution.py:54
  32.5 3.1 %collective-permute-start.7 = (f32[7,4,192]{2,1,0:T(4,128)S(1)}, f32[7,4,192]{2,1,0:T(4,128)S(1)}, u32[]{:S(2)}, u32[]{:S(2)}) collective-permute-start(f32[7,4,192]{2,1,0:T(4,128)S(1)} %add_add_fusion), channel_id=1, source_target_pairs={{0,16},{2,18},{4,20},{6,22},{8,24},{10,26},{12,28},{14,30},{16,0},... | collective-permute-start | bytes 64520 | tf_op jit(solution)/shard_map/ppermute | solution.py:54
  35.5 1.9 %feature_gradients.7 = (bf16[3,128,3072]{2,1,0:T(8,128)(2,1)}, f32[7,4,192]{2,1,0:T(4,128)S(1)}) custom-call(f32[7,4,384]{2,1,0:T(4,128)S(1)} %maximum_convert_fusion.weights_ref.refs_0_, f32[3,1024,128]{2,1,0:T(8,128)S(1)} %get-tuple-element.34.refs_1_, f32[3,1024,128]{2,1,0:T(8,128)S(1)} %get-tuple-element.35.refs_2_, ...), custom_call_target="tpu_custom_call", output_to_operand_aliasing={{0}: (6, {})} | custom-call | flops 5505024 | bytes 1769472 | tf_op jit(solution)/shard_map/feature_gradients/pallas_call | solution.py:723
  37.4 0.0 collective-permute-done.7
  37.4 0.6 %multiply_bitcast_fusion = f32[4,7,192]{2,0,1:T(4,128)} fusion(f32[7,4,192]{2,1,0:T(4,128)S(1)} %get-tuple-element.62, f32[7,4,192]{2,1,0:T(4,128)S(1)} %add_add_fusion, f32[7,4,192]{2,1,0:T(4,128)S(1)} %collective-permute-done.7), kind=kLoop, calls=%fused_computation | loop fusion | flops 16128 | bytes 86016 | tf_op jit(solution)/shard_map/transpose | solution.py:782
  (4 shorter events, 0.1 us)
Async XLA Ops:
  0.6 5.6 %copy-start = (bf16[3,128,3072]{2,1,0:T(8,128)(2,1)S(1)}, bf16[3,128,3072]{2,1,0:T(8,128)(2,1)}, u32[]{:S(2)}) copy-start(bf16[3,128,3072]{2,1,0:T(8,128)(2,1)} %features_ref.1) | copy-start | bytes 7077892
  2.4 3.8 %collective-permute-start = (bf16[7,4,192]{2,1,0:T(4,128)(2,1)S(1)}, bf16[7,4,192]{2,1,0:T(4,128)(2,1)S(1)}, u32[]{:S(2)}, u32[]{:S(2)}) collective-permute-start(bf16[7,4,192]{2,1,0:T(4,128)(2,1)S(1)} %get-tuple-element.33), channel_id=1, source_target_pairs={{0,1},{1,0},{2,3},{3,2},{4,5},{5,4},{6,7},{7,6},{8,9},{9,8},{10,11... | collective-permute-start | bytes 32264 | tf_op jit(solution)/shard_map/ppermute | solution.py:40
  2.9 13.7 %collective-permute-start.1 = (bf16[36,3072]{1,0:T(8,128)(2,1)S(1)}, bf16[36,3072]{1,0:T(8,128)(2,1)S(1)}, u32[]{:S(2)}, u32[]{:S(2)}) collective-permute-start(bf16[36,3072]{1,0:T(8,128)(2,1)S(1)} %get-tuple-element.37), channel_id=1, source_target_pairs={{0,2},{2,0},{4,6},{6,4},{8,10},{10,8},{12,14},{14,12},{16,18},{18,... | collective-permute-start | bytes 663560 | tf_op jit(solution)/shard_map/ppermute | solution.py:28
  5.5 11.1 %collective-permute-start.2 = (bf16[36,3072]{1,0:T(8,128)(2,1)S(1)}, bf16[36,3072]{1,0:T(8,128)(2,1)S(1)}, u32[]{:S(2)}, u32[]{:S(2)}) collective-permute-start(bf16[36,3072]{1,0:T(8,128)(2,1)S(1)} %get-tuple-element.38), channel_id=1, source_target_pairs={{2,4},{4,2},{6,8},{8,6},{10,12},{12,10},{14,16},{16,14},{18,20},{2... | collective-permute-start | bytes 663560 | tf_op jit(solution)/shard_map/ppermute | solution.py:27
  17.8 1.3 %collective-permute-start.3 = (f32[7,4,192]{2,1,0:T(4,128)S(1)}, f32[7,4,192]{2,1,0:T(4,128)S(1)}, u32[]{:S(2)}, u32[]{:S(2)}) collective-permute-start(f32[7,4,192]{2,1,0:T(4,128)S(1)} %slice_select_fusion), channel_id=1, source_target_pairs={{0,1},{1,0},{2,3},{3,2},{4,5},{5,4},{6,7},{7,6},{8,9},{9,8},{10,11... | collective-permute-start | bytes 64520 | tf_op jit(solution)/shard_map/ppermute | solution.py:71
  19.2 5.3 %collective-permute-start.4 = (f32[7,4,192]{2,1,0:T(4,128)S(1)}, f32[7,4,192]{2,1,0:T(4,128)S(1)}, u32[]{:S(2)}, u32[]{:S(2)}) collective-permute-start(f32[7,4,192]{2,1,0:T(4,128)S(1)} %select_add_fusion), channel_id=1, source_target_pairs={{0,2},{2,0},{4,6},{6,4},{8,10},{10,8},{12,14},{14,12},{16,18},{18,... | collective-permute-start | bytes 64520 | tf_op jit(solution)/shard_map/ppermute | solution.py:54
  24.6 3.9 %collective-permute-start.5 = (f32[7,4,192]{2,1,0:T(4,128)S(1)}, f32[7,4,192]{2,1,0:T(4,128)S(1)}, u32[]{:S(2)}, u32[]{:S(2)}) collective-permute-start(f32[7,4,192]{2,1,0:T(4,128)S(1)} %add_add_fusion.2), channel_id=1, source_target_pairs={{0,4},{2,6},{4,0},{6,2},{8,12},{10,14},{12,8},{14,10},{16,20},{18,... | collective-permute-start | bytes 64520 | tf_op jit(solution)/shard_map/ppermute | solution.py:54
  28.5 3.9 %collective-permute-start.6 = (f32[7,4,192]{2,1,0:T(4,128)S(1)}, f32[7,4,192]{2,1,0:T(4,128)S(1)}, u32[]{:S(2)}, u32[]{:S(2)}) collective-permute-start(f32[7,4,192]{2,1,0:T(4,128)S(1)} %add_add_fusion.1), channel_id=1, source_target_pairs={{0,8},{2,10},{4,12},{6,14},{8,0},{10,2},{12,4},{14,6},{16,24},{18,... | collective-permute-start | bytes 64520 | tf_op jit(solution)/shard_map/ppermute | solution.py:54
  32.5 4.9 %collective-permute-start.7 = (f32[7,4,192]{2,1,0:T(4,128)S(1)}, f32[7,4,192]{2,1,0:T(4,128)S(1)}, u32[]{:S(2)}, u32[]{:S(2)}) collective-permute-start(f32[7,4,192]{2,1,0:T(4,128)S(1)} %add_add_fusion), channel_id=1, source_target_pairs={{0,16},{2,18},{4,20},{6,22},{8,24},{10,26},{12,28},{14,30},{16,0},... | collective-permute-start | bytes 64520 | tf_op jit(solution)/shard_map/ppermute | solution.py:54

commit v6 on v5

--- a/solution.py
+++ b/solution.py
@@ -119,6 +119,26 @@
         return self.ref[(*self.lead, self.strided(token, repeat, count), slice(None))]
 
 
+class Halo:
+    def __init__(self, ref, repeats, columns):
+        self.ref, self.repeats, self.columns = ref, repeats, columns
+
+    def put(self, token, column, repeat, value):
+        start = (token * self.columns + column) * self.repeats + repeat
+        rows = pl.ds(start, value.shape[0], stride=self.columns * self.repeats)
+        self.ref[rows, :] = value
+
+    def tokens(self, column):
+        class View:
+            def __getitem__(_, token):
+                start = (token * self.columns + column) * self.repeats
+                if not isinstance(start, int):
+                    start = pl.multiple_of(start, self.repeats)
+                return self.ref[pl.ds(start, self.repeats), :]
+
+        return View()
+
+
 def held_tokens(reach):
     wide = 2 * reach
     return (
@@ -178,6 +198,7 @@
 
 def pack_kernel(
     reach,
+    columns,
     features_hbm,
     cotangent_hbm,
     master_hbm,
@@ -202,33 +223,39 @@
     for copy in copies:
         copy.start()
     even = is_even("ctx")
-    b_s[...] = jnp.zeros_like(b_s)
+    repeats = upstream.shape[1] // (columns * LANES)
+    block = reach * columns * repeats
+    b_s[-block:, :] = jnp.zeros((block, LANES), F32)
+    last, first = Halo(b_s, repeats, columns), Halo(a_s, repeats, columns)
     for copy in copies:
         copy.wait()
     rounded_ref[...] = master[...].astype(rounded_ref.dtype)
-
-    def column(index, carry):
-        lanes = lane_slice(index)
-
-        def rows(ref, bank, start, stop):
-            return ref[bank, :, lanes].astype(F32)[start:stop]
-
-        b_s[0:reach, :] = rows(tail, 0, PAD - reach, PAD)
-        b_s[reach : 3 * reach, :] = rows(tail, 1, PAD - 2 * reach, PAD)
-        b_s[3 * reach : 5 * reach, :] = rows(tail, 2, PAD - 2 * reach, PAD)
-        a_s[0 : 2 * reach, :] = rows(head, 0, 0, 2 * reach)
-        a_s[2 * reach : 4 * reach, :] = upstream[:, lanes].astype(F32)[: 2 * reach]
-        a_s[4 * reach : 5 * reach, :] = rows(head, 1, 0, reach)
-        a_s[5 * reach : 6 * reach, :] = rows(head, 2, 0, reach)
-        last, first = b_s[...], a_s[...]
-        near_ref[:, lanes] = jnp.where(even, last, first).astype(near_ref.dtype)
-        far_ref[:, lanes] = jnp.where(even, first, last).astype(far_ref.dtype)
+    wide = 2 * reach
+
+    def repeat_step(repeat, carry):
+        for column in range(columns):
+            lanes = lane_slice(repeat * columns + column)
+
+            def put(message, token, ref, start, stop):
+                value = ref[:, lanes].astype(F32)[start:stop]
+                message.put(token, column, repeat, value)
+
+            put(last, 0, tail.at[0], PAD - reach, PAD)
+            put(last, reach, tail.at[1], PAD - wide, PAD)
+            put(last, 3 * reach, tail.at[2], PAD - wide, PAD)
+            put(first, 0, head.at[0], 0, wide)
+            put(first, wide, upstream, 0, wide)
+            put(first, 2 * wide, head.at[1], 0, reach)
+            put(first, 5 * reach, head.at[2], 0, reach)
         return carry
 
-    lax.fori_loop(0, near_ref.shape[1] // LANES, column, 0)
-
-
-def pack(features, cotangent, master):
+    lax.fori_loop(0, repeats, repeat_step, 0)
+    ending, opening = b_s[...], a_s[...]
+    near_ref[...] = jnp.where(even, ending, opening).astype(near_ref.dtype)
+    far_ref[...] = jnp.where(even, opening, ending).astype(far_ref.dtype)
+
+
+def pack(features, cotangent, master, groups):
     reach = master.shape[0] - 1
     banks, length, channels = features.shape
     kind = features.dtype
@@ -236,9 +263,9 @@
         pltpu.with_memory_space_constraint(value, pltpu.HBM)
         for value in (features, cotangent, master)
     ]
-    message = jax.ShapeDtypeStruct((6 * reach, channels), kind)
+    message = jax.ShapeDtypeStruct((6 * reach * channels // LANES, LANES), kind)
     return pl.pallas_call(
-        functools.partial(pack_kernel, reach),
+        functools.partial(pack_kernel, reach, groups // LANES),
         out_shape=(message, message, jax.ShapeDtypeStruct(master.shape, jnp.bfloat16)),
         in_specs=[pl.BlockSpec(memory_space=pltpu.HBM)] * 3,
         out_specs=(VMEM_SPEC,) * 3,
@@ -247,8 +274,8 @@
             pltpu.VMEM((banks, PAD, channels), kind),
             pltpu.VMEM((PAD, channels), kind),
             pltpu.VMEM(master.shape, F32),
-            pltpu.VMEM((6 * reach, LANES), F32),
-            pltpu.VMEM((6 * reach, LANES), F32),
+            pltpu.VMEM(message.shape, F32),
+            pltpu.VMEM(message.shape, F32),
             pltpu.SemaphoreType.DMA((4,)),
         ],
         cost_estimate=pl.CostEstimate(flops=10**6, bytes_accessed=10**6, transcendentals=0),
@@ -271,7 +298,9 @@
 ):
     *held_refs, sums_ref = refs[:9]
     *work_refs, m_s, cotangent_ref, sem = refs[9:]
+    *work_refs, k_other, v_other = work_refs
     q_s, k_s, v_s, c_s, kc_s, vc_s, p_s, gm_s = work_refs
+    pairs = ((k_s, v_s), (k_other, v_other))
     reach = taps - 1
     groups = weights_ref.shape[2]
     length = cotangent_ref.shape[0]
@@ -281,27 +310,47 @@
     sums_ref[...] = jnp.zeros_like(sums_ref)
     m_t = Tokens(m_s, repeats)
 
-    def column_step(column, carry):
-        lanes = lane_slice(column)
+    def part_of(repeat, column):
+        first = repeat * groups + column * LANES
+        return slice(first, first + LANES)
+
+    zero = jnp.zeros((reach * repeats, LANES), F32)
+    for ref in (q_s, p_s, k_s, v_s, k_other, v_other):
+        ref[(PAD - reach) * repeats : PAD * repeats, :] = zero
+    gm_s[(PAD + length) * repeats : (PAD + length + reach) * repeats, :] = zero
+    q_t, c_t, kc_t, vc_t, p_t, gm_t = (
+        Tokens(ref, repeats, PAD) for ref in (q_s, c_s, kc_s, vc_s, p_s, gm_s)
+    )
+    columns = groups // LANES
+
+    def put_pair(column, base, rows):
+        for bank, ref in enumerate(pairs[column % 2]):
+            view = Tokens(ref, repeats, PAD)
+            for repeat in range(repeats):
+                part = part_of(repeat, column)
+                view.put(base, repeat, features_ref[1 + bank, rows, part].astype(F32))
+
+    def chunks(body):
+        def step_body(step, carry):
+            base = pl.multiple_of(step * CHUNK, CHUNK)
+            body(step, base, pl.ds(base, CHUNK))
+            return carry
+
+        lax.fori_loop(0, count, step_body, 0)
+
+    chunks(lambda step, base, rows: put_pair(0, base, rows))
+    for column in range(columns):
+        lanes = slice(column * LANES, (column + 1) * LANES)
         gq_t, gk_t, gv_t = (
             Tokens(ref, repeats, 0, (column,)) for ref in (gq_ref, gk_ref, gv_ref)
         )
-        q_t, k_t, v_t, c_t, kc_t, vc_t, p_t, gm_t = (
-            Tokens(ref, repeats, PAD) for ref in work_refs
-        )
-        zero = jnp.zeros((reach * repeats, LANES), F32)
-        for ref in (q_s, k_s, v_s, p_s):
-            ref[(PAD - reach) * repeats : PAD * repeats, :] = zero
-        gm_s[gm_t.rows(length, reach), :] = zero
+        k_t, v_t = (Tokens(ref, repeats, PAD) for ref in pairs[column % 2])
         wq, wk, wv, wm = (weight_rows(weights_ref, bank, lanes) for bank in range(4))
 
-        def products(step, carry):
-            base = pl.multiple_of(step * CHUNK, CHUNK)
-            rows = pl.ds(base, CHUNK)
+        def products(step, base, rows):
             for repeat in range(repeats):
-                part = part_slice(repeat, groups, column)
-                k_t.put(base, repeat, features_ref[1, rows, part].astype(F32))
-                v_t.put(base, repeat, features_ref[2, rows, part].astype(F32))
+                part = part_of(repeat, column)
+                q_t.put(base, repeat, features_ref[0, rows, part].astype(F32))
             k_w, v_w = (Window(lambda t, view=view: view[base + t]) for view in (k_t, v_t))
             for token in range(CHUNK):
                 kc = dot_taps(wk, k_w.back(token, taps))
@@ -309,15 +358,13 @@
                 kc_t[base + token] = kc
                 vc_t[base + token] = vc
                 p_t[base + token] = kc * vc
-            return carry
-
-        def forward(step, carry):
-            base = pl.multiple_of(step * CHUNK, CHUNK)
-            rows = pl.ds(base, CHUNK)
+
+        def forward(step, base, rows):
             for repeat in range(repeats):
-                part = part_slice(repeat, groups, column)
-                q_t.put(base, repeat, features_ref[0, rows, part].astype(F32))
+                part = part_of(repeat, column)
                 c_t.put(base, repeat, cotangent_ref[rows, part].astype(F32))
+            if column + 1 < columns:
+                put_pair(column + 1, base, rows)
             sums = Sums(taps)
             q_w, p_w = (Window(lambda t, view=view: view[base + t]) for view in (q_t, p_t))
             for token in range(CHUNK):
@@ -338,12 +385,10 @@
                 sums.add(3, gm, inner)
             sums.store(sums_ref, lanes)
             for repeat in range(repeats):
-                part = part_slice(repeat, groups, column)
+                part = part_of(repeat, column)
                 mixed_ref[rows, part] = m_t.take(0, repeat, CHUNK).astype(mixed_ref.dtype)
-            return carry
-
-        def backward(step, carry):
-            base = pl.multiple_of(step * CHUNK, CHUNK)
+
+        def backward(step, base, rows):
             k_w, v_w, gm_w = (
                 Window(lambda t, view=view: view[base + t]) for view in (k_t, v_t, gm_t)
             )
@@ -361,24 +406,18 @@
                 sums.add(1, gk, k_w.back(token, taps))
                 sums.add(2, gv, v_w.back(token, taps))
             sums.store(sums_ref, lanes)
-            return carry
-
-        lax.fori_loop(0, count, products, 0)
-
-        @pl.when(column == 0)
-        def _():
+
+        chunks(products)
+        if column == 0:
             fetch.wait()
-
-        lax.fori_loop(0, count, forward, 0)
-        lax.fori_loop(0, count, backward, 0)
-        for ref, work, (first, last, tail) in zip(held_refs, work_refs, held_tokens(reach)):
+        chunks(forward)
+        chunks(backward)
+        sources = (q_s, *pairs[column % 2], c_s, kc_s, vc_s, p_s, gm_s)
+        for ref, work, (first, last, tail) in zip(held_refs, sources, held_tokens(reach)):
+            target, source = Tokens(ref, repeats, 0, (column,)), Tokens(work, repeats, PAD)
             for token in (*range(first, last), *range(length - tail, length)):
                 row = token - first if token < last else token - length + last - first + tail
-                target = Tokens(ref, repeats, 0, (column,))
-                target[row] = Tokens(work, repeats, PAD)[token]
-        return carry
-
-    lax.fori_loop(0, groups // LANES, column_step, 0)
+                target[row] = source[token]
 
 
 def interior(features, cotangent, weights):
@@ -403,7 +442,7 @@
         ),
         in_specs=[VMEM_SPEC, pl.BlockSpec(memory_space=pltpu.HBM), VMEM_SPEC],
         out_specs=(VMEM_SPEC,) * 13,
-        scratch_shapes=[pltpu.VMEM(work_shape, F32) for _ in range(8)]
+        scratch_shapes=[pltpu.VMEM(work_shape, F32) for _ in range(10)]
         + [
             pltpu.VMEM((CHUNK * repeats, LANES), F32),
             pltpu.VMEM(cotangent.shape, cotangent.dtype),
@@ -416,12 +455,6 @@
         name="interior",
     )(features, pltpu.with_memory_space_constraint(cotangent, pltpu.HBM), weights)
     return mixed, (gq, gk, gv), arrays, sums
-
-
-def stage_halo(load, n_s, view, repeats, groups, column, rows):
-    for repeat in range(repeats):
-        n_s[0:rows, :] = load(part_slice(repeat, groups, column)).astype(F32)
-        view.put(0, repeat, n_s[...])
 
 
 def edge_kernel(
@@ -445,8 +478,7 @@
     after_ref,
     sums_ref,
     acc,
-    n_s,
-    h_s,
+    before_s,
     kc_s,
     vc_s,
     p_s,
@@ -457,7 +489,11 @@
     groups = weights_ref.shape[2]
     acc[...] = sums_in_ref[...]
     even = is_even("ctx")
-    h_t, m_t = Tokens(h_s, repeats), Tokens(m_s, repeats)
+    columns = groups // LANES
+    near, far = near_ref[...].astype(F32), far_ref[...].astype(F32)
+    before_s[...] = jnp.where(even, far, near)
+    after_ref[...] = jnp.where(even, near, far)
+    m_t = Tokens(m_s, repeats)
     kc_t, vc_t, p_t, gm_t = (Tokens(ref, repeats, PAD) for ref in (kc_s, vc_s, p_s, gm_s))
 
     def column_step(column, carry):
@@ -471,18 +507,7 @@
         )
         sums = Sums(taps)
 
-        def before(part):
-            rows = slice(0, 5 * reach)
-            return jnp.where(
-                even, far_ref[rows, part].astype(F32), near_ref[rows, part].astype(F32)
-            )
-
-        def after(part):
-            value = jnp.where(even, near_ref[:, part].astype(F32), far_ref[:, part].astype(F32))
-            after_ref[:, part] = value.astype(after_ref.dtype)
-            return value
-
-        stage_halo(before, n_s, h_t, repeats, groups, column, 5 * reach)
+        h_t = Halo(before_s, repeats, columns).tokens(column)
         q_w = Window(lambda t: q_t[t] if t >= 0 else h_t[reach + t])
         k_w = Window(lambda t: k_t[t] if t >= 0 else h_t[3 * reach + t])
         v_w = Window(lambda t: v_t[t] if t >= 0 else h_t[5 * reach + t])
@@ -522,11 +547,11 @@
             part = part_slice(repeat, groups, column)
             mixed_ref[:, part] = m_t.take(0, repeat, CHUNK).astype(mixed_ref.dtype)
 
-        stage_halo(after, n_s, h_t, repeats, groups, column, 6 * reach)
-        q_w = Window(lambda t: q_t[t] if t < 0 else h_t[t])
+        n_t = Halo(after_ref, repeats, columns).tokens(column)
+        q_w = Window(lambda t: q_t[t] if t < 0 else n_t[t])
         gk_o, gv_o = (Tokens(gtail_ref, repeats, reach, (bank, column)) for bank in range(2))
         for token in range(reach):
-            gm_t[token] = h_t[2 * reach + token] * dot_taps(wq, q_w.back(token, taps))
+            gm_t[token] = n_t[2 * reach + token] * dot_taps(wq, q_w.back(token, taps))
         gm_w = Window(lambda t: gm_i[t] if t < 0 else gm_t[t])
         k_w, v_w = (Window(lambda t, view=view: view[t]) for view in (k_t, v_t))
         for token in range(-reach, 0):
@@ -547,26 +572,24 @@
 
 def edge(weights, near, far, sums, arrays):
     taps, banks, groups = weights.shape
-    channels = near.shape[1]
-    repeats = channels // groups
     columns = groups // LANES
     reach = taps - 1
-    halo_rows = -(-6 * reach // 8) * 8
+    repeats = near.shape[0] // (6 * reach * columns)
+    channels = repeats * groups
     return pl.pallas_call(
         functools.partial(edge_kernel, taps, repeats),
         out_shape=(
             jax.ShapeDtypeStruct((CHUNK, channels), near.dtype),
             jax.ShapeDtypeStruct((3, columns, 2 * reach * repeats, LANES), F32),
             jax.ShapeDtypeStruct((2, columns, reach * repeats, LANES), F32),
-            jax.ShapeDtypeStruct(near.shape, near.dtype),
+            jax.ShapeDtypeStruct(near.shape, F32),
             jax.ShapeDtypeStruct((taps, banks, groups), F32),
         ),
         in_specs=[VMEM_SPEC] * 12,
         out_specs=(VMEM_SPEC,) * 5,
         scratch_shapes=[
             pltpu.VMEM(sums.shape, F32),
-            pltpu.VMEM((halo_rows, LANES), F32),
-            pltpu.VMEM((halo_rows * repeats, LANES), F32),
+            pltpu.VMEM(near.shape, F32),
         ]
         + [pltpu.VMEM((2 * PAD * repeats, LANES), F32) for _ in range(4)]
         + [pltpu.VMEM((CHUNK * repeats, LANES), F32)],
@@ -622,15 +645,15 @@
         return Tokens((gq, gk, gv)[bank], repeats, 0, (column,))[token]
 
     def next_shard(column, carry):
-        gnext, n_s, h_s, p_s, gm_s = refs[:5]
+        gnext, p_s, gm_s = refs[:3]
         lanes = lane_slice(column)
         wq, wk, wv, wm = (weight_rows(weights_ref, bank, lanes) for bank in range(4))
-        h_t, p_t, gm_t = (Tokens(ref, repeats) for ref in (h_s, p_s, gm_s))
+        p_t, gm_t = (Tokens(ref, repeats) for ref in (p_s, gm_s))
+        h_t = Halo(after_ref, repeats, columns).tokens(column)
         q_t, k_t, v_t, p_i = (
             Held(ref, repeats, column, held_tokens(reach)[which])
             for ref, which in zip(ahead_of, (0, 1, 2, 6))
         )
-        stage_halo(lambda part: after_ref[:, part], n_s, h_t, repeats, groups, column, 6 * reach)
         q_w = Window(lambda t: q_t[t] if t < 0 else h_t[t])
         k_w = Window(lambda t: k_t[t] if t < 0 else h_t[4 * reach + t])
         v_w = Window(lambda t: v_t[t] if t < 0 else h_t[5 * reach + t])
@@ -711,11 +734,8 @@
         q_a, k_a, v_a, _, _, _, p_a, _ = arrays
         operands += [after, q_a, k_a, v_a, p_a]
         in_specs += [VMEM_SPEC] * 5
-        halo_rows = -(-after.shape[0] // 8) * 8
         scratch = [
             pltpu.VMEM((3, columns, reach * repeats, LANES), F32),
-            pltpu.VMEM((halo_rows, LANES), F32),
-            pltpu.VMEM((halo_rows * repeats, LANES), F32),
             pltpu.VMEM((reach * repeats, LANES), F32),
             pltpu.VMEM((2 * reach * repeats, LANES), F32),
         ]
@@ -744,7 +764,12 @@
 
 def per_device(features, cotangent, master_filters):
     length = features.shape[1]
-    near, far, rounded = pack(features, cotangent, jnp.transpose(master_filters, (1, 0, 2)))
+    near, far, rounded = pack(
+        features,
+        cotangent,
+        jnp.transpose(master_filters, (1, 0, 2)),
+        master_filters.shape[2] * lax.axis_size("fsdp"),
+    )
     weights = gather_filters(rounded, "fsdp").astype(F32)
     halos = swap_pairs(near, far, "ctx")
     middle, grads, arrays, sums = interior(features, cotangent, weights)

time: 38.2 us -> 37.3 us (0.976)
  Pallas kernels: 18.6 us -> 17.6 us
  starting transfers between devices: 13.9 us -> 14.5 us
  waiting for transfers between devices: 3.79 us -> 3.27 us
    ppermute x4, starting transfers between devices: 10.1 us -> 10.7 us  [sum_over(): received = lax.ppermute(value, axis, pairs)]
    pallas_call x1, Pallas kernels: 9.42 us -> 8.88 us  [interior(): pl.pallas_call(functools.partial(interior_kernel, taps, repeats), out_sha...]
    ppermute x1, waiting for transfers between devices: 0.86 us -> 0.35 us  [swap_pairs(): near = lax.ppermute(near, axis, inner)]
  transfers between devices with their start and end apart: 8 -> 8, of which waited for: 5 -> 6; matrix products, arithmetic and copies ran while one was open for 0% -> 0% of each run, Pallas kernels for 41% -> 41%
where the time goes in v6:
time: 37.3 us; the launch traced here: 37.1 us
  Pallas kernels  17.6 us (47%)
  starting transfers between devices  14.5 us (39%)
  waiting for transfers between devices  3.27 us (9%)
  other arithmetic  0.92 us (2%)
  between operations  0.76 us (2%)
    ppermute x4, starting transfers between devices, sum_over(): received = lax.ppermute(value, axis, pairs)  10.7 us
    pallas_call x1, Pallas kernels, interior(): pl.pallas_call(functools.partial(interior_kernel, taps, repeats), out_sha...  8.88 us
    pallas_call x4, Pallas kernels, feature_gradients(): pl.pallas_call(functools.partial(grads_kernel, taps, repeats, first, step...  6.17 us
    ppermute x1, starting transfers between devices, swap_pairs(): near = lax.ppermute(near, axis, inner)  2.56 us
    ppermute x4, waiting for transfers between devices, sum_over(): received = lax.ppermute(value, axis, pairs)  1.73 us
    pallas_call x1, Pallas kernels, pack(): pl.pallas_call(functools.partial(pack_kernel, reach, groups // LANES), ou...  1.6 us
    ppermute x1, waiting for transfers between devices, sum_scatter(): sent = lax.ppermute(jnp.where(first, high, low), axis, [(0, 1), (1, 0)])  1.19 us
    pallas_call x1, Pallas kernels, edge(): pl.pallas_call(functools.partial(edge_kernel, taps, repeats), out_shape=(...  0.99 us
  transfers between devices with their start and end apart: 8, of which 6 were waited for; matrix products, arithmetic and copies ran while one was open for 0% of the time, Pallas kernels for 41%

profile of v6, /device:TPU:0, one launch (start us, length us, event | category | flops | bytes accessed | tf_op | source)
XLA Modules:
  0.0 37.1 jit_solution(843430121399507827)
XLA Ops:
  0.6 0.0 copy-start
  0.6 1.6 %pack_halos.1 = (bf16[864,128]{1,0:T(8,128)(2,1)S(1)}, bf16[864,128]{1,0:T(8,128)(2,1)S(1)}, bf16[7,4,192]{2,1,0:T(4,128)(2,1)S(1)}) custom-call(bf16[3,128,3072]{2,1,0:T(8,128)(2,1)} %features_ref.1, bf16[128,3072]{1,0:T(8,128)(2,1)} %cotangent_hbm.3, f32[7,4,192]{2,1,0:T(4,128)} %bitcast.3), custom_call_target="tpu_custom_call" | custom-call | flops 1000000 | bytes 1000000 | tf_op jit(solution)/shard_map/pack_halos/pallas_call | solution.py:267
  2.2 0.5 %collective-permute-start = (bf16[7,4,192]{2,1,0:T(4,128)(2,1)S(1)}, bf16[7,4,192]{2,1,0:T(4,128)(2,1)S(1)}, u32[]{:S(2)}, u32[]{:S(2)}) collective-permute-start(bf16[7,4,192]{2,1,0:T(4,128)(2,1)S(1)} %get-tuple-element.33), channel_id=1, source_target_pairs={{0,1},{1,0},{2,3},{3,2},{4,5},{5,4},{6,7},{7,6},{8,9},{9,8},{10,11... | collective-permute-start | bytes 32264 | tf_op jit(solution)/shard_map/ppermute | solution.py:40
  2.8 2.6 %collective-permute-start.1 = (bf16[864,128]{1,0:T(8,128)(2,1)S(1)}, bf16[864,128]{1,0:T(8,128)(2,1)S(1)}, u32[]{:S(2)}, u32[]{:S(2)}) collective-permute-start(bf16[864,128]{1,0:T(8,128)(2,1)S(1)} %get-tuple-element.37), channel_id=1, source_target_pairs={{0,2},{2,0},{4,6},{6,4},{8,10},{10,8},{12,14},{14,12},{16,18},{18,... | collective-permute-start | bytes 663560 | tf_op jit(solution)/shard_map/ppermute | solution.py:28
  5.3 0.7 %collective-permute-start.2 = (bf16[864,128]{1,0:T(8,128)(2,1)S(1)}, bf16[864,128]{1,0:T(8,128)(2,1)S(1)}, u32[]{:S(2)}, u32[]{:S(2)}) collective-permute-start(bf16[864,128]{1,0:T(8,128)(2,1)S(1)} %get-tuple-element.38), channel_id=1, source_target_pairs={{2,4},{4,2},{6,8},{8,6},{10,12},{12,10},{14,16},{16,14},{18,20},{2... | collective-permute-start | bytes 663560 | tf_op jit(solution)/shard_map/ppermute | solution.py:27
  6.0 0.0 collective-permute-done
  6.0 0.1 maximum_convert_fusion.weights_ref.refs_0_
  6.1 0.0 copy-done
  6.1 8.9 %interior.1 = (bf16[128,3072]{1,0:T(8,128)(2,1)S(1)}, f32[3,1024,128]{2,1,0:T(8,128)S(1)}, f32[3,1024,128]{2,1,0:T(8,128)S(1)}, f32[3,1024,128]{2,1,0:T(8,128)S(...) custom-call(bf16[3,128,3072]{2,1,0:T(8,128)(2,1)S(1)} %copy-done, ...), custom_call_target="tpu_custom_call" | custom-call | flops 49545216 | bytes 8650752 | tf_op jit(solution)/shard_map/interior/pallas_call | solution.py:435
  15.0 0.3 collective-permute-done.1.near_ref
  15.4 0.0 collective-permute-done.2.far_ref
  15.4 1.0 %edge.1 = (bf16[16,3072]{1,0:T(8,128)(2,1)S(1)}, f32[3,3,96,128]{3,2,1,0:T(8,128)S(1)}, f32[2,3,48,128]{3,2,1,0:T(8,128)S(1)}, f32[864,128]{1,0:T(8,128)S(1)}, f32[7,4,384]{2,1,0:T(4,128)S(1)}) custom-call(f32[7,4,384]{2,1,0:T(4,128)S(1)} %maximum_convert_fusion.weights_ref.refs_0_, bf16[864,128]{1,0:T(8,128)(2,1)S(1)} %collective-permute-done.1.near_ref, ...), custom_call_target="tpu_custom_call" | custom-call | flops 10000000 | bytes 4000000 | tf_op jit(solution)/shard_map/edge/pallas_call | solution.py:579
  16.4 0.1 slice_select_fusion
  16.4 0.1 collective-permute-start.3
  16.5 1.2 %collective-permute-done.3 = f32[7,4,192]{2,1,0:T(4,128)S(1)} collective-permute-done((f32[7,4,192]{2,1,0:T(4,128)S(1)}, f32[7,4,192]{2,1,0:T(4,128)S(1)}, u32[]{:S(2)}, u32[]{:S(2)}) %collective-permute-start.3) | collective-permute-done | bytes 21536 | tf_op jit(solution)/shard_map/ppermute | solution.py:71
  17.7 0.1 select_add_fusion
  17.8 4.0 %collective-permute-start.4 = (f32[7,4,192]{2,1,0:T(4,128)S(1)}, f32[7,4,192]{2,1,0:T(4,128)S(1)}, u32[]{:S(2)}, u32[]{:S(2)}) collective-permute-start(f32[7,4,192]{2,1,0:T(4,128)S(1)} %select_add_fusion), channel_id=1, source_target_pairs={{0,2},{2,0},{4,6},{6,4},{8,10},{10,8},{12,14},{14,12},{16,18},{18,... | collective-permute-start | bytes 64520 | tf_op jit(solution)/shard_map/ppermute | solution.py:54
  21.8 1.5 %feature_gradients.4 = (bf16[3,128,3072]{2,1,0:T(8,128)(2,1)}, f32[7,4,192]{2,1,0:T(4,128)S(1)}, bf16[128,3072]{1,0:T(8,128)(2,1)}) custom-call(f32[7,4,384]{2,1,0:T(4,128)S(1)} %maximum_convert_fusion.weights_ref.refs_0_, f32[3,1024,128]{2,1,0:T(8,128)S(1)} %get-tuple-element.34.refs_1_, f32[3,1024,128]{2,1,0:T(8,128)S(1)} %get-tuple-element.35.refs_2_, ...), custom_call_target="tpu_custom_call" | custom-call | flops 5505024 | bytes 1769472 | tf_op jit(solution)/shard_map/feature_gradients/pallas_call | solution.py:743
  23.3 0.4 collective-permute-done.4
  23.6 1.6 %collective-permute-start.5 = (f32[7,4,192]{2,1,0:T(4,128)S(1)}, f32[7,4,192]{2,1,0:T(4,128)S(1)}, u32[]{:S(2)}, u32[]{:S(2)}) collective-permute-start(f32[7,4,192]{2,1,0:T(4,128)S(1)} %add_add_fusion.2), channel_id=1, source_target_pairs={{0,4},{2,6},{4,0},{6,2},{8,12},{10,14},{12,8},{14,10},{16,20},{18,... | collective-permute-start | bytes 64520 | tf_op jit(solution)/shard_map/ppermute | solution.py:54
  25.2 1.5 %feature_gradients.5 = (bf16[3,128,3072]{2,1,0:T(8,128)(2,1)}, f32[7,4,192]{2,1,0:T(4,128)S(1)}) custom-call(f32[7,4,384]{2,1,0:T(4,128)S(1)} %maximum_convert_fusion.weights_ref.refs_0_, f32[3,1024,128]{2,1,0:T(8,128)S(1)} %get-tuple-element.34.refs_1_, f32[3,1024,128]{2,1,0:T(8,128)S(1)} %get-tuple-element.35.refs_2_, ...), custom_call_target="tpu_custom_call", output_to_operand_aliasing={{0}: (6, {})} | custom-call | flops 5505024 | bytes 1769472 | tf_op jit(solution)/shard_map/feature_gradients/pallas_call | solution.py:743
  26.7 0.9 %collective-permute-done.5 = f32[7,4,192]{2,1,0:T(4,128)S(1)} collective-permute-done((f32[7,4,192]{2,1,0:T(4,128)S(1)}, f32[7,4,192]{2,1,0:T(4,128)S(1)}, u32[]{:S(2)}, u32[]{:S(2)}) %collective-permute-start.5) | collective-permute-done | bytes 21536 | tf_op jit(solution)/shard_map/ppermute | solution.py:54
  27.6 2.1 %collective-permute-start.6 = (f32[7,4,192]{2,1,0:T(4,128)S(1)}, f32[7,4,192]{2,1,0:T(4,128)S(1)}, u32[]{:S(2)}, u32[]{:S(2)}) collective-permute-start(f32[7,4,192]{2,1,0:T(4,128)S(1)} %add_add_fusion.1), channel_id=1, source_target_pairs={{0,8},{2,10},{4,12},{6,14},{8,0},{10,2},{12,4},{14,6},{16,24},{18,... | collective-permute-start | bytes 64520 | tf_op jit(solution)/shard_map/ppermute | solution.py:54
  29.6 1.5 %feature_gradients.6 = (bf16[3,128,3072]{2,1,0:T(8,128)(2,1)}, f32[7,4,192]{2,1,0:T(4,128)S(1)}) custom-call(f32[7,4,384]{2,1,0:T(4,128)S(1)} %maximum_convert_fusion.weights_ref.refs_0_, f32[3,1024,128]{2,1,0:T(8,128)S(1)} %get-tuple-element.34.refs_1_, f32[3,1024,128]{2,1,0:T(8,128)S(1)} %get-tuple-element.35.refs_2_, ...), custom_call_target="tpu_custom_call", output_to_operand_aliasing={{0}: (6, {})} | custom-call | flops 5505024 | bytes 1769472 | tf_op jit(solution)/shard_map/feature_gradients/pallas_call | solution.py:743
  31.1 0.4 %collective-permute-done.6 = f32[7,4,192]{2,1,0:T(4,128)S(1)} collective-permute-done((f32[7,4,192]{2,1,0:T(4,128)S(1)}, f32[7,4,192]{2,1,0:T(4,128)S(1)}, u32[]{:S(2)}, u32[]{:S(2)}) %collective-permute-start.6) | collective-permute-done | bytes 21536 | tf_op jit(solution)/shard_map/ppermute | solution.py:54
  31.5 3.1 %collective-permute-start.7 = (f32[7,4,192]{2,1,0:T(4,128)S(1)}, f32[7,4,192]{2,1,0:T(4,128)S(1)}, u32[]{:S(2)}, u32[]{:S(2)}) collective-permute-start(f32[7,4,192]{2,1,0:T(4,128)S(1)} %add_add_fusion), channel_id=1, source_target_pairs={{0,16},{2,18},{4,20},{6,22},{8,24},{10,26},{12,28},{14,30},{16,0},... | collective-permute-start | bytes 64520 | tf_op jit(solution)/shard_map/ppermute | solution.py:54
  34.6 1.7 %feature_gradients.7 = (bf16[3,128,3072]{2,1,0:T(8,128)(2,1)}, f32[7,4,192]{2,1,0:T(4,128)S(1)}) custom-call(f32[7,4,384]{2,1,0:T(4,128)S(1)} %maximum_convert_fusion.weights_ref.refs_0_, f32[3,1024,128]{2,1,0:T(8,128)S(1)} %get-tuple-element.34.refs_1_, f32[3,1024,128]{2,1,0:T(8,128)S(1)} %get-tuple-element.35.refs_2_, ...), custom_call_target="tpu_custom_call", output_to_operand_aliasing={{0}: (6, {})} | custom-call | flops 5505024 | bytes 1769472 | tf_op jit(solution)/shard_map/feature_gradients/pallas_call | solution.py:743
  36.4 0.1 collective-permute-done.7
  36.5 0.6 %multiply_bitcast_fusion = f32[4,7,192]{2,0,1:T(4,128)} fusion(f32[7,4,192]{2,1,0:T(4,128)S(1)} %get-tuple-element.62, f32[7,4,192]{2,1,0:T(4,128)S(1)} %add_add_fusion, f32[7,4,192]{2,1,0:T(4,128)S(1)} %collective-permute-done.7), kind=kLoop, calls=%fused_computation | loop fusion | flops 16128 | bytes 86016 | tf_op jit(solution)/shard_map/transpose | solution.py:807
  (4 shorter events, 0.1 us)
Async XLA Ops:
  0.6 5.5 %copy-start = (bf16[3,128,3072]{2,1,0:T(8,128)(2,1)S(1)}, bf16[3,128,3072]{2,1,0:T(8,128)(2,1)}, u32[]{:S(2)}) copy-start(bf16[3,128,3072]{2,1,0:T(8,128)(2,1)} %features_ref.1) | copy-start | bytes 7077892
  2.2 3.8 %collective-permute-start = (bf16[7,4,192]{2,1,0:T(4,128)(2,1)S(1)}, bf16[7,4,192]{2,1,0:T(4,128)(2,1)S(1)}, u32[]{:S(2)}, u32[]{:S(2)}) collective-permute-start(bf16[7,4,192]{2,1,0:T(4,128)(2,1)S(1)} %get-tuple-element.33), channel_id=1, source_target_pairs={{0,1},{1,0},{2,3},{3,2},{4,5},{5,4},{6,7},{7,6},{8,9},{9,8},{10,11... | collective-permute-start | bytes 32264 | tf_op jit(solution)/shard_map/ppermute | solution.py:40
  2.8 12.6 %collective-permute-start.1 = (bf16[864,128]{1,0:T(8,128)(2,1)S(1)}, bf16[864,128]{1,0:T(8,128)(2,1)S(1)}, u32[]{:S(2)}, u32[]{:S(2)}) collective-permute-start(bf16[864,128]{1,0:T(8,128)(2,1)S(1)} %get-tuple-element.37), channel_id=1, source_target_pairs={{0,2},{2,0},{4,6},{6,4},{8,10},{10,8},{12,14},{14,12},{16,18},{18,... | collective-permute-start | bytes 663560 | tf_op jit(solution)/shard_map/ppermute | solution.py:28
  5.3 10.0 %collective-permute-start.2 = (bf16[864,128]{1,0:T(8,128)(2,1)S(1)}, bf16[864,128]{1,0:T(8,128)(2,1)S(1)}, u32[]{:S(2)}, u32[]{:S(2)}) collective-permute-start(bf16[864,128]{1,0:T(8,128)(2,1)S(1)} %get-tuple-element.38), channel_id=1, source_target_pairs={{2,4},{4,2},{6,8},{8,6},{10,12},{12,10},{14,16},{16,14},{18,20},{2... | collective-permute-start | bytes 663560 | tf_op jit(solution)/shard_map/ppermute | solution.py:27
  16.4 1.3 %collective-permute-start.3 = (f32[7,4,192]{2,1,0:T(4,128)S(1)}, f32[7,4,192]{2,1,0:T(4,128)S(1)}, u32[]{:S(2)}, u32[]{:S(2)}) collective-permute-start(f32[7,4,192]{2,1,0:T(4,128)S(1)} %slice_select_fusion), channel_id=1, source_target_pairs={{0,1},{1,0},{2,3},{3,2},{4,5},{5,4},{6,7},{7,6},{8,9},{9,8},{10,11... | collective-permute-start | bytes 64520 | tf_op jit(solution)/shard_map/ppermute | solution.py:71
  17.8 5.8 %collective-permute-start.4 = (f32[7,4,192]{2,1,0:T(4,128)S(1)}, f32[7,4,192]{2,1,0:T(4,128)S(1)}, u32[]{:S(2)}, u32[]{:S(2)}) collective-permute-start(f32[7,4,192]{2,1,0:T(4,128)S(1)} %select_add_fusion), channel_id=1, source_target_pairs={{0,2},{2,0},{4,6},{6,4},{8,10},{10,8},{12,14},{14,12},{16,18},{18,... | collective-permute-start | bytes 64520 | tf_op jit(solution)/shard_map/ppermute | solution.py:54
  23.6 3.9 %collective-permute-start.5 = (f32[7,4,192]{2,1,0:T(4,128)S(1)}, f32[7,4,192]{2,1,0:T(4,128)S(1)}, u32[]{:S(2)}, u32[]{:S(2)}) collective-permute-start(f32[7,4,192]{2,1,0:T(4,128)S(1)} %add_add_fusion.2), channel_id=1, source_target_pairs={{0,4},{2,6},{4,0},{6,2},{8,12},{10,14},{12,8},{14,10},{16,20},{18,... | collective-permute-start | bytes 64520 | tf_op jit(solution)/shard_map/ppermute | solution.py:54
  27.6 3.9 %collective-permute-start.6 = (f32[7,4,192]{2,1,0:T(4,128)S(1)}, f32[7,4,192]{2,1,0:T(4,128)S(1)}, u32[]{:S(2)}, u32[]{:S(2)}) collective-permute-start(f32[7,4,192]{2,1,0:T(4,128)S(1)} %add_add_fusion.1), channel_id=1, source_target_pairs={{0,8},{2,10},{4,12},{6,14},{8,0},{10,2},{12,4},{14,6},{16,24},{18,... | collective-permute-start | bytes 64520 | tf_op jit(solution)/shard_map/ppermute | solution.py:54
  31.5 4.9 %collective-permute-start.7 = (f32[7,4,192]{2,1,0:T(4,128)S(1)}, f32[7,4,192]{2,1,0:T(4,128)S(1)}, u32[]{:S(2)}, u32[]{:S(2)}) collective-permute-start(f32[7,4,192]{2,1,0:T(4,128)S(1)} %add_add_fusion), channel_id=1, source_target_pairs={{0,16},{2,18},{4,20},{6,22},{8,24},{10,26},{12,28},{14,30},{16,0},... | collective-permute-start | bytes 64520 | tf_op jit(solution)/shard_map/ppermute | solution.py:54

commit v7 on v6

--- a/solution.py
+++ b/solution.py
@@ -12,7 +12,7 @@
 CHUNK = 16
 PAD = 16
 PIECES = 4
-VMEM_LIMIT = 12 * 1024 * 1024
+VMEM_LIMIT = 28 * 1024 * 1024
 PACK_LIMIT = 16 * 1024 * 1024
 F32 = jnp.float32
 VMEM_SPEC = pl.BlockSpec(memory_space=pltpu.VMEM)
@@ -142,13 +142,13 @@
 def held_tokens(reach):
     wide = 2 * reach
     return (
-        (0, CHUNK, reach),
+        (0, wide, reach),
         (0, reach, wide),
         (0, reach, wide),
-        (0, CHUNK, 0),
+        (0, wide, 0),
         (0, 0, reach),
         (0, 0, reach),
-        (reach, CHUNK, reach),
+        (reach, wide, reach),
         (0, 0, reach),
     )
 
@@ -215,42 +215,53 @@
 ):
     length = cotangent_hbm.shape[0]
     copies = [
-        pltpu.make_async_copy(master_hbm, master, sems.at[3]),
         pltpu.make_async_copy(features_hbm.at[:, length - PAD :, :], tail, sems.at[0]),
         pltpu.make_async_copy(features_hbm.at[:, :PAD, :], head, sems.at[1]),
         pltpu.make_async_copy(cotangent_hbm.at[:PAD, :], upstream, sems.at[2]),
+        pltpu.make_async_copy(master_hbm, master, sems.at[3]),
     ]
     for copy in copies:
         copy.start()
     even = is_even("ctx")
     repeats = upstream.shape[1] // (columns * LANES)
     block = reach * columns * repeats
-    b_s[-block:, :] = jnp.zeros((block, LANES), F32)
+    b_s[5 * block : 6 * block, :] = jnp.zeros((block, LANES), F32)
     last, first = Halo(b_s, repeats, columns), Halo(a_s, repeats, columns)
-    for copy in copies:
+    wide = 2 * reach
+
+    def place(message, parts):
+        def repeat_step(repeat, carry):
+            for column in range(columns):
+                lanes = lane_slice(repeat * columns + column)
+                for token, ref, start, stop in parts:
+                    value = ref[:, lanes].astype(F32)[start:stop]
+                    message.put(token, column, repeat, value)
+            return carry
+
+        lax.fori_loop(0, repeats, repeat_step, 0)
+
+    copies[0].wait()
+    place(
+        last,
+        (
+            (0, tail.at[0], PAD - reach, PAD),
+            (reach, tail.at[1], PAD - wide, PAD),
+            (3 * reach, tail.at[2], PAD - wide, PAD),
+        ),
+    )
+    for copy in copies[1:]:
         copy.wait()
     rounded_ref[...] = master[...].astype(rounded_ref.dtype)
-    wide = 2 * reach
-
-    def repeat_step(repeat, carry):
-        for column in range(columns):
-            lanes = lane_slice(repeat * columns + column)
-
-            def put(message, token, ref, start, stop):
-                value = ref[:, lanes].astype(F32)[start:stop]
-                message.put(token, column, repeat, value)
-
-            put(last, 0, tail.at[0], PAD - reach, PAD)
-            put(last, reach, tail.at[1], PAD - wide, PAD)
-            put(last, 3 * reach, tail.at[2], PAD - wide, PAD)
-            put(first, 0, head.at[0], 0, wide)
-            put(first, wide, upstream, 0, wide)
-            put(first, 2 * wide, head.at[1], 0, reach)
-            put(first, 5 * reach, head.at[2], 0, reach)
-        return carry
-
-    lax.fori_loop(0, repeats, repeat_step, 0)
-    ending, opening = b_s[...], a_s[...]
+    place(
+        first,
+        (
+            (0, head.at[0], 0, wide),
+            (wide, upstream, 0, wide),
+            (2 * wide, head.at[1], 0, reach),
+            (5 * reach, head.at[2], 0, reach),
+        ),
+    )
+    ending, opening = b_s[: 6 * block, :], a_s[: 6 * block, :]
     near_ref[...] = jnp.where(even, ending, opening).astype(near_ref.dtype)
     far_ref[...] = jnp.where(even, opening, ending).astype(far_ref.dtype)
 
@@ -264,6 +275,7 @@
         for value in (features, cotangent, master)
     ]
     message = jax.ShapeDtypeStruct((6 * reach * channels // LANES, LANES), kind)
+    room = ((6 * reach + 8) * channels // LANES, LANES)
     return pl.pallas_call(
         functools.partial(pack_kernel, reach, groups // LANES),
         out_shape=(message, message, jax.ShapeDtypeStruct(master.shape, jnp.bfloat16)),
@@ -274,8 +286,8 @@
             pltpu.VMEM((banks, PAD, channels), kind),
             pltpu.VMEM((PAD, channels), kind),
             pltpu.VMEM(master.shape, F32),
-            pltpu.VMEM(message.shape, F32),
-            pltpu.VMEM(message.shape, F32),
+            pltpu.VMEM(room, F32),
+            pltpu.VMEM(room, F32),
             pltpu.SemaphoreType.DMA((4,)),
         ],
         cost_estimate=pl.CostEstimate(flops=10**6, bytes_accessed=10**6, transcendentals=0),
@@ -297,7 +309,7 @@
     *refs,
 ):
     *held_refs, sums_ref = refs[:9]
-    *work_refs, m_s, cotangent_ref, sem = refs[9:]
+    *work_refs, cotangent_ref, sem = refs[9:]
     *work_refs, k_other, v_other = work_refs
     q_s, k_s, v_s, c_s, kc_s, vc_s, p_s, gm_s = work_refs
     pairs = ((k_s, v_s), (k_other, v_other))
@@ -308,7 +320,6 @@
     fetch = pltpu.make_async_copy(cotangent_hbm, cotangent_ref, sem)
     fetch.start()
     sums_ref[...] = jnp.zeros_like(sums_ref)
-    m_t = Tokens(m_s, repeats)
 
     def part_of(repeat, column):
         first = repeat * groups + column * LANES
@@ -341,8 +352,8 @@
     chunks(lambda step, base, rows: put_pair(0, base, rows))
     for column in range(columns):
         lanes = slice(column * LANES, (column + 1) * LANES)
-        gq_t, gk_t, gv_t = (
-            Tokens(ref, repeats, 0, (column,)) for ref in (gq_ref, gk_ref, gv_ref)
+        m_t, gq_t, gk_t, gv_t = (
+            Tokens(ref, repeats, 0, (column,)) for ref in (mixed_ref, gq_ref, gk_ref, gv_ref)
         )
         k_t, v_t = (Tokens(ref, repeats, PAD) for ref in pairs[column % 2])
         wq, wk, wv, wm = (weight_rows(weights_ref, bank, lanes) for bank in range(4))
@@ -375,7 +386,7 @@
                 mixer = dot_taps(wm, inner)
                 gq = up * mixer
                 gm = up * qc
-                m_t[token] = qc * mixer
+                m_t[base + token] = qc * mixer
                 gm_t[base + token] = gm
                 gq_t[base + token] = gq
                 if token < 2 * reach:
@@ -384,9 +395,6 @@
                 sums.add(0, gq, sources)
                 sums.add(3, gm, inner)
             sums.store(sums_ref, lanes)
-            for repeat in range(repeats):
-                part = part_of(repeat, column)
-                mixed_ref[rows, part] = m_t.take(0, repeat, CHUNK).astype(mixed_ref.dtype)
 
         def backward(step, base, rows):
             k_w, v_w, gm_w = (
@@ -435,8 +443,7 @@
     mixed, gq, gk, gv, *arrays, sums = pl.pallas_call(
         functools.partial(interior_kernel, taps, repeats),
         out_shape=(
-            jax.ShapeDtypeStruct(cotangent.shape, cotangent.dtype),
-            *[grad] * 3,
+            *[grad] * 4,
             *held,
             jax.ShapeDtypeStruct((banks, taps, repeats, groups), F32),
         ),
@@ -444,7 +451,6 @@
         out_specs=(VMEM_SPEC,) * 13,
         scratch_shapes=[pltpu.VMEM(work_shape, F32) for _ in range(10)]
         + [
-            pltpu.VMEM((CHUNK * repeats, LANES), F32),
             pltpu.VMEM(cotangent.shape, cotangent.dtype),
             pltpu.SemaphoreType.DMA,
         ],
@@ -483,7 +489,6 @@
     vc_s,
     p_s,
     gm_s,
-    m_s,
 ):
     reach = taps - 1
     groups = weights_ref.shape[2]
@@ -493,7 +498,6 @@
     near, far = near_ref[...].astype(F32), far_ref[...].astype(F32)
     before_s[...] = jnp.where(even, far, near)
     after_ref[...] = jnp.where(even, near, far)
-    m_t = Tokens(m_s, repeats)
     kc_t, vc_t, p_t, gm_t = (Tokens(ref, repeats, PAD) for ref in (kc_s, vc_s, p_s, gm_s))
 
     def column_step(column, carry):
@@ -512,6 +516,7 @@
         k_w = Window(lambda t: k_t[t] if t >= 0 else h_t[3 * reach + t])
         v_w = Window(lambda t: v_t[t] if t >= 0 else h_t[5 * reach + t])
         gq_o, gk_o, gv_o = (Tokens(ghead_ref, repeats, 0, (bank, column)) for bank in range(3))
+        m_o = Tokens(mixed_ref, repeats, 0, (column,))
         for token in range(-reach, reach):
             kc = dot_taps(wk, k_w.back(token, taps))
             vc = dot_taps(wv, v_w.back(token, taps))
@@ -520,20 +525,19 @@
                 kc_t[token] = kc
                 vc_t[token] = vc
         p_w = Window(lambda t: p_t[t] if t < reach else p_i[t])
-        for token in range(CHUNK):
+        for token in range(2 * reach):
             up = c_t[token]
             sources = q_w.back(token, taps)
             products = p_w.back(token, taps)
             qc = dot_taps(wq, sources)
             mixer = dot_taps(wm, products)
-            m_t[token] = qc * mixer
-            if token < 2 * reach:
-                gq = up * mixer
-                gm = up * qc
-                gm_t[token] = gm
-                gq_o[token] = gq
-                sums.add(0, gq, sources)
-                sums.add(3, gm, products)
+            gq = up * mixer
+            gm = up * qc
+            m_o[token] = qc * mixer
+            gm_t[token] = gm
+            gq_o[token] = gq
+            sums.add(0, gq, sources)
+            sums.add(3, gm, products)
         gm_w = Window(lambda t: gm_t[t])
         for token in range(reach):
             gp = dot_taps(wm, gm_w.ahead(token, taps))
@@ -543,9 +547,6 @@
             gv_o[token] = gv
             sums.add(1, gk, k_w.back(token, taps))
             sums.add(2, gv, v_w.back(token, taps))
-        for repeat in range(repeats):
-            part = part_slice(repeat, groups, column)
-            mixed_ref[:, part] = m_t.take(0, repeat, CHUNK).astype(mixed_ref.dtype)
 
         n_t = Halo(after_ref, repeats, columns).tokens(column)
         q_w = Window(lambda t: q_t[t] if t < 0 else n_t[t])
@@ -575,11 +576,10 @@
     columns = groups // LANES
     reach = taps - 1
     repeats = near.shape[0] // (6 * reach * columns)
-    channels = repeats * groups
     return pl.pallas_call(
         functools.partial(edge_kernel, taps, repeats),
         out_shape=(
-            jax.ShapeDtypeStruct((CHUNK, channels), near.dtype),
+            jax.ShapeDtypeStruct((columns, 2 * reach * repeats, LANES), F32),
             jax.ShapeDtypeStruct((3, columns, 2 * reach * repeats, LANES), F32),
             jax.ShapeDtypeStruct((2, columns, reach * repeats, LANES), F32),
             jax.ShapeDtypeStruct(near.shape, F32),
@@ -591,8 +591,7 @@
             pltpu.VMEM(sums.shape, F32),
             pltpu.VMEM(near.shape, F32),
         ]
-        + [pltpu.VMEM((2 * PAD * repeats, LANES), F32) for _ in range(4)]
-        + [pltpu.VMEM((CHUNK * repeats, LANES), F32)],
+        + [pltpu.VMEM((2 * PAD * repeats, LANES), F32) for _ in range(4)],
         cost_estimate=pl.CostEstimate(
             flops=10**7, bytes_accessed=4 * 10**6, transcendentals=0
         ),
@@ -601,6 +600,52 @@
     )(weights, near, far, sums, *arrays)
 
 
+def mixed_kernel(repeats, middle, top, out_ref, zero_ref, o_s):
+    columns, rows, _ = middle.shape
+    groups = columns * LANES
+    ready = top.shape[1] // repeats
+    zero_ref[...] = jnp.zeros_like(zero_ref)
+
+    def column_step(column, carry):
+        m_t, t_t = (Tokens(ref, repeats, 0, (column,)) for ref in (middle, top))
+        o_t = Tokens(o_s, repeats)
+        for token in range(CHUNK):
+            o_t[token] = t_t[token] if token < ready else m_t[token]
+        for repeat in range(repeats):
+            part = part_slice(repeat, groups, column)
+            out_ref[:CHUNK, part] = o_t.take(0, repeat, CHUNK).astype(out_ref.dtype)
+
+        def chunk_step(chunk, carry):
+            base = pl.multiple_of(chunk * CHUNK, CHUNK)
+            for repeat in range(repeats):
+                part = part_slice(repeat, groups, column)
+                value = m_t.take(base, repeat, CHUNK)
+                out_ref[pl.ds(base, CHUNK), part] = value.astype(out_ref.dtype)
+            return carry
+
+        return lax.fori_loop(1, rows // repeats // CHUNK, chunk_step, carry)
+
+    lax.fori_loop(0, columns, column_step, 0)
+
+
+def round_mixed(middle, top, cotangent, zero):
+    columns, rows, _ = middle.shape
+    length, channels = cotangent.shape
+    repeats = rows // length
+    return pl.pallas_call(
+        functools.partial(mixed_kernel, repeats),
+        out_shape=(jax.ShapeDtypeStruct(cotangent.shape, cotangent.dtype), zero),
+        in_specs=[VMEM_SPEC] * 2,
+        out_specs=(VMEM_SPEC,) * 2,
+        scratch_shapes=[pltpu.VMEM((CHUNK * repeats, LANES), F32)],
+        cost_estimate=pl.CostEstimate(
+            flops=length * channels, bytes_accessed=6 * length * channels, transcendentals=0
+        ),
+        compiler_params=pltpu.CompilerParams(vmem_limit_bytes=VMEM_LIMIT),
+        name="round_mixed",
+    )(middle, top)
+
+
 def grads_kernel(taps, repeats, first, steps, count, *refs):
     refs = list(refs)
     top, bottom = first == 0, first + steps == count
@@ -611,7 +656,7 @@
 
     weights_ref, gq, gk, gv, ghead, gtail = pop(6)
     if top:
-        middle, head = pop(2)
+        (whole,) = pop(1)
     else:
         pop(1)
     if bottom:
@@ -626,12 +671,7 @@
     zero_ref[...] = jnp.zeros_like(zero_ref)
     if top:
         (mixed_hbm,) = pop(1)
-        copies = [
-            pltpu.make_async_copy(head, mixed_hbm.at[:CHUNK, :], sems.at[steps]),
-            pltpu.make_async_copy(
-                middle.at[CHUNK:, :], mixed_hbm.at[CHUNK:, :], sems.at[steps + 1]
-            ),
-        ]
+        copies = [pltpu.make_async_copy(whole, mixed_hbm, sems.at[steps])]
         for copy in copies:
             copy.start()
 
@@ -722,9 +762,9 @@
     aliases = {}
     scratch = []
     if piece == 0:
-        operands += mixed
-        in_specs += [VMEM_SPEC] * 2
-        out_shape.append(jax.ShapeDtypeStruct(mixed[0].shape, mixed[0].dtype))
+        operands.append(mixed)
+        in_specs.append(VMEM_SPEC)
+        out_shape.append(jax.ShapeDtypeStruct(mixed.shape, mixed.dtype))
         out_specs.append(ANY_SPEC)
     else:
         aliases = {len(operands): 0}
@@ -749,7 +789,7 @@
         + [
             pltpu.VMEM((steps, banks, CHUNK, channels), features.dtype),
             pltpu.VMEM((CHUNK * repeats, LANES), F32),
-            pltpu.SemaphoreType.DMA((steps + 2,)),
+            pltpu.SemaphoreType.DMA((steps + 1,)),
         ],
         input_output_aliases=aliases,
         cost_estimate=pl.CostEstimate(
@@ -776,13 +816,16 @@
     top, ghead, gtail, after, sums = edge(weights, *halos, sums, arrays)
     repeats = features.shape[2] // weights.shape[2]
     pieces = PIECES if (length // CHUNK) % PIECES == 0 else 1
-    owned = sum_scatter(sums, "fsdp")
+    portion = sums.shape[2] // lax.axis_size("fsdp")
+    zero = jax.ShapeDtypeStruct((*sums.shape[:2], portion), F32)
+    whole, nothing = round_mixed(middle, top, cotangent, zero)
+    owned = sum_scatter(sums, "fsdp") + nothing
     made = {"grads": None}
 
     def beside(piece):
         if piece >= pieces:
             return 0.0
-        made["grads"], zero, *rest = feature_gradients(
+        made["grads"], nothing, *rest = feature_gradients(
             piece,
             pieces,
             features,
@@ -790,15 +833,15 @@
             grads,
             ghead,
             gtail,
-            (middle, top),
+            whole,
             after,
             arrays,
             made["grads"],
-            jax.ShapeDtypeStruct(owned.shape, F32),
+            zero,
         )
         if rest:
             made["mixed"] = rest[0]
-        return zero
+        return nothing
 
     summed, done = sum_over(owned, "ctx", beside)
     for piece in range(done, pieces):

time: 37.3 us -> 36.9 us (0.989)
    ppermute x1, waiting for transfers between devices: 1.19 us -> 0.76 us  [sum_scatter(): sent = lax.ppermute(jnp.where(first, high, low), axis, [(0, 1), (1, 0)])]
    pallas_call x0 -> x1, Pallas kernels: none -> 0.42 us  [round_mixed(): pl.pallas_call(functools.partial(mixed_kernel, repeats), out_shape=(jax.S...]
  transfers between devices with their start and end apart: 8 -> 8, of which waited for: 6 -> 6; matrix products, arithmetic and copies ran while one was open for 0% -> 0% of each run, Pallas kernels for 41% -> 42%
where the time goes in v7:
time: 36.9 us; the launch traced here: 36.7 us
  Pallas kernels  17.7 us (48%)
  starting transfers between devices  14.3 us (39%)
  waiting for transfers between devices  3.07 us (8%)
  other arithmetic  0.93 us (3%)
  between operations  0.76 us (2%)
    ppermute x4, starting transfers between devices, sum_over(): received = lax.ppermute(value, axis, pairs)  10.5 us
    pallas_call x1, Pallas kernels, interior(): pl.pallas_call(functools.partial(interior_kernel, taps, repeats), out_sha...  8.69 us
    pallas_call x4, Pallas kernels, feature_gradients(): pl.pallas_call(functools.partial(grads_kernel, taps, repeats, first, step...  6.14 us
    ppermute x1, starting transfers between devices, swap_pairs(): near = lax.ppermute(near, axis, inner)  2.56 us
    ppermute x4, waiting for transfers between devices, sum_over(): received = lax.ppermute(value, axis, pairs)  1.76 us
    pallas_call x1, Pallas kernels, pack(): pl.pallas_call(functools.partial(pack_kernel, reach, groups // LANES), ou...  1.49 us
    pallas_call x1, Pallas kernels, edge(): pl.pallas_call(functools.partial(edge_kernel, taps, repeats), out_shape=(...  0.94 us
    ppermute x1, waiting for transfers between devices, sum_scatter(): sent = lax.ppermute(jnp.where(first, high, low), axis, [(0, 1), (1, 0)])  0.76 us
  transfers between devices with their start and end apart: 8, of which 6 were waited for; matrix products, arithmetic and copies ran while one was open for 0% of the time, Pallas kernels for 42%

profile of v7, /device:TPU:0, one launch (start us, length us, event | category | flops | bytes accessed | tf_op | source)
XLA Modules:
  0.0 36.7 jit_solution(8529255807110151628)
XLA Ops:
  0.6 0.0 copy-start
  0.6 1.5 %pack_halos.1 = (bf16[864,128]{1,0:T(8,128)(2,1)S(1)}, bf16[864,128]{1,0:T(8,128)(2,1)S(1)}, bf16[7,4,192]{2,1,0:T(4,128)(2,1)S(1)}) custom-call(bf16[3,128,3072]{2,1,0:T(8,128)(2,1)} %features_ref.1, bf16[128,3072]{1,0:T(8,128)(2,1)} %cotangent_hbm.3, f32[7,4,192]{2,1,0:T(4,128)} %bitcast.3), custom_call_target="tpu_custom_call" | custom-call | flops 1000000 | bytes 1000000 | tf_op jit(solution)/shard_map/pack_halos/pallas_call | solution.py:279
  2.1 0.5 %collective-permute-start = (bf16[7,4,192]{2,1,0:T(4,128)(2,1)S(1)}, bf16[7,4,192]{2,1,0:T(4,128)(2,1)S(1)}, u32[]{:S(2)}, u32[]{:S(2)}) collective-permute-start(bf16[7,4,192]{2,1,0:T(4,128)(2,1)S(1)} %get-tuple-element.35), channel_id=1, source_target_pairs={{0,1},{1,0},{2,3},{3,2},{4,5},{5,4},{6,7},{7,6},{8,9},{9,8},{10,11... | collective-permute-start | bytes 32264 | tf_op jit(solution)/shard_map/ppermute | solution.py:40
  2.7 2.6 %collective-permute-start.1 = (bf16[864,128]{1,0:T(8,128)(2,1)S(1)}, bf16[864,128]{1,0:T(8,128)(2,1)S(1)}, u32[]{:S(2)}, u32[]{:S(2)}) collective-permute-start(bf16[864,128]{1,0:T(8,128)(2,1)S(1)} %get-tuple-element.39), channel_id=1, source_target_pairs={{0,2},{2,0},{4,6},{6,4},{8,10},{10,8},{12,14},{14,12},{16,18},{18,... | collective-permute-start | bytes 663560 | tf_op jit(solution)/shard_map/ppermute | solution.py:28
  5.2 0.7 %collective-permute-start.2 = (bf16[864,128]{1,0:T(8,128)(2,1)S(1)}, bf16[864,128]{1,0:T(8,128)(2,1)S(1)}, u32[]{:S(2)}, u32[]{:S(2)}) collective-permute-start(bf16[864,128]{1,0:T(8,128)(2,1)S(1)} %get-tuple-element.40), channel_id=1, source_target_pairs={{2,4},{4,2},{6,8},{8,6},{10,12},{12,10},{14,16},{16,14},{18,20},{2... | collective-permute-start | bytes 663560 | tf_op jit(solution)/shard_map/ppermute | solution.py:27
  5.9 0.0 collective-permute-done
  5.9 0.1 maximum_convert_fusion.weights_ref.refs_0_
  6.0 0.0 copy-done
  6.0 8.7 %interior.1 = (f32[3,1024,128]{2,1,0:T(8,128)S(1)}, f32[3,1024,128]{2,1,0:T(8,128)S(1)}, f32[3,1024,128]{2,1,0:T(8,128)S(1)}, f32[3,1024,128]{2,1,0:T(8,128)S(1)...) custom-call(bf16[3,128,3072]{2,1,0:T(8,128)(2,1)S(1)} %copy-done, ...), custom_call_target="tpu_custom_call" | custom-call | flops 49545216 | bytes 8650752 | tf_op jit(solution)/shard_map/interior/pallas_call | solution.py:443
  14.7 0.5 %collective-permute-done.1.near_ref = bf16[864,128]{1,0:T(8,128)(2,1)S(1)} collective-permute-done((bf16[864,128]{1,0:T(8,128)(2,1)S(1)}, bf16[864,128]{1,0:T(8,128)(2,1)S(1)}, u32[]{:S(2)}, u32[]{:S(2)}) %collective-permute-start.1) | collective-permute-done | bytes 221216 | tf_op jit(solution)/shard_map/ppermute | solution.py:28
  15.3 0.0 collective-permute-done.2.far_ref
  15.3 0.9 %edge.1 = (f32[3,96,128]{2,1,0:T(8,128)S(1)}, f32[3,3,96,128]{3,2,1,0:T(8,128)S(1)}, f32[2,3,48,128]{3,2,1,0:T(8,128)S(1)}, f32[864,128]{1,0:T(8,128)S(1)}, f32[7,4,384]{2,1,0:T(4,128)S(1)}) custom-call(f32[7,4,384]{2,1,0:T(4,128)S(1)} %maximum_convert_fusion.weights_ref.refs_0_, bf16[864,128]{1,0:T(8,128)(2,1)S(1)} %collective-permute-done.1.near_ref, ...), custom_call_target="tpu_custom_call" | custom-call | flops 10000000 | bytes 4000000 | tf_op jit(solution)/shard_map/edge/pallas_call | solution.py:579
  16.2 0.1 slice_select_fusion
  16.3 0.1 collective-permute-start.3
  16.4 0.4 %round_mixed.1 = (bf16[128,3072]{1,0:T(8,128)(2,1)S(1)}, f32[7,4,192]{2,1,0:T(4,128)S(1)}) custom-call(f32[3,1024,128]{2,1,0:T(8,128)S(1)} %get-tuple-element.52.middle, f32[3,96,128]{2,1,0:T(8,128)S(1)} %get-tuple-element.53.top), custom_call_target="tpu_custom_call" | custom-call | flops 393216 | bytes 2359296 | tf_op jit(solution)/shard_map/round_mixed/pallas_call | solution.py:635
  16.8 0.8 %collective-permute-done.3 = f32[7,4,192]{2,1,0:T(4,128)S(1)} collective-permute-done((f32[7,4,192]{2,1,0:T(4,128)S(1)}, f32[7,4,192]{2,1,0:T(4,128)S(1)}, u32[]{:S(2)}, u32[]{:S(2)}) %collective-permute-start.3) | collective-permute-done | bytes 21536 | tf_op jit(solution)/shard_map/ppermute | solution.py:71
  17.6 0.1 add_add_fusion.3
  17.6 3.8 %collective-permute-start.4 = (f32[7,4,192]{2,1,0:T(4,128)S(1)}, f32[7,4,192]{2,1,0:T(4,128)S(1)}, u32[]{:S(2)}, u32[]{:S(2)}) collective-permute-start(f32[7,4,192]{2,1,0:T(4,128)S(1)} %add_add_fusion.3), channel_id=1, source_target_pairs={{0,2},{2,0},{4,6},{6,4},{8,10},{10,8},{12,14},{14,12},{16,18},{18,... | collective-permute-start | bytes 64520 | tf_op jit(solution)/shard_map/ppermute | solution.py:54
  21.4 1.5 %feature_gradients.4 = (bf16[3,128,3072]{2,1,0:T(8,128)(2,1)}, f32[7,4,192]{2,1,0:T(4,128)S(1)}, bf16[128,3072]{1,0:T(8,128)(2,1)}) custom-call(f32[7,4,384]{2,1,0:T(4,128)S(1)} %maximum_convert_fusion.weights_ref.refs_0_, f32[3,1024,128]{2,1,0:T(8,128)S(1)} %get-tuple-element.36.refs_1_, f32[3,1024,128]{2,1,0:T(8,128)S(1)} %get-tuple-element.37.refs_2_, ...), custom_call_target="tpu_custom_call" | custom-call | flops 5505024 | bytes 1769472 | tf_op jit(solution)/shard_map/feature_gradients/pallas_call | solution.py:783
  22.9 0.4 %collective-permute-done.4 = f32[7,4,192]{2,1,0:T(4,128)S(1)} collective-permute-done((f32[7,4,192]{2,1,0:T(4,128)S(1)}, f32[7,4,192]{2,1,0:T(4,128)S(1)}, u32[]{:S(2)}, u32[]{:S(2)}) %collective-permute-start.4) | collective-permute-done | bytes 21536 | tf_op jit(solution)/shard_map/ppermute | solution.py:54
  23.3 1.6 %collective-permute-start.5 = (f32[7,4,192]{2,1,0:T(4,128)S(1)}, f32[7,4,192]{2,1,0:T(4,128)S(1)}, u32[]{:S(2)}, u32[]{:S(2)}) collective-permute-start(f32[7,4,192]{2,1,0:T(4,128)S(1)} %add_add_fusion.2), channel_id=1, source_target_pairs={{0,4},{2,6},{4,0},{6,2},{8,12},{10,14},{12,8},{14,10},{16,20},{18,... | collective-permute-start | bytes 64520 | tf_op jit(solution)/shard_map/ppermute | solution.py:54
  24.9 1.5 %feature_gradients.5 = (bf16[3,128,3072]{2,1,0:T(8,128)(2,1)}, f32[7,4,192]{2,1,0:T(4,128)S(1)}) custom-call(f32[7,4,384]{2,1,0:T(4,128)S(1)} %maximum_convert_fusion.weights_ref.refs_0_, f32[3,1024,128]{2,1,0:T(8,128)S(1)} %get-tuple-element.36.refs_1_, f32[3,1024,128]{2,1,0:T(8,128)S(1)} %get-tuple-element.37.refs_2_, ...), custom_call_target="tpu_custom_call", output_to_operand_aliasing={{0}: (6, {})} | custom-call | flops 5505024 | bytes 1769472 | tf_op jit(solution)/shard_map/feature_gradients/pallas_call | solution.py:783
  26.3 0.9 %collective-permute-done.5 = f32[7,4,192]{2,1,0:T(4,128)S(1)} collective-permute-done((f32[7,4,192]{2,1,0:T(4,128)S(1)}, f32[7,4,192]{2,1,0:T(4,128)S(1)}, u32[]{:S(2)}, u32[]{:S(2)}) %collective-permute-start.5) | collective-permute-done | bytes 21536 | tf_op jit(solution)/shard_map/ppermute | solution.py:54
  27.2 2.1 %collective-permute-start.6 = (f32[7,4,192]{2,1,0:T(4,128)S(1)}, f32[7,4,192]{2,1,0:T(4,128)S(1)}, u32[]{:S(2)}, u32[]{:S(2)}) collective-permute-start(f32[7,4,192]{2,1,0:T(4,128)S(1)} %add_add_fusion.1), channel_id=1, source_target_pairs={{0,8},{2,10},{4,12},{6,14},{8,0},{10,2},{12,4},{14,6},{16,24},{18,... | collective-permute-start | bytes 64520 | tf_op jit(solution)/shard_map/ppermute | solution.py:54
  29.3 1.5 %feature_gradients.6 = (bf16[3,128,3072]{2,1,0:T(8,128)(2,1)}, f32[7,4,192]{2,1,0:T(4,128)S(1)}) custom-call(f32[7,4,384]{2,1,0:T(4,128)S(1)} %maximum_convert_fusion.weights_ref.refs_0_, f32[3,1024,128]{2,1,0:T(8,128)S(1)} %get-tuple-element.36.refs_1_, f32[3,1024,128]{2,1,0:T(8,128)S(1)} %get-tuple-element.37.refs_2_, ...), custom_call_target="tpu_custom_call", output_to_operand_aliasing={{0}: (6, {})} | custom-call | flops 5505024 | bytes 1769472 | tf_op jit(solution)/shard_map/feature_gradients/pallas_call | solution.py:783
  30.8 0.4 %collective-permute-done.6 = f32[7,4,192]{2,1,0:T(4,128)S(1)} collective-permute-done((f32[7,4,192]{2,1,0:T(4,128)S(1)}, f32[7,4,192]{2,1,0:T(4,128)S(1)}, u32[]{:S(2)}, u32[]{:S(2)}) %collective-permute-start.6) | collective-permute-done | bytes 21536 | tf_op jit(solution)/shard_map/ppermute | solution.py:54
  31.2 3.1 %collective-permute-start.7 = (f32[7,4,192]{2,1,0:T(4,128)S(1)}, f32[7,4,192]{2,1,0:T(4,128)S(1)}, u32[]{:S(2)}, u32[]{:S(2)}) collective-permute-start(f32[7,4,192]{2,1,0:T(4,128)S(1)} %add_add_fusion), channel_id=1, source_target_pairs={{0,16},{2,18},{4,20},{6,22},{8,24},{10,26},{12,28},{14,30},{16,0},... | collective-permute-start | bytes 64520 | tf_op jit(solution)/shard_map/ppermute | solution.py:54
  34.2 1.7 %feature_gradients.7 = (bf16[3,128,3072]{2,1,0:T(8,128)(2,1)}, f32[7,4,192]{2,1,0:T(4,128)S(1)}) custom-call(f32[7,4,384]{2,1,0:T(4,128)S(1)} %maximum_convert_fusion.weights_ref.refs_0_, f32[3,1024,128]{2,1,0:T(8,128)S(1)} %get-tuple-element.36.refs_1_, f32[3,1024,128]{2,1,0:T(8,128)S(1)} %get-tuple-element.37.refs_2_, ...), custom_call_target="tpu_custom_call", output_to_operand_aliasing={{0}: (6, {})} | custom-call | flops 5505024 | bytes 1769472 | tf_op jit(solution)/shard_map/feature_gradients/pallas_call | solution.py:783
  36.0 0.1 collective-permute-done.7
  36.1 0.6 %multiply_bitcast_fusion = f32[4,7,192]{2,0,1:T(4,128)} fusion(f32[7,4,192]{2,1,0:T(4,128)S(1)} %get-tuple-element.66, f32[7,4,192]{2,1,0:T(4,128)S(1)} %add_add_fusion, f32[7,4,192]{2,1,0:T(4,128)S(1)} %collective-permute-done.7), kind=kLoop, calls=%fused_computation | loop fusion | flops 16128 | bytes 86016 | tf_op jit(solution)/shard_map/transpose | solution.py:850
  (4 shorter events, 0.1 us)
Async XLA Ops:
  0.6 5.4 %copy-start = (bf16[3,128,3072]{2,1,0:T(8,128)(2,1)S(1)}, bf16[3,128,3072]{2,1,0:T(8,128)(2,1)}, u32[]{:S(2)}) copy-start(bf16[3,128,3072]{2,1,0:T(8,128)(2,1)} %features_ref.1) | copy-start | bytes 7077892
  2.1 3.8 %collective-permute-start = (bf16[7,4,192]{2,1,0:T(4,128)(2,1)S(1)}, bf16[7,4,192]{2,1,0:T(4,128)(2,1)S(1)}, u32[]{:S(2)}, u32[]{:S(2)}) collective-permute-start(bf16[7,4,192]{2,1,0:T(4,128)(2,1)S(1)} %get-tuple-element.35), channel_id=1, source_target_pairs={{0,1},{1,0},{2,3},{3,2},{4,5},{5,4},{6,7},{7,6},{8,9},{9,8},{10,11... | collective-permute-start | bytes 32264 | tf_op jit(solution)/shard_map/ppermute | solution.py:40
  2.7 12.6 %collective-permute-start.1 = (bf16[864,128]{1,0:T(8,128)(2,1)S(1)}, bf16[864,128]{1,0:T(8,128)(2,1)S(1)}, u32[]{:S(2)}, u32[]{:S(2)}) collective-permute-start(bf16[864,128]{1,0:T(8,128)(2,1)S(1)} %get-tuple-element.39), channel_id=1, source_target_pairs={{0,2},{2,0},{4,6},{6,4},{8,10},{10,8},{12,14},{14,12},{16,18},{18,... | collective-permute-start | bytes 663560 | tf_op jit(solution)/shard_map/ppermute | solution.py:28
  5.2 10.0 %collective-permute-start.2 = (bf16[864,128]{1,0:T(8,128)(2,1)S(1)}, bf16[864,128]{1,0:T(8,128)(2,1)S(1)}, u32[]{:S(2)}, u32[]{:S(2)}) collective-permute-start(bf16[864,128]{1,0:T(8,128)(2,1)S(1)} %get-tuple-element.40), channel_id=1, source_target_pairs={{2,4},{4,2},{6,8},{8,6},{10,12},{12,10},{14,16},{16,14},{18,20},{2... | collective-permute-start | bytes 663560 | tf_op jit(solution)/shard_map/ppermute | solution.py:27
  16.3 1.3 %collective-permute-start.3 = (f32[7,4,192]{2,1,0:T(4,128)S(1)}, f32[7,4,192]{2,1,0:T(4,128)S(1)}, u32[]{:S(2)}, u32[]{:S(2)}) collective-permute-start(f32[7,4,192]{2,1,0:T(4,128)S(1)} %slice_select_fusion), channel_id=1, source_target_pairs={{0,1},{1,0},{2,3},{3,2},{4,5},{5,4},{6,7},{7,6},{8,9},{9,8},{10,11... | collective-permute-start | bytes 64520 | tf_op jit(solution)/shard_map/ppermute | solution.py:71
  17.6 5.6 %collective-permute-start.4 = (f32[7,4,192]{2,1,0:T(4,128)S(1)}, f32[7,4,192]{2,1,0:T(4,128)S(1)}, u32[]{:S(2)}, u32[]{:S(2)}) collective-permute-start(f32[7,4,192]{2,1,0:T(4,128)S(1)} %add_add_fusion.3), channel_id=1, source_target_pairs={{0,2},{2,0},{4,6},{6,4},{8,10},{10,8},{12,14},{14,12},{16,18},{18,... | collective-permute-start | bytes 64520 | tf_op jit(solution)/shard_map/ppermute | solution.py:54
  23.3 3.9 %collective-permute-start.5 = (f32[7,4,192]{2,1,0:T(4,128)S(1)}, f32[7,4,192]{2,1,0:T(4,128)S(1)}, u32[]{:S(2)}, u32[]{:S(2)}) collective-permute-start(f32[7,4,192]{2,1,0:T(4,128)S(1)} %add_add_fusion.2), channel_id=1, source_target_pairs={{0,4},{2,6},{4,0},{6,2},{8,12},{10,14},{12,8},{14,10},{16,20},{18,... | collective-permute-start | bytes 64520 | tf_op jit(solution)/shard_map/ppermute | solution.py:54
  27.2 3.9 %collective-permute-start.6 = (f32[7,4,192]{2,1,0:T(4,128)S(1)}, f32[7,4,192]{2,1,0:T(4,128)S(1)}, u32[]{:S(2)}, u32[]{:S(2)}) collective-permute-start(f32[7,4,192]{2,1,0:T(4,128)S(1)} %add_add_fusion.1), channel_id=1, source_target_pairs={{0,8},{2,10},{4,12},{6,14},{8,0},{10,2},{12,4},{14,6},{16,24},{18,... | collective-permute-start | bytes 64520 | tf_op jit(solution)/shard_map/ppermute | solution.py:54
  31.2 4.9 %collective-permute-start.7 = (f32[7,4,192]{2,1,0:T(4,128)S(1)}, f32[7,4,192]{2,1,0:T(4,128)S(1)}, u32[]{:S(2)}, u32[]{:S(2)}) collective-permute-start(f32[7,4,192]{2,1,0:T(4,128)S(1)} %add_add_fusion), channel_id=1, source_target_pairs={{0,16},{2,18},{4,20},{6,22},{8,24},{10,26},{12,28},{14,30},{16,0},... | collective-permute-start | bytes 64520 | tf_op jit(solution)/shard_map/ppermute | solution.py:54

commit v8 on v7

--- a/solution.py
+++ b/solution.py
@@ -483,7 +483,6 @@
     gtail_ref,
     after_ref,
     sums_ref,
-    acc,
     before_s,
     kc_s,
     vc_s,
@@ -492,16 +491,17 @@
 ):
     reach = taps - 1
     groups = weights_ref.shape[2]
-    acc[...] = sums_in_ref[...]
     even = is_even("ctx")
     columns = groups // LANES
     near, far = near_ref[...].astype(F32), far_ref[...].astype(F32)
     before_s[...] = jnp.where(even, far, near)
     after_ref[...] = jnp.where(even, near, far)
-    kc_t, vc_t, p_t, gm_t = (Tokens(ref, repeats, PAD) for ref in (kc_s, vc_s, p_s, gm_s))
-
-    def column_step(column, carry):
-        lanes = lane_slice(column)
+
+    for column in range(columns):
+        lanes = slice(column * LANES, (column + 1) * LANES)
+        kc_t, vc_t, p_t, gm_t = (
+            Tokens(ref, repeats, reach, (column,)) for ref in (kc_s, vc_s, p_s, gm_s)
+        )
         wq, wk, wv, wm = (weight_rows(weights_ref, bank, lanes) for bank in range(4))
         q_t, k_t, v_t, c_t, kc_i, vc_i, p_i, gm_i = (
             Held(ref, repeats, column, span)
@@ -563,12 +563,9 @@
             gv_o[token] = gv
             sums.add(1, gk, k_w.back(token, taps))
             sums.add(2, gv, v_w.back(token, taps))
-        sums.store(acc, lanes)
-        return carry
-
-    lax.fori_loop(0, groups // LANES, column_step, 0)
-    for bank in range(sums_ref.shape[1]):
-        sums_ref[:, bank, :] = jnp.sum(acc[bank], axis=1)
+        for (bank, lag), value in sums.held.items():
+            total = sums_in_ref[bank, lag, :, lanes] + value
+            sums_ref[lag, bank : bank + 1, lanes] = jnp.sum(total, axis=0, keepdims=True)
 
 
 def edge(weights, near, far, sums, arrays):
@@ -588,10 +585,9 @@
         in_specs=[VMEM_SPEC] * 12,
         out_specs=(VMEM_SPEC,) * 5,
         scratch_shapes=[
-            pltpu.VMEM(sums.shape, F32),
             pltpu.VMEM(near.shape, F32),
         ]
-        + [pltpu.VMEM((2 * PAD * repeats, LANES), F32) for _ in range(4)],
+        + [pltpu.VMEM((columns, 3 * reach * repeats, LANES), F32) for _ in range(4)],
         cost_estimate=pl.CostEstimate(
             flops=10**7, bytes_accessed=4 * 10**6, transcendentals=0
         ),

time: 36.9 us -> 36.9 us (level)
  no operation moved by 1% of the time
where the time goes in v8:
time: 36.9 us; the launch traced here: 36.7 us
  Pallas kernels  17.6 us (48%)
  starting transfers between devices  14.3 us (39%)
  waiting for transfers between devices  3.07 us (8%)
  other arithmetic  0.93 us (3%)
  between operations  0.76 us (2%)
    ppermute x4, starting transfers between devices, sum_over(): received = lax.ppermute(value, axis, pairs)  10.5 us
    pallas_call x1, Pallas kernels, interior(): pl.pallas_call(functools.partial(interior_kernel, taps, repeats), out_sha...  8.69 us
    pallas_call x4, Pallas kernels, feature_gradients(): pl.pallas_call(functools.partial(grads_kernel, taps, repeats, first, step...  6.14 us
    ppermute x1, starting transfers between devices, swap_pairs(): near = lax.ppermute(near, axis, inner)  2.56 us
    ppermute x4, waiting for transfers between devices, sum_over(): received = lax.ppermute(value, axis, pairs)  1.76 us
    pallas_call x1, Pallas kernels, pack(): pl.pallas_call(functools.partial(pack_kernel, reach, groups // LANES), ou...  1.49 us
    pallas_call x1, Pallas kernels, edge(): pl.pallas_call(functools.partial(edge_kernel, taps, repeats), out_shape=(...  0.87 us
    ppermute x1, waiting for transfers between devices, sum_scatter(): sent = lax.ppermute(jnp.where(first, high, low), axis, [(0, 1), (1, 0)])  0.76 us
  transfers between devices with their start and end apart: 8, of which 6 were waited for; matrix products, arithmetic and copies ran while one was open for 0% of the time, Pallas kernels for 42%

profile of v8, /device:TPU:0, one launch (start us, length us, event | category | flops | bytes accessed | tf_op | source)
XLA Modules:
  0.0 36.7 jit_solution(953898988522280157)
XLA Ops:
  0.6 0.0 copy-start
  0.6 1.5 %pack_halos.1 = (bf16[864,128]{1,0:T(8,128)(2,1)S(1)}, bf16[864,128]{1,0:T(8,128)(2,1)S(1)}, bf16[7,4,192]{2,1,0:T(4,128)(2,1)S(1)}) custom-call(bf16[3,128,3072]{2,1,0:T(8,128)(2,1)} %features_ref.1, bf16[128,3072]{1,0:T(8,128)(2,1)} %cotangent_hbm.3, f32[7,4,192]{2,1,0:T(4,128)} %bitcast.3), custom_call_target="tpu_custom_call" | custom-call | flops 1000000 | bytes 1000000 | tf_op jit(solution)/shard_map/pack_halos/pallas_call | solution.py:279
  2.1 0.5 %collective-permute-start = (bf16[7,4,192]{2,1,0:T(4,128)(2,1)S(1)}, bf16[7,4,192]{2,1,0:T(4,128)(2,1)S(1)}, u32[]{:S(2)}, u32[]{:S(2)}) collective-permute-start(bf16[7,4,192]{2,1,0:T(4,128)(2,1)S(1)} %get-tuple-element.35), channel_id=1, source_target_pairs={{0,1},{1,0},{2,3},{3,2},{4,5},{5,4},{6,7},{7,6},{8,9},{9,8},{10,11... | collective-permute-start | bytes 32264 | tf_op jit(solution)/shard_map/ppermute | solution.py:40
  2.7 2.6 %collective-permute-start.1 = (bf16[864,128]{1,0:T(8,128)(2,1)S(1)}, bf16[864,128]{1,0:T(8,128)(2,1)S(1)}, u32[]{:S(2)}, u32[]{:S(2)}) collective-permute-start(bf16[864,128]{1,0:T(8,128)(2,1)S(1)} %get-tuple-element.39), channel_id=1, source_target_pairs={{0,2},{2,0},{4,6},{6,4},{8,10},{10,8},{12,14},{14,12},{16,18},{18,... | collective-permute-start | bytes 663560 | tf_op jit(solution)/shard_map/ppermute | solution.py:28
  5.2 0.7 %collective-permute-start.2 = (bf16[864,128]{1,0:T(8,128)(2,1)S(1)}, bf16[864,128]{1,0:T(8,128)(2,1)S(1)}, u32[]{:S(2)}, u32[]{:S(2)}) collective-permute-start(bf16[864,128]{1,0:T(8,128)(2,1)S(1)} %get-tuple-element.40), channel_id=1, source_target_pairs={{2,4},{4,2},{6,8},{8,6},{10,12},{12,10},{14,16},{16,14},{18,20},{2... | collective-permute-start | bytes 663560 | tf_op jit(solution)/shard_map/ppermute | solution.py:27
  5.9 0.0 collective-permute-done
  5.9 0.1 maximum_convert_fusion.weights_ref.refs_0_
  6.0 0.0 copy-done
  6.0 8.7 %interior.1 = (f32[3,1024,128]{2,1,0:T(8,128)S(1)}, f32[3,1024,128]{2,1,0:T(8,128)S(1)}, f32[3,1024,128]{2,1,0:T(8,128)S(1)}, f32[3,1024,128]{2,1,0:T(8,128)S(1)...) custom-call(bf16[3,128,3072]{2,1,0:T(8,128)(2,1)S(1)} %copy-done, ...), custom_call_target="tpu_custom_call" | custom-call | flops 49545216 | bytes 8650752 | tf_op jit(solution)/shard_map/interior/pallas_call | solution.py:443
  14.7 0.5 %collective-permute-done.1.near_ref = bf16[864,128]{1,0:T(8,128)(2,1)S(1)} collective-permute-done((bf16[864,128]{1,0:T(8,128)(2,1)S(1)}, bf16[864,128]{1,0:T(8,128)(2,1)S(1)}, u32[]{:S(2)}, u32[]{:S(2)}) %collective-permute-start.1) | collective-permute-done | bytes 221216 | tf_op jit(solution)/shard_map/ppermute | solution.py:28
  15.3 0.0 collective-permute-done.2.far_ref
  15.3 0.9 %edge.1 = (f32[3,96,128]{2,1,0:T(8,128)S(1)}, f32[3,3,96,128]{3,2,1,0:T(8,128)S(1)}, f32[2,3,48,128]{3,2,1,0:T(8,128)S(1)}, f32[864,128]{1,0:T(8,128)S(1)}, f32[7,4,384]{2,1,0:T(4,128)S(1)}) custom-call(f32[7,4,384]{2,1,0:T(4,128)S(1)} %maximum_convert_fusion.weights_ref.refs_0_, bf16[864,128]{1,0:T(8,128)(2,1)S(1)} %collective-permute-done.1.near_ref, ...), custom_call_target="tpu_custom_call" | custom-call | flops 10000000 | bytes 4000000 | tf_op jit(solution)/shard_map/edge/pallas_call | solution.py:576
  16.1 0.1 slice_select_fusion
  16.2 0.1 collective-permute-start.3
  16.3 0.4 %round_mixed.1 = (bf16[128,3072]{1,0:T(8,128)(2,1)S(1)}, f32[7,4,192]{2,1,0:T(4,128)S(1)}) custom-call(f32[3,1024,128]{2,1,0:T(8,128)S(1)} %get-tuple-element.52.middle, f32[3,96,128]{2,1,0:T(8,128)S(1)} %get-tuple-element.53.top), custom_call_target="tpu_custom_call" | custom-call | flops 393216 | bytes 2359296 | tf_op jit(solution)/shard_map/round_mixed/pallas_call | solution.py:631
  16.7 0.8 %collective-permute-done.3 = f32[7,4,192]{2,1,0:T(4,128)S(1)} collective-permute-done((f32[7,4,192]{2,1,0:T(4,128)S(1)}, f32[7,4,192]{2,1,0:T(4,128)S(1)}, u32[]{:S(2)}, u32[]{:S(2)}) %collective-permute-start.3) | collective-permute-done | bytes 21536 | tf_op jit(solution)/shard_map/ppermute | solution.py:71
  17.5 0.1 add_add_fusion.3
  17.6 3.8 %collective-permute-start.4 = (f32[7,4,192]{2,1,0:T(4,128)S(1)}, f32[7,4,192]{2,1,0:T(4,128)S(1)}, u32[]{:S(2)}, u32[]{:S(2)}) collective-permute-start(f32[7,4,192]{2,1,0:T(4,128)S(1)} %add_add_fusion.3), channel_id=1, source_target_pairs={{0,2},{2,0},{4,6},{6,4},{8,10},{10,8},{12,14},{14,12},{16,18},{18,... | collective-permute-start | bytes 64520 | tf_op jit(solution)/shard_map/ppermute | solution.py:54
  21.3 1.5 %feature_gradients.4 = (bf16[3,128,3072]{2,1,0:T(8,128)(2,1)}, f32[7,4,192]{2,1,0:T(4,128)S(1)}, bf16[128,3072]{1,0:T(8,128)(2,1)}) custom-call(f32[7,4,384]{2,1,0:T(4,128)S(1)} %maximum_convert_fusion.weights_ref.refs_0_, f32[3,1024,128]{2,1,0:T(8,128)S(1)} %get-tuple-element.36.refs_1_, f32[3,1024,128]{2,1,0:T(8,128)S(1)} %get-tuple-element.37.refs_2_, ...), custom_call_target="tpu_custom_call" | custom-call | flops 5505024 | bytes 1769472 | tf_op jit(solution)/shard_map/feature_gradients/pallas_call | solution.py:779
  22.8 0.4 %collective-permute-done.4 = f32[7,4,192]{2,1,0:T(4,128)S(1)} collective-permute-done((f32[7,4,192]{2,1,0:T(4,128)S(1)}, f32[7,4,192]{2,1,0:T(4,128)S(1)}, u32[]{:S(2)}, u32[]{:S(2)}) %collective-permute-start.4) | collective-permute-done | bytes 21536 | tf_op jit(solution)/shard_map/ppermute | solution.py:54
  23.2 1.6 %collective-permute-start.5 = (f32[7,4,192]{2,1,0:T(4,128)S(1)}, f32[7,4,192]{2,1,0:T(4,128)S(1)}, u32[]{:S(2)}, u32[]{:S(2)}) collective-permute-start(f32[7,4,192]{2,1,0:T(4,128)S(1)} %add_add_fusion.2), channel_id=1, source_target_pairs={{0,4},{2,6},{4,0},{6,2},{8,12},{10,14},{12,8},{14,10},{16,20},{18,... | collective-permute-start | bytes 64520 | tf_op jit(solution)/shard_map/ppermute | solution.py:54
  24.8 1.5 %feature_gradients.5 = (bf16[3,128,3072]{2,1,0:T(8,128)(2,1)}, f32[7,4,192]{2,1,0:T(4,128)S(1)}) custom-call(f32[7,4,384]{2,1,0:T(4,128)S(1)} %maximum_convert_fusion.weights_ref.refs_0_, f32[3,1024,128]{2,1,0:T(8,128)S(1)} %get-tuple-element.36.refs_1_, f32[3,1024,128]{2,1,0:T(8,128)S(1)} %get-tuple-element.37.refs_2_, ...), custom_call_target="tpu_custom_call", output_to_operand_aliasing={{0}: (6, {})} | custom-call | flops 5505024 | bytes 1769472 | tf_op jit(solution)/shard_map/feature_gradients/pallas_call | solution.py:779
  26.3 0.9 %collective-permute-done.5 = f32[7,4,192]{2,1,0:T(4,128)S(1)} collective-permute-done((f32[7,4,192]{2,1,0:T(4,128)S(1)}, f32[7,4,192]{2,1,0:T(4,128)S(1)}, u32[]{:S(2)}, u32[]{:S(2)}) %collective-permute-start.5) | collective-permute-done | bytes 21536 | tf_op jit(solution)/shard_map/ppermute | solution.py:54
  27.2 2.1 %collective-permute-start.6 = (f32[7,4,192]{2,1,0:T(4,128)S(1)}, f32[7,4,192]{2,1,0:T(4,128)S(1)}, u32[]{:S(2)}, u32[]{:S(2)}) collective-permute-start(f32[7,4,192]{2,1,0:T(4,128)S(1)} %add_add_fusion.1), channel_id=1, source_target_pairs={{0,8},{2,10},{4,12},{6,14},{8,0},{10,2},{12,4},{14,6},{16,24},{18,... | collective-permute-start | bytes 64520 | tf_op jit(solution)/shard_map/ppermute | solution.py:54
  29.2 1.5 %feature_gradients.6 = (bf16[3,128,3072]{2,1,0:T(8,128)(2,1)}, f32[7,4,192]{2,1,0:T(4,128)S(1)}) custom-call(f32[7,4,384]{2,1,0:T(4,128)S(1)} %maximum_convert_fusion.weights_ref.refs_0_, f32[3,1024,128]{2,1,0:T(8,128)S(1)} %get-tuple-element.36.refs_1_, f32[3,1024,128]{2,1,0:T(8,128)S(1)} %get-tuple-element.37.refs_2_, ...), custom_call_target="tpu_custom_call", output_to_operand_aliasing={{0}: (6, {})} | custom-call | flops 5505024 | bytes 1769472 | tf_op jit(solution)/shard_map/feature_gradients/pallas_call | solution.py:779
  30.7 0.4 %collective-permute-done.6 = f32[7,4,192]{2,1,0:T(4,128)S(1)} collective-permute-done((f32[7,4,192]{2,1,0:T(4,128)S(1)}, f32[7,4,192]{2,1,0:T(4,128)S(1)}, u32[]{:S(2)}, u32[]{:S(2)}) %collective-permute-start.6) | collective-permute-done | bytes 21536 | tf_op jit(solution)/shard_map/ppermute | solution.py:54
  31.1 3.1 %collective-permute-start.7 = (f32[7,4,192]{2,1,0:T(4,128)S(1)}, f32[7,4,192]{2,1,0:T(4,128)S(1)}, u32[]{:S(2)}, u32[]{:S(2)}) collective-permute-start(f32[7,4,192]{2,1,0:T(4,128)S(1)} %add_add_fusion), channel_id=1, source_target_pairs={{0,16},{2,18},{4,20},{6,22},{8,24},{10,26},{12,28},{14,30},{16,0},... | collective-permute-start | bytes 64520 | tf_op jit(solution)/shard_map/ppermute | solution.py:54
  34.2 1.7 %feature_gradients.7 = (bf16[3,128,3072]{2,1,0:T(8,128)(2,1)}, f32[7,4,192]{2,1,0:T(4,128)S(1)}) custom-call(f32[7,4,384]{2,1,0:T(4,128)S(1)} %maximum_convert_fusion.weights_ref.refs_0_, f32[3,1024,128]{2,1,0:T(8,128)S(1)} %get-tuple-element.36.refs_1_, f32[3,1024,128]{2,1,0:T(8,128)S(1)} %get-tuple-element.37.refs_2_, ...), custom_call_target="tpu_custom_call", output_to_operand_aliasing={{0}: (6, {})} | custom-call | flops 5505024 | bytes 1769472 | tf_op jit(solution)/shard_map/feature_gradients/pallas_call | solution.py:779
  35.9 0.1 collective-permute-done.7
  36.0 0.6 %multiply_bitcast_fusion = f32[4,7,192]{2,0,1:T(4,128)} fusion(f32[7,4,192]{2,1,0:T(4,128)S(1)} %get-tuple-element.66, f32[7,4,192]{2,1,0:T(4,128)S(1)} %add_add_fusion, f32[7,4,192]{2,1,0:T(4,128)S(1)} %collective-permute-done.7), kind=kLoop, calls=%fused_computation | loop fusion | flops 16128 | bytes 86016 | tf_op jit(solution)/shard_map/transpose | solution.py:846
  (4 shorter events, 0.1 us)
Async XLA Ops:
  0.6 5.4 %copy-start = (bf16[3,128,3072]{2,1,0:T(8,128)(2,1)S(1)}, bf16[3,128,3072]{2,1,0:T(8,128)(2,1)}, u32[]{:S(2)}) copy-start(bf16[3,128,3072]{2,1,0:T(8,128)(2,1)} %features_ref.1) | copy-start | bytes 7077892
  2.1 3.8 %collective-permute-start = (bf16[7,4,192]{2,1,0:T(4,128)(2,1)S(1)}, bf16[7,4,192]{2,1,0:T(4,128)(2,1)S(1)}, u32[]{:S(2)}, u32[]{:S(2)}) collective-permute-start(bf16[7,4,192]{2,1,0:T(4,128)(2,1)S(1)} %get-tuple-element.35), channel_id=1, source_target_pairs={{0,1},{1,0},{2,3},{3,2},{4,5},{5,4},{6,7},{7,6},{8,9},{9,8},{10,11... | collective-permute-start | bytes 32264 | tf_op jit(solution)/shard_map/ppermute | solution.py:40
  2.7 12.6 %collective-permute-start.1 = (bf16[864,128]{1,0:T(8,128)(2,1)S(1)}, bf16[864,128]{1,0:T(8,128)(2,1)S(1)}, u32[]{:S(2)}, u32[]{:S(2)}) collective-permute-start(bf16[864,128]{1,0:T(8,128)(2,1)S(1)} %get-tuple-element.39), channel_id=1, source_target_pairs={{0,2},{2,0},{4,6},{6,4},{8,10},{10,8},{12,14},{14,12},{16,18},{18,... | collective-permute-start | bytes 663560 | tf_op jit(solution)/shard_map/ppermute | solution.py:28
  5.2 10.0 %collective-permute-start.2 = (bf16[864,128]{1,0:T(8,128)(2,1)S(1)}, bf16[864,128]{1,0:T(8,128)(2,1)S(1)}, u32[]{:S(2)}, u32[]{:S(2)}) collective-permute-start(bf16[864,128]{1,0:T(8,128)(2,1)S(1)} %get-tuple-element.40), channel_id=1, source_target_pairs={{2,4},{4,2},{6,8},{8,6},{10,12},{12,10},{14,16},{16,14},{18,20},{2... | collective-permute-start | bytes 663560 | tf_op jit(solution)/shard_map/ppermute | solution.py:27
  16.2 1.3 %collective-permute-start.3 = (f32[7,4,192]{2,1,0:T(4,128)S(1)}, f32[7,4,192]{2,1,0:T(4,128)S(1)}, u32[]{:S(2)}, u32[]{:S(2)}) collective-permute-start(f32[7,4,192]{2,1,0:T(4,128)S(1)} %slice_select_fusion), channel_id=1, source_target_pairs={{0,1},{1,0},{2,3},{3,2},{4,5},{5,4},{6,7},{7,6},{8,9},{9,8},{10,11... | collective-permute-start | bytes 64520 | tf_op jit(solution)/shard_map/ppermute | solution.py:71
  17.6 5.6 %collective-permute-start.4 = (f32[7,4,192]{2,1,0:T(4,128)S(1)}, f32[7,4,192]{2,1,0:T(4,128)S(1)}, u32[]{:S(2)}, u32[]{:S(2)}) collective-permute-start(f32[7,4,192]{2,1,0:T(4,128)S(1)} %add_add_fusion.3), channel_id=1, source_target_pairs={{0,2},{2,0},{4,6},{6,4},{8,10},{10,8},{12,14},{14,12},{16,18},{18,... | collective-permute-start | bytes 64520 | tf_op jit(solution)/shard_map/ppermute | solution.py:54
  23.2 3.9 %collective-permute-start.5 = (f32[7,4,192]{2,1,0:T(4,128)S(1)}, f32[7,4,192]{2,1,0:T(4,128)S(1)}, u32[]{:S(2)}, u32[]{:S(2)}) collective-permute-start(f32[7,4,192]{2,1,0:T(4,128)S(1)} %add_add_fusion.2), channel_id=1, source_target_pairs={{0,4},{2,6},{4,0},{6,2},{8,12},{10,14},{12,8},{14,10},{16,20},{18,... | collective-permute-start | bytes 64520 | tf_op jit(solution)/shard_map/ppermute | solution.py:54
  27.2 3.9 %collective-permute-start.6 = (f32[7,4,192]{2,1,0:T(4,128)S(1)}, f32[7,4,192]{2,1,0:T(4,128)S(1)}, u32[]{:S(2)}, u32[]{:S(2)}) collective-permute-start(f32[7,4,192]{2,1,0:T(4,128)S(1)} %add_add_fusion.1), channel_id=1, source_target_pairs={{0,8},{2,10},{4,12},{6,14},{8,0},{10,2},{12,4},{14,6},{16,24},{18,... | collective-permute-start | bytes 64520 | tf_op jit(solution)/shard_map/ppermute | solution.py:54
  31.1 4.9 %collective-permute-start.7 = (f32[7,4,192]{2,1,0:T(4,128)S(1)}, f32[7,4,192]{2,1,0:T(4,128)S(1)}, u32[]{:S(2)}, u32[]{:S(2)}) collective-permute-start(f32[7,4,192]{2,1,0:T(4,128)S(1)} %add_add_fusion), channel_id=1, source_target_pairs={{0,16},{2,18},{4,20},{6,22},{8,24},{10,26},{12,28},{14,30},{16,0},... | collective-permute-start | bytes 64520 | tf_op jit(solution)/shard_map/ppermute | solution.py:54

commit v9 on v8

--- a/solution.py
+++ b/solution.py
@@ -58,18 +58,16 @@
     return value, rounds
 
 
-def sum_scatter(value, axis):
-    size = lax.axis_size(axis)
-    portion = value.shape[-1] // size
-    if size != 2:
-        total, _ = sum_over(value, axis)
-        return lax.dynamic_slice_in_dim(
-            total, lax.axis_index(axis) * portion, portion, value.ndim - 1
-        )
-    first = lax.axis_index(axis) == 0
-    low, high = value[..., :portion], value[..., portion:]
-    sent = lax.ppermute(jnp.where(first, high, low), axis, [(0, 1), (1, 0)])
-    return jnp.where(first, low, high) + sent
+def sum_scatter(parts, axis):
+    if len(parts) == 2:
+        kept, sent = parts
+        return kept + lax.ppermute(sent, axis, [(0, 1), (1, 0)])
+    (value,) = parts
+    portion = value.shape[-1] // lax.axis_size(axis)
+    total, _ = sum_over(value, axis)
+    return lax.dynamic_slice_in_dim(
+        total, lax.axis_index(axis) * portion, portion, value.ndim - 1
+    )
 
 
 def dot_taps(weights, pieces):
@@ -482,13 +480,9 @@
     ghead_ref,
     gtail_ref,
     after_ref,
-    sums_ref,
-    before_s,
-    kc_s,
-    vc_s,
-    p_s,
-    gm_s,
+    *refs,
 ):
+    *sums_out, sums_ref, before_s, kc_s, vc_s, p_s, gm_s = refs
     reach = taps - 1
     groups = weights_ref.shape[2]
     even = is_even("ctx")
@@ -566,6 +560,13 @@
         for (bank, lag), value in sums.held.items():
             total = sums_in_ref[bank, lag, :, lanes] + value
             sums_ref[lag, bank : bank + 1, lanes] = jnp.sum(total, axis=0, keepdims=True)
+    if len(sums_out) == 1:
+        sums_out[0][...] = sums_ref[...]
+    else:
+        low, high = sums_ref[:, :, : groups // 2], sums_ref[:, :, groups // 2 :]
+        first = lax.axis_index("fsdp") == 0
+        sums_out[0][...] = jnp.where(first, low, high)
+        sums_out[1][...] = jnp.where(first, high, low)
 
 
 def edge(weights, near, far, sums, arrays):
@@ -573,6 +574,7 @@
     columns = groups // LANES
     reach = taps - 1
     repeats = near.shape[0] // (6 * reach * columns)
+    parts = 2 if lax.axis_size("fsdp") == 2 else 1
     return pl.pallas_call(
         functools.partial(edge_kernel, taps, repeats),
         out_shape=(
@@ -580,11 +582,12 @@
             jax.ShapeDtypeStruct((3, columns, 2 * reach * repeats, LANES), F32),
             jax.ShapeDtypeStruct((2, columns, reach * repeats, LANES), F32),
             jax.ShapeDtypeStruct(near.shape, F32),
-            jax.ShapeDtypeStruct((taps, banks, groups), F32),
+            *[jax.ShapeDtypeStruct((taps, banks, groups // parts), F32)] * parts,
         ),
         in_specs=[VMEM_SPEC] * 12,
-        out_specs=(VMEM_SPEC,) * 5,
+        out_specs=(VMEM_SPEC,) * (4 + parts),
         scratch_shapes=[
+            pltpu.VMEM((taps, banks, groups), F32),
             pltpu.VMEM(near.shape, F32),
         ]
         + [pltpu.VMEM((columns, 3 * reach * repeats, LANES), F32) for _ in range(4)],
@@ -809,11 +812,12 @@
     weights = gather_filters(rounded, "fsdp").astype(F32)
     halos = swap_pairs(near, far, "ctx")
     middle, grads, arrays, sums = interior(features, cotangent, weights)
-    top, ghead, gtail, after, sums = edge(weights, *halos, sums, arrays)
+    top, ghead, gtail, after, *sums = edge(weights, *halos, sums, arrays)
     repeats = features.shape[2] // weights.shape[2]
     pieces = PIECES if (length // CHUNK) % PIECES == 0 else 1
-    portion = sums.shape[2] // lax.axis_size("fsdp")
-    zero = jax.ShapeDtypeStruct((*sums.shape[:2], portion), F32)
+    zero = jax.ShapeDtypeStruct(
+        (*weights.shape[:2], weights.shape[2] // lax.axis_size("fsdp")), F32
+    )
     whole, nothing = round_mixed(middle, top, cotangent, zero)
     owned = sum_scatter(sums, "fsdp") + nothing
     made = {"grads": None}

time: 36.9 us -> 36.8 us (level)
  no operation moved by 1% of the time
where the time goes in v9:
time: 36.8 us; the launch traced here: 36.6 us
  Pallas kernels  17.7 us (48%)
  starting transfers between devices  14.3 us (39%)
  waiting for transfers between devices  3.07 us (8%)
  other arithmetic  0.78 us (2%)
  between operations  0.75 us (2%)
    ppermute x4, starting transfers between devices, sum_over(): received = lax.ppermute(value, axis, pairs)  10.5 us
    pallas_call x1, Pallas kernels, interior(): pl.pallas_call(functools.partial(interior_kernel, taps, repeats), out_sha...  8.69 us
    pallas_call x4, Pallas kernels, feature_gradients(): pl.pallas_call(functools.partial(grads_kernel, taps, repeats, first, step...  6.14 us
    ppermute x1, starting transfers between devices, swap_pairs(): near = lax.ppermute(near, axis, inner)  2.56 us
    ppermute x4, waiting for transfers between devices, sum_over(): received = lax.ppermute(value, axis, pairs)  1.76 us
    pallas_call x1, Pallas kernels, pack(): pl.pallas_call(functools.partial(pack_kernel, reach, groups // LANES), ou...  1.49 us
    pallas_call x1, Pallas kernels, edge(): pl.pallas_call(functools.partial(edge_kernel, taps, repeats), out_shape=(...  0.98 us
    ppermute x1, waiting for transfers between devices, sum_scatter(): return kept + lax.ppermute(sent, axis, [(0, 1), (1, 0)])  0.76 us
  transfers between devices with their start and end apart: 8, of which 6 were waited for; matrix products, arithmetic and copies ran while one was open for 0% of the time, Pallas kernels for 42%

profile of v9, /device:TPU:0, one launch (start us, length us, event | category | flops | bytes accessed | tf_op | source)
XLA Modules:
  0.0 36.6 jit_solution(9008879028489368073)
XLA Ops:
  0.6 0.0 copy-start
  0.6 1.5 %pack_halos.1 = (bf16[864,128]{1,0:T(8,128)(2,1)S(1)}, bf16[864,128]{1,0:T(8,128)(2,1)S(1)}, bf16[7,4,192]{2,1,0:T(4,128)(2,1)S(1)}) custom-call(bf16[3,128,3072]{2,1,0:T(8,128)(2,1)} %features_ref.1, bf16[128,3072]{1,0:T(8,128)(2,1)} %cotangent_hbm.3, f32[7,4,192]{2,1,0:T(4,128)} %bitcast.3), custom_call_target="tpu_custom_call" | custom-call | flops 1000000 | bytes 1000000 | tf_op jit(solution)/shard_map/pack_halos/pallas_call | solution.py:277
  2.1 0.5 %collective-permute-start = (bf16[7,4,192]{2,1,0:T(4,128)(2,1)S(1)}, bf16[7,4,192]{2,1,0:T(4,128)(2,1)S(1)}, u32[]{:S(2)}, u32[]{:S(2)}) collective-permute-start(bf16[7,4,192]{2,1,0:T(4,128)(2,1)S(1)} %get-tuple-element.36), channel_id=1, source_target_pairs={{0,1},{1,0},{2,3},{3,2},{4,5},{5,4},{6,7},{7,6},{8,9},{9,8},{10,11... | collective-permute-start | bytes 32264 | tf_op jit(solution)/shard_map/ppermute | solution.py:40
  2.7 2.6 %collective-permute-start.1 = (bf16[864,128]{1,0:T(8,128)(2,1)S(1)}, bf16[864,128]{1,0:T(8,128)(2,1)S(1)}, u32[]{:S(2)}, u32[]{:S(2)}) collective-permute-start(bf16[864,128]{1,0:T(8,128)(2,1)S(1)} %get-tuple-element.40), channel_id=1, source_target_pairs={{0,2},{2,0},{4,6},{6,4},{8,10},{10,8},{12,14},{14,12},{16,18},{18,... | collective-permute-start | bytes 663560 | tf_op jit(solution)/shard_map/ppermute | solution.py:28
  5.2 0.7 %collective-permute-start.2 = (bf16[864,128]{1,0:T(8,128)(2,1)S(1)}, bf16[864,128]{1,0:T(8,128)(2,1)S(1)}, u32[]{:S(2)}, u32[]{:S(2)}) collective-permute-start(bf16[864,128]{1,0:T(8,128)(2,1)S(1)} %get-tuple-element.41), channel_id=1, source_target_pairs={{2,4},{4,2},{6,8},{8,6},{10,12},{12,10},{14,16},{16,14},{18,20},{2... | collective-permute-start | bytes 663560 | tf_op jit(solution)/shard_map/ppermute | solution.py:27
  5.9 0.0 collective-permute-done
  5.9 0.1 maximum_convert_fusion.weights_ref.refs_0_
  6.0 0.0 copy-done
  6.0 8.7 %interior.1 = (f32[3,1024,128]{2,1,0:T(8,128)S(1)}, f32[3,1024,128]{2,1,0:T(8,128)S(1)}, f32[3,1024,128]{2,1,0:T(8,128)S(1)}, f32[3,1024,128]{2,1,0:T(8,128)S(1)...) custom-call(bf16[3,128,3072]{2,1,0:T(8,128)(2,1)S(1)} %copy-done, ...), custom_call_target="tpu_custom_call" | custom-call | flops 49545216 | bytes 8650752 | tf_op jit(solution)/shard_map/interior/pallas_call | solution.py:441
  14.7 0.5 %collective-permute-done.1.near_ref = bf16[864,128]{1,0:T(8,128)(2,1)S(1)} collective-permute-done((bf16[864,128]{1,0:T(8,128)(2,1)S(1)}, bf16[864,128]{1,0:T(8,128)(2,1)S(1)}, u32[]{:S(2)}, u32[]{:S(2)}) %collective-permute-start.1) | collective-permute-done | bytes 221216 | tf_op jit(solution)/shard_map/ppermute | solution.py:28
  15.3 0.0 collective-permute-done.2.far_ref
  15.3 1.0 %edge.1 = (f32[3,96,128]{2,1,0:T(8,128)S(1)}, f32[3,3,96,128]{3,2,1,0:T(8,128)S(1)}, f32[2,3,48,128]{3,2,1,0:T(8,128)S(1)}, f32[864,128]{1,0:T(8,128)S(1)}, f32[...) custom-call(f32[7,4,384]{2,1,0:T(4,128)S(1)} %maximum_convert_fusion.weights_ref.refs_0_, ...), custom_call_target="tpu_custom_call" | custom-call | flops 10000000 | bytes 4000000 | tf_op jit(solution)/shard_map/edge/pallas_call | solution.py:578
  16.2 0.1 collective-permute-start.3
  16.3 0.4 %round_mixed.1 = (bf16[128,3072]{1,0:T(8,128)(2,1)S(1)}, f32[7,4,192]{2,1,0:T(4,128)S(1)}) custom-call(f32[3,1024,128]{2,1,0:T(8,128)S(1)} %get-tuple-element.53.middle, f32[3,96,128]{2,1,0:T(8,128)S(1)} %get-tuple-element.54.top), custom_call_target="tpu_custom_call" | custom-call | flops 393216 | bytes 2359296 | tf_op jit(solution)/shard_map/round_mixed/pallas_call | solution.py:634
  16.7 0.8 %collective-permute-done.3 = f32[7,4,192]{2,1,0:T(4,128)S(1)} collective-permute-done((f32[7,4,192]{2,1,0:T(4,128)S(1)}, f32[7,4,192]{2,1,0:T(4,128)S(1)}, u32[]{:S(2)}, u32[]{:S(2)}) %collective-permute-start.3) | collective-permute-done | bytes 21536 | tf_op jit(solution)/shard_map/ppermute | solution.py:64
  17.5 3.8 %collective-permute-start.4 = (f32[7,4,192]{2,1,0:T(4,128)S(1)}, f32[7,4,192]{2,1,0:T(4,128)S(1)}, u32[]{:S(2)}, u32[]{:S(2)}) collective-permute-start(f32[7,4,192]{2,1,0:T(4,128)S(1)} %add_add_fusion.3), channel_id=1, source_target_pairs={{0,2},{2,0},{4,6},{6,4},{8,10},{10,8},{12,14},{14,12},{16,18},{18,... | collective-permute-start | bytes 64520 | tf_op jit(solution)/shard_map/ppermute | solution.py:54
  21.3 1.5 %feature_gradients.4 = (bf16[3,128,3072]{2,1,0:T(8,128)(2,1)}, f32[7,4,192]{2,1,0:T(4,128)S(1)}, bf16[128,3072]{1,0:T(8,128)(2,1)}) custom-call(f32[7,4,384]{2,1,0:T(4,128)S(1)} %maximum_convert_fusion.weights_ref.refs_0_, f32[3,1024,128]{2,1,0:T(8,128)S(1)} %get-tuple-element.37.refs_1_, f32[3,1024,128]{2,1,0:T(8,128)S(1)} %get-tuple-element.38.refs_2_, ...), custom_call_target="tpu_custom_call" | custom-call | flops 5505024 | bytes 1769472 | tf_op jit(solution)/shard_map/feature_gradients/pallas_call | solution.py:782
  22.8 0.4 %collective-permute-done.4 = f32[7,4,192]{2,1,0:T(4,128)S(1)} collective-permute-done((f32[7,4,192]{2,1,0:T(4,128)S(1)}, f32[7,4,192]{2,1,0:T(4,128)S(1)}, u32[]{:S(2)}, u32[]{:S(2)}) %collective-permute-start.4) | collective-permute-done | bytes 21536 | tf_op jit(solution)/shard_map/ppermute | solution.py:54
  23.2 1.6 %collective-permute-start.5 = (f32[7,4,192]{2,1,0:T(4,128)S(1)}, f32[7,4,192]{2,1,0:T(4,128)S(1)}, u32[]{:S(2)}, u32[]{:S(2)}) collective-permute-start(f32[7,4,192]{2,1,0:T(4,128)S(1)} %add_add_fusion.2), channel_id=1, source_target_pairs={{0,4},{2,6},{4,0},{6,2},{8,12},{10,14},{12,8},{14,10},{16,20},{18,... | collective-permute-start | bytes 64520 | tf_op jit(solution)/shard_map/ppermute | solution.py:54
  24.7 1.5 %feature_gradients.5 = (bf16[3,128,3072]{2,1,0:T(8,128)(2,1)}, f32[7,4,192]{2,1,0:T(4,128)S(1)}) custom-call(f32[7,4,384]{2,1,0:T(4,128)S(1)} %maximum_convert_fusion.weights_ref.refs_0_, f32[3,1024,128]{2,1,0:T(8,128)S(1)} %get-tuple-element.37.refs_1_, f32[3,1024,128]{2,1,0:T(8,128)S(1)} %get-tuple-element.38.refs_2_, ...), custom_call_target="tpu_custom_call", output_to_operand_aliasing={{0}: (6, {})} | custom-call | flops 5505024 | bytes 1769472 | tf_op jit(solution)/shard_map/feature_gradients/pallas_call | solution.py:782
  26.2 0.9 %collective-permute-done.5 = f32[7,4,192]{2,1,0:T(4,128)S(1)} collective-permute-done((f32[7,4,192]{2,1,0:T(4,128)S(1)}, f32[7,4,192]{2,1,0:T(4,128)S(1)}, u32[]{:S(2)}, u32[]{:S(2)}) %collective-permute-start.5) | collective-permute-done | bytes 21536 | tf_op jit(solution)/shard_map/ppermute | solution.py:54
  27.1 2.1 %collective-permute-start.6 = (f32[7,4,192]{2,1,0:T(4,128)S(1)}, f32[7,4,192]{2,1,0:T(4,128)S(1)}, u32[]{:S(2)}, u32[]{:S(2)}) collective-permute-start(f32[7,4,192]{2,1,0:T(4,128)S(1)} %add_add_fusion.1), channel_id=1, source_target_pairs={{0,8},{2,10},{4,12},{6,14},{8,0},{10,2},{12,4},{14,6},{16,24},{18,... | collective-permute-start | bytes 64520 | tf_op jit(solution)/shard_map/ppermute | solution.py:54
  29.2 1.5 %feature_gradients.6 = (bf16[3,128,3072]{2,1,0:T(8,128)(2,1)}, f32[7,4,192]{2,1,0:T(4,128)S(1)}) custom-call(f32[7,4,384]{2,1,0:T(4,128)S(1)} %maximum_convert_fusion.weights_ref.refs_0_, f32[3,1024,128]{2,1,0:T(8,128)S(1)} %get-tuple-element.37.refs_1_, f32[3,1024,128]{2,1,0:T(8,128)S(1)} %get-tuple-element.38.refs_2_, ...), custom_call_target="tpu_custom_call", output_to_operand_aliasing={{0}: (6, {})} | custom-call | flops 5505024 | bytes 1769472 | tf_op jit(solution)/shard_map/feature_gradients/pallas_call | solution.py:782
  30.6 0.4 %collective-permute-done.6 = f32[7,4,192]{2,1,0:T(4,128)S(1)} collective-permute-done((f32[7,4,192]{2,1,0:T(4,128)S(1)}, f32[7,4,192]{2,1,0:T(4,128)S(1)}, u32[]{:S(2)}, u32[]{:S(2)}) %collective-permute-start.6) | collective-permute-done | bytes 21536 | tf_op jit(solution)/shard_map/ppermute | solution.py:54
  31.1 3.1 %collective-permute-start.7 = (f32[7,4,192]{2,1,0:T(4,128)S(1)}, f32[7,4,192]{2,1,0:T(4,128)S(1)}, u32[]{:S(2)}, u32[]{:S(2)}) collective-permute-start(f32[7,4,192]{2,1,0:T(4,128)S(1)} %add_add_fusion), channel_id=1, source_target_pairs={{0,16},{2,18},{4,20},{6,22},{8,24},{10,26},{12,28},{14,30},{16,0},... | collective-permute-start | bytes 64520 | tf_op jit(solution)/shard_map/ppermute | solution.py:54
  34.1 1.7 %feature_gradients.7 = (bf16[3,128,3072]{2,1,0:T(8,128)(2,1)}, f32[7,4,192]{2,1,0:T(4,128)S(1)}) custom-call(f32[7,4,384]{2,1,0:T(4,128)S(1)} %maximum_convert_fusion.weights_ref.refs_0_, f32[3,1024,128]{2,1,0:T(8,128)S(1)} %get-tuple-element.37.refs_1_, f32[3,1024,128]{2,1,0:T(8,128)S(1)} %get-tuple-element.38.refs_2_, ...), custom_call_target="tpu_custom_call", output_to_operand_aliasing={{0}: (6, {})} | custom-call | flops 5505024 | bytes 1769472 | tf_op jit(solution)/shard_map/feature_gradients/pallas_call | solution.py:782
  35.9 0.1 collective-permute-done.7
  36.0 0.6 %multiply_bitcast_fusion = f32[4,7,192]{2,0,1:T(4,128)} fusion(f32[7,4,192]{2,1,0:T(4,128)S(1)} %get-tuple-element.68, f32[7,4,192]{2,1,0:T(4,128)S(1)} %add_add_fusion, f32[7,4,192]{2,1,0:T(4,128)S(1)} %collective-permute-done.7), kind=kLoop, calls=%fused_computation | loop fusion | flops 16128 | bytes 86016 | tf_op jit(solution)/shard_map/transpose | solution.py:850
  (5 shorter events, 0.1 us)
Async XLA Ops:
  0.6 5.4 %copy-start = (bf16[3,128,3072]{2,1,0:T(8,128)(2,1)S(1)}, bf16[3,128,3072]{2,1,0:T(8,128)(2,1)}, u32[]{:S(2)}) copy-start(bf16[3,128,3072]{2,1,0:T(8,128)(2,1)} %features_ref.1) | copy-start | bytes 7077892
  2.1 3.8 %collective-permute-start = (bf16[7,4,192]{2,1,0:T(4,128)(2,1)S(1)}, bf16[7,4,192]{2,1,0:T(4,128)(2,1)S(1)}, u32[]{:S(2)}, u32[]{:S(2)}) collective-permute-start(bf16[7,4,192]{2,1,0:T(4,128)(2,1)S(1)} %get-tuple-element.36), channel_id=1, source_target_pairs={{0,1},{1,0},{2,3},{3,2},{4,5},{5,4},{6,7},{7,6},{8,9},{9,8},{10,11... | collective-permute-start | bytes 32264 | tf_op jit(solution)/shard_map/ppermute | solution.py:40
  2.7 12.6 %collective-permute-start.1 = (bf16[864,128]{1,0:T(8,128)(2,1)S(1)}, bf16[864,128]{1,0:T(8,128)(2,1)S(1)}, u32[]{:S(2)}, u32[]{:S(2)}) collective-permute-start(bf16[864,128]{1,0:T(8,128)(2,1)S(1)} %get-tuple-element.40), channel_id=1, source_target_pairs={{0,2},{2,0},{4,6},{6,4},{8,10},{10,8},{12,14},{14,12},{16,18},{18,... | collective-permute-start | bytes 663560 | tf_op jit(solution)/shard_map/ppermute | solution.py:28
  5.2 10.0 %collective-permute-start.2 = (bf16[864,128]{1,0:T(8,128)(2,1)S(1)}, bf16[864,128]{1,0:T(8,128)(2,1)S(1)}, u32[]{:S(2)}, u32[]{:S(2)}) collective-permute-start(bf16[864,128]{1,0:T(8,128)(2,1)S(1)} %get-tuple-element.41), channel_id=1, source_target_pairs={{2,4},{4,2},{6,8},{8,6},{10,12},{12,10},{14,16},{16,14},{18,20},{2... | collective-permute-start | bytes 663560 | tf_op jit(solution)/shard_map/ppermute | solution.py:27
  16.2 1.3 %collective-permute-start.3 = (f32[7,4,192]{2,1,0:T(4,128)S(1)}, f32[7,4,192]{2,1,0:T(4,128)S(1)}, u32[]{:S(2)}, u32[]{:S(2)}) collective-permute-start(f32[7,4,192]{2,1,0:T(4,128)S(1)} %get-tuple-element.63), channel_id=1, source_target_pairs={{0,1},{1,0},{2,3},{3,2},{4,5},{5,4},{6,7},{7,6},{8,9},{9,8},{10,11... | collective-permute-start | bytes 64520 | tf_op jit(solution)/shard_map/ppermute | solution.py:64
  17.5 5.6 %collective-permute-start.4 = (f32[7,4,192]{2,1,0:T(4,128)S(1)}, f32[7,4,192]{2,1,0:T(4,128)S(1)}, u32[]{:S(2)}, u32[]{:S(2)}) collective-permute-start(f32[7,4,192]{2,1,0:T(4,128)S(1)} %add_add_fusion.3), channel_id=1, source_target_pairs={{0,2},{2,0},{4,6},{6,4},{8,10},{10,8},{12,14},{14,12},{16,18},{18,... | collective-permute-start | bytes 64520 | tf_op jit(solution)/shard_map/ppermute | solution.py:54
  23.2 3.9 %collective-permute-start.5 = (f32[7,4,192]{2,1,0:T(4,128)S(1)}, f32[7,4,192]{2,1,0:T(4,128)S(1)}, u32[]{:S(2)}, u32[]{:S(2)}) collective-permute-start(f32[7,4,192]{2,1,0:T(4,128)S(1)} %add_add_fusion.2), channel_id=1, source_target_pairs={{0,4},{2,6},{4,0},{6,2},{8,12},{10,14},{12,8},{14,10},{16,20},{18,... | collective-permute-start | bytes 64520 | tf_op jit(solution)/shard_map/ppermute | solution.py:54
  27.1 3.9 %collective-permute-start.6 = (f32[7,4,192]{2,1,0:T(4,128)S(1)}, f32[7,4,192]{2,1,0:T(4,128)S(1)}, u32[]{:S(2)}, u32[]{:S(2)}) collective-permute-start(f32[7,4,192]{2,1,0:T(4,128)S(1)} %add_add_fusion.1), channel_id=1, source_target_pairs={{0,8},{2,10},{4,12},{6,14},{8,0},{10,2},{12,4},{14,6},{16,24},{18,... | collective-permute-start | bytes 64520 | tf_op jit(solution)/shard_map/ppermute | solution.py:54
  31.1 4.9 %collective-permute-start.7 = (f32[7,4,192]{2,1,0:T(4,128)S(1)}, f32[7,4,192]{2,1,0:T(4,128)S(1)}, u32[]{:S(2)}, u32[]{:S(2)}) collective-permute-start(f32[7,4,192]{2,1,0:T(4,128)S(1)} %add_add_fusion), channel_id=1, source_target_pairs={{0,16},{2,18},{4,20},{6,22},{8,24},{10,26},{12,28},{14,30},{16,0},... | collective-permute-start | bytes 64520 | tf_op jit(solution)/shard_map/ppermute | solution.py:54

commit v10 on v9

--- a/solution.py
+++ b/solution.py
@@ -236,7 +236,7 @@
                     message.put(token, column, repeat, value)
             return carry
 
-        lax.fori_loop(0, repeats, repeat_step, 0)
+        lax.fori_loop(0, repeats, repeat_step, 0, unroll=True)
 
     copies[0].wait()
     place(

time: 36.8 us -> 36.8 us (level)
  no operation moved by 1% of the time
where the time goes in v10:
time: 36.8 us; the launch traced here: 36.6 us
  Pallas kernels  17.7 us (48%)
  starting transfers between devices  14.3 us (39%)
  waiting for transfers between devices  3.07 us (8%)
  other arithmetic  0.78 us (2%)
  between operations  0.75 us (2%)
    ppermute x4, starting transfers between devices, sum_over(): received = lax.ppermute(value, axis, pairs)  10.5 us
    pallas_call x1, Pallas kernels, interior(): pl.pallas_call(functools.partial(interior_kernel, taps, repeats), out_sha...  8.69 us
    pallas_call x4, Pallas kernels, feature_gradients(): pl.pallas_call(functools.partial(grads_kernel, taps, repeats, first, step...  6.14 us
    ppermute x1, starting transfers between devices, swap_pairs(): near = lax.ppermute(near, axis, inner)  2.56 us
    ppermute x4, waiting for transfers between devices, sum_over(): received = lax.ppermute(value, axis, pairs)  1.76 us
    pallas_call x1, Pallas kernels, pack(): pl.pallas_call(functools.partial(pack_kernel, reach, groups // LANES), ou...  1.49 us
    pallas_call x1, Pallas kernels, edge(): pl.pallas_call(functools.partial(edge_kernel, taps, repeats), out_shape=(...  0.98 us
    ppermute x1, waiting for transfers between devices, sum_scatter(): return kept + lax.ppermute(sent, axis, [(0, 1), (1, 0)])  0.76 us
  transfers between devices with their start and end apart: 8, of which 6 were waited for; matrix products, arithmetic and copies ran while one was open for 0% of the time, Pallas kernels for 42%

profile of v10, /device:TPU:0, one launch (start us, length us, event | category | flops | bytes accessed | tf_op | source)
XLA Modules:
  0.0 36.6 jit_solution(18308060377801090459)
XLA Ops:
  0.6 0.0 copy-start
  0.6 1.5 %pack_halos.1 = (bf16[864,128]{1,0:T(8,128)(2,1)S(1)}, bf16[864,128]{1,0:T(8,128)(2,1)S(1)}, bf16[7,4,192]{2,1,0:T(4,128)(2,1)S(1)}) custom-call(bf16[3,128,3072]{2,1,0:T(8,128)(2,1)} %features_ref.1, bf16[128,3072]{1,0:T(8,128)(2,1)} %cotangent_hbm.3, f32[7,4,192]{2,1,0:T(4,128)} %bitcast.3), custom_call_target="tpu_custom_call" | custom-call | flops 1000000 | bytes 1000000 | tf_op jit(solution)/shard_map/pack_halos/pallas_call | solution.py:277
  2.1 0.5 %collective-permute-start = (bf16[7,4,192]{2,1,0:T(4,128)(2,1)S(1)}, bf16[7,4,192]{2,1,0:T(4,128)(2,1)S(1)}, u32[]{:S(2)}, u32[]{:S(2)}) collective-permute-start(bf16[7,4,192]{2,1,0:T(4,128)(2,1)S(1)} %get-tuple-element.36), channel_id=1, source_target_pairs={{0,1},{1,0},{2,3},{3,2},{4,5},{5,4},{6,7},{7,6},{8,9},{9,8},{10,11... | collective-permute-start | bytes 32264 | tf_op jit(solution)/shard_map/ppermute | solution.py:40
  2.7 2.6 %collective-permute-start.1 = (bf16[864,128]{1,0:T(8,128)(2,1)S(1)}, bf16[864,128]{1,0:T(8,128)(2,1)S(1)}, u32[]{:S(2)}, u32[]{:S(2)}) collective-permute-start(bf16[864,128]{1,0:T(8,128)(2,1)S(1)} %get-tuple-element.40), channel_id=1, source_target_pairs={{0,2},{2,0},{4,6},{6,4},{8,10},{10,8},{12,14},{14,12},{16,18},{18,... | collective-permute-start | bytes 663560 | tf_op jit(solution)/shard_map/ppermute | solution.py:28
  5.2 0.7 %collective-permute-start.2 = (bf16[864,128]{1,0:T(8,128)(2,1)S(1)}, bf16[864,128]{1,0:T(8,128)(2,1)S(1)}, u32[]{:S(2)}, u32[]{:S(2)}) collective-permute-start(bf16[864,128]{1,0:T(8,128)(2,1)S(1)} %get-tuple-element.41), channel_id=1, source_target_pairs={{2,4},{4,2},{6,8},{8,6},{10,12},{12,10},{14,16},{16,14},{18,20},{2... | collective-permute-start | bytes 663560 | tf_op jit(solution)/shard_map/ppermute | solution.py:27
  5.9 0.0 collective-permute-done
  5.9 0.1 maximum_convert_fusion.weights_ref.refs_0_
  6.0 0.0 copy-done
  6.0 8.7 %interior.1 = (f32[3,1024,128]{2,1,0:T(8,128)S(1)}, f32[3,1024,128]{2,1,0:T(8,128)S(1)}, f32[3,1024,128]{2,1,0:T(8,128)S(1)}, f32[3,1024,128]{2,1,0:T(8,128)S(1)...) custom-call(bf16[3,128,3072]{2,1,0:T(8,128)(2,1)S(1)} %copy-done, ...), custom_call_target="tpu_custom_call" | custom-call | flops 49545216 | bytes 8650752 | tf_op jit(solution)/shard_map/interior/pallas_call | solution.py:441
  14.7 0.5 %collective-permute-done.1.near_ref = bf16[864,128]{1,0:T(8,128)(2,1)S(1)} collective-permute-done((bf16[864,128]{1,0:T(8,128)(2,1)S(1)}, bf16[864,128]{1,0:T(8,128)(2,1)S(1)}, u32[]{:S(2)}, u32[]{:S(2)}) %collective-permute-start.1) | collective-permute-done | bytes 221216 | tf_op jit(solution)/shard_map/ppermute | solution.py:28
  15.3 0.0 collective-permute-done.2.far_ref
  15.3 1.0 %edge.1 = (f32[3,96,128]{2,1,0:T(8,128)S(1)}, f32[3,3,96,128]{3,2,1,0:T(8,128)S(1)}, f32[2,3,48,128]{3,2,1,0:T(8,128)S(1)}, f32[864,128]{1,0:T(8,128)S(1)}, f32[...) custom-call(f32[7,4,384]{2,1,0:T(4,128)S(1)} %maximum_convert_fusion.weights_ref.refs_0_, ...), custom_call_target="tpu_custom_call" | custom-call | flops 10000000 | bytes 4000000 | tf_op jit(solution)/shard_map/edge/pallas_call | solution.py:578
  16.2 0.1 collective-permute-start.3
  16.3 0.4 %round_mixed.1 = (bf16[128,3072]{1,0:T(8,128)(2,1)S(1)}, f32[7,4,192]{2,1,0:T(4,128)S(1)}) custom-call(f32[3,1024,128]{2,1,0:T(8,128)S(1)} %get-tuple-element.53.middle, f32[3,96,128]{2,1,0:T(8,128)S(1)} %get-tuple-element.54.top), custom_call_target="tpu_custom_call" | custom-call | flops 393216 | bytes 2359296 | tf_op jit(solution)/shard_map/round_mixed/pallas_call | solution.py:634
  16.7 0.8 %collective-permute-done.3 = f32[7,4,192]{2,1,0:T(4,128)S(1)} collective-permute-done((f32[7,4,192]{2,1,0:T(4,128)S(1)}, f32[7,4,192]{2,1,0:T(4,128)S(1)}, u32[]{:S(2)}, u32[]{:S(2)}) %collective-permute-start.3) | collective-permute-done | bytes 21536 | tf_op jit(solution)/shard_map/ppermute | solution.py:64
  17.5 3.8 %collective-permute-start.4 = (f32[7,4,192]{2,1,0:T(4,128)S(1)}, f32[7,4,192]{2,1,0:T(4,128)S(1)}, u32[]{:S(2)}, u32[]{:S(2)}) collective-permute-start(f32[7,4,192]{2,1,0:T(4,128)S(1)} %add_add_fusion.3), channel_id=1, source_target_pairs={{0,2},{2,0},{4,6},{6,4},{8,10},{10,8},{12,14},{14,12},{16,18},{18,... | collective-permute-start | bytes 64520 | tf_op jit(solution)/shard_map/ppermute | solution.py:54
  21.3 1.5 %feature_gradients.4 = (bf16[3,128,3072]{2,1,0:T(8,128)(2,1)}, f32[7,4,192]{2,1,0:T(4,128)S(1)}, bf16[128,3072]{1,0:T(8,128)(2,1)}) custom-call(f32[7,4,384]{2,1,0:T(4,128)S(1)} %maximum_convert_fusion.weights_ref.refs_0_, f32[3,1024,128]{2,1,0:T(8,128)S(1)} %get-tuple-element.37.refs_1_, f32[3,1024,128]{2,1,0:T(8,128)S(1)} %get-tuple-element.38.refs_2_, ...), custom_call_target="tpu_custom_call" | custom-call | flops 5505024 | bytes 1769472 | tf_op jit(solution)/shard_map/feature_gradients/pallas_call | solution.py:782
  22.8 0.4 %collective-permute-done.4 = f32[7,4,192]{2,1,0:T(4,128)S(1)} collective-permute-done((f32[7,4,192]{2,1,0:T(4,128)S(1)}, f32[7,4,192]{2,1,0:T(4,128)S(1)}, u32[]{:S(2)}, u32[]{:S(2)}) %collective-permute-start.4) | collective-permute-done | bytes 21536 | tf_op jit(solution)/shard_map/ppermute | solution.py:54
  23.2 1.6 %collective-permute-start.5 = (f32[7,4,192]{2,1,0:T(4,128)S(1)}, f32[7,4,192]{2,1,0:T(4,128)S(1)}, u32[]{:S(2)}, u32[]{:S(2)}) collective-permute-start(f32[7,4,192]{2,1,0:T(4,128)S(1)} %add_add_fusion.2), channel_id=1, source_target_pairs={{0,4},{2,6},{4,0},{6,2},{8,12},{10,14},{12,8},{14,10},{16,20},{18,... | collective-permute-start | bytes 64520 | tf_op jit(solution)/shard_map/ppermute | solution.py:54
  24.7 1.5 %feature_gradients.5 = (bf16[3,128,3072]{2,1,0:T(8,128)(2,1)}, f32[7,4,192]{2,1,0:T(4,128)S(1)}) custom-call(f32[7,4,384]{2,1,0:T(4,128)S(1)} %maximum_convert_fusion.weights_ref.refs_0_, f32[3,1024,128]{2,1,0:T(8,128)S(1)} %get-tuple-element.37.refs_1_, f32[3,1024,128]{2,1,0:T(8,128)S(1)} %get-tuple-element.38.refs_2_, ...), custom_call_target="tpu_custom_call", output_to_operand_aliasing={{0}: (6, {})} | custom-call | flops 5505024 | bytes 1769472 | tf_op jit(solution)/shard_map/feature_gradients/pallas_call | solution.py:782
  26.2 0.9 %collective-permute-done.5 = f32[7,4,192]{2,1,0:T(4,128)S(1)} collective-permute-done((f32[7,4,192]{2,1,0:T(4,128)S(1)}, f32[7,4,192]{2,1,0:T(4,128)S(1)}, u32[]{:S(2)}, u32[]{:S(2)}) %collective-permute-start.5) | collective-permute-done | bytes 21536 | tf_op jit(solution)/shard_map/ppermute | solution.py:54
  27.1 2.1 %collective-permute-start.6 = (f32[7,4,192]{2,1,0:T(4,128)S(1)}, f32[7,4,192]{2,1,0:T(4,128)S(1)}, u32[]{:S(2)}, u32[]{:S(2)}) collective-permute-start(f32[7,4,192]{2,1,0:T(4,128)S(1)} %add_add_fusion.1), channel_id=1, source_target_pairs={{0,8},{2,10},{4,12},{6,14},{8,0},{10,2},{12,4},{14,6},{16,24},{18,... | collective-permute-start | bytes 64520 | tf_op jit(solution)/shard_map/ppermute | solution.py:54
  29.2 1.5 %feature_gradients.6 = (bf16[3,128,3072]{2,1,0:T(8,128)(2,1)}, f32[7,4,192]{2,1,0:T(4,128)S(1)}) custom-call(f32[7,4,384]{2,1,0:T(4,128)S(1)} %maximum_convert_fusion.weights_ref.refs_0_, f32[3,1024,128]{2,1,0:T(8,128)S(1)} %get-tuple-element.37.refs_1_, f32[3,1024,128]{2,1,0:T(8,128)S(1)} %get-tuple-element.38.refs_2_, ...), custom_call_target="tpu_custom_call", output_to_operand_aliasing={{0}: (6, {})} | custom-call | flops 5505024 | bytes 1769472 | tf_op jit(solution)/shard_map/feature_gradients/pallas_call | solution.py:782
  30.6 0.4 %collective-permute-done.6 = f32[7,4,192]{2,1,0:T(4,128)S(1)} collective-permute-done((f32[7,4,192]{2,1,0:T(4,128)S(1)}, f32[7,4,192]{2,1,0:T(4,128)S(1)}, u32[]{:S(2)}, u32[]{:S(2)}) %collective-permute-start.6) | collective-permute-done | bytes 21536 | tf_op jit(solution)/shard_map/ppermute | solution.py:54
  31.1 3.1 %collective-permute-start.7 = (f32[7,4,192]{2,1,0:T(4,128)S(1)}, f32[7,4,192]{2,1,0:T(4,128)S(1)}, u32[]{:S(2)}, u32[]{:S(2)}) collective-permute-start(f32[7,4,192]{2,1,0:T(4,128)S(1)} %add_add_fusion), channel_id=1, source_target_pairs={{0,16},{2,18},{4,20},{6,22},{8,24},{10,26},{12,28},{14,30},{16,0},... | collective-permute-start | bytes 64520 | tf_op jit(solution)/shard_map/ppermute | solution.py:54
  34.1 1.7 %feature_gradients.7 = (bf16[3,128,3072]{2,1,0:T(8,128)(2,1)}, f32[7,4,192]{2,1,0:T(4,128)S(1)}) custom-call(f32[7,4,384]{2,1,0:T(4,128)S(1)} %maximum_convert_fusion.weights_ref.refs_0_, f32[3,1024,128]{2,1,0:T(8,128)S(1)} %get-tuple-element.37.refs_1_, f32[3,1024,128]{2,1,0:T(8,128)S(1)} %get-tuple-element.38.refs_2_, ...), custom_call_target="tpu_custom_call", output_to_operand_aliasing={{0}: (6, {})} | custom-call | flops 5505024 | bytes 1769472 | tf_op jit(solution)/shard_map/feature_gradients/pallas_call | solution.py:782
  35.9 0.1 collective-permute-done.7
  36.0 0.6 %multiply_bitcast_fusion = f32[4,7,192]{2,0,1:T(4,128)} fusion(f32[7,4,192]{2,1,0:T(4,128)S(1)} %get-tuple-element.68, f32[7,4,192]{2,1,0:T(4,128)S(1)} %add_add_fusion, f32[7,4,192]{2,1,0:T(4,128)S(1)} %collective-permute-done.7), kind=kLoop, calls=%fused_computation | loop fusion | flops 16128 | bytes 86016 | tf_op jit(solution)/shard_map/transpose | solution.py:850
  (5 shorter events, 0.1 us)
Async XLA Ops:
  0.6 5.4 %copy-start = (bf16[3,128,3072]{2,1,0:T(8,128)(2,1)S(1)}, bf16[3,128,3072]{2,1,0:T(8,128)(2,1)}, u32[]{:S(2)}) copy-start(bf16[3,128,3072]{2,1,0:T(8,128)(2,1)} %features_ref.1) | copy-start | bytes 7077892
  2.1 3.8 %collective-permute-start = (bf16[7,4,192]{2,1,0:T(4,128)(2,1)S(1)}, bf16[7,4,192]{2,1,0:T(4,128)(2,1)S(1)}, u32[]{:S(2)}, u32[]{:S(2)}) collective-permute-start(bf16[7,4,192]{2,1,0:T(4,128)(2,1)S(1)} %get-tuple-element.36), channel_id=1, source_target_pairs={{0,1},{1,0},{2,3},{3,2},{4,5},{5,4},{6,7},{7,6},{8,9},{9,8},{10,11... | collective-permute-start | bytes 32264 | tf_op jit(solution)/shard_map/ppermute | solution.py:40
  2.7 12.6 %collective-permute-start.1 = (bf16[864,128]{1,0:T(8,128)(2,1)S(1)}, bf16[864,128]{1,0:T(8,128)(2,1)S(1)}, u32[]{:S(2)}, u32[]{:S(2)}) collective-permute-start(bf16[864,128]{1,0:T(8,128)(2,1)S(1)} %get-tuple-element.40), channel_id=1, source_target_pairs={{0,2},{2,0},{4,6},{6,4},{8,10},{10,8},{12,14},{14,12},{16,18},{18,... | collective-permute-start | bytes 663560 | tf_op jit(solution)/shard_map/ppermute | solution.py:28
  5.2 10.0 %collective-permute-start.2 = (bf16[864,128]{1,0:T(8,128)(2,1)S(1)}, bf16[864,128]{1,0:T(8,128)(2,1)S(1)}, u32[]{:S(2)}, u32[]{:S(2)}) collective-permute-start(bf16[864,128]{1,0:T(8,128)(2,1)S(1)} %get-tuple-element.41), channel_id=1, source_target_pairs={{2,4},{4,2},{6,8},{8,6},{10,12},{12,10},{14,16},{16,14},{18,20},{2... | collective-permute-start | bytes 663560 | tf_op jit(solution)/shard_map/ppermute | solution.py:27
  16.2 1.3 %collective-permute-start.3 = (f32[7,4,192]{2,1,0:T(4,128)S(1)}, f32[7,4,192]{2,1,0:T(4,128)S(1)}, u32[]{:S(2)}, u32[]{:S(2)}) collective-permute-start(f32[7,4,192]{2,1,0:T(4,128)S(1)} %get-tuple-element.63), channel_id=1, source_target_pairs={{0,1},{1,0},{2,3},{3,2},{4,5},{5,4},{6,7},{7,6},{8,9},{9,8},{10,11... | collective-permute-start | bytes 64520 | tf_op jit(solution)/shard_map/ppermute | solution.py:64
  17.5 5.6 %collective-permute-start.4 = (f32[7,4,192]{2,1,0:T(4,128)S(1)}, f32[7,4,192]{2,1,0:T(4,128)S(1)}, u32[]{:S(2)}, u32[]{:S(2)}) collective-permute-start(f32[7,4,192]{2,1,0:T(4,128)S(1)} %add_add_fusion.3), channel_id=1, source_target_pairs={{0,2},{2,0},{4,6},{6,4},{8,10},{10,8},{12,14},{14,12},{16,18},{18,... | collective-permute-start | bytes 64520 | tf_op jit(solution)/shard_map/ppermute | solution.py:54
  23.2 3.9 %collective-permute-start.5 = (f32[7,4,192]{2,1,0:T(4,128)S(1)}, f32[7,4,192]{2,1,0:T(4,128)S(1)}, u32[]{:S(2)}, u32[]{:S(2)}) collective-permute-start(f32[7,4,192]{2,1,0:T(4,128)S(1)} %add_add_fusion.2), channel_id=1, source_target_pairs={{0,4},{2,6},{4,0},{6,2},{8,12},{10,14},{12,8},{14,10},{16,20},{18,... | collective-permute-start | bytes 64520 | tf_op jit(solution)/shard_map/ppermute | solution.py:54
  27.1 3.9 %collective-permute-start.6 = (f32[7,4,192]{2,1,0:T(4,128)S(1)}, f32[7,4,192]{2,1,0:T(4,128)S(1)}, u32[]{:S(2)}, u32[]{:S(2)}) collective-permute-start(f32[7,4,192]{2,1,0:T(4,128)S(1)} %add_add_fusion.1), channel_id=1, source_target_pairs={{0,8},{2,10},{4,12},{6,14},{8,0},{10,2},{12,4},{14,6},{16,24},{18,... | collective-permute-start | bytes 64520 | tf_op jit(solution)/shard_map/ppermute | solution.py:54
  31.1 4.9 %collective-permute-start.7 = (f32[7,4,192]{2,1,0:T(4,128)S(1)}, f32[7,4,192]{2,1,0:T(4,128)S(1)}, u32[]{:S(2)}, u32[]{:S(2)}) collective-permute-start(f32[7,4,192]{2,1,0:T(4,128)S(1)} %add_add_fusion), channel_id=1, source_target_pairs={{0,16},{2,18},{4,20},{6,22},{8,24},{10,26},{12,28},{14,30},{16,0},... | collective-permute-start | bytes 64520 | tf_op jit(solution)/shard_map/ppermute | solution.py:54
